TPU v7x, 32 devices: a whole 2x2x4 slice. The times are simulated.
32 devices in a mesh: dp: 16 (over z, y, x), tensor: 2 (over core).
Axes of the slice: x: 2, y: 2, z: 4, core: 2. Of those that a mesh axis runs over, the one named last changes fastest.
Arguments:
- tokens: bfloat16 [16384, 1536], P(('dp', 'tensor')), may hold values from -6 to 6
- routes: int32 [16384, 6], P('dp'), may hold values from 0 to 15, all different within a row; in each aligned block of 1024 rows (0 to 1023, 1024 to 2047, ...) at most 416 rows name the same one
- gain_in: float32 [1536], replicated, may hold values from 0.5 to 1.5
- w_zx: bfloat16 [1536, 2, 3072], P('dp', None, 'tensor'), may hold values from -0.15625 to 0.15625
- w_dt: bfloat16 [1536, 48], P('dp', 'tensor'), may hold values from -0.078125 to 0.078125
- w_bc: bfloat16 [1536, 256], P(('dp', 'tensor')), may hold values from -0.15625 to 0.15625
- conv_w: float32 [4, 3328], replicated, may hold values from -0.5 to 0.5
- conv_b: float32 [3328], replicated, may hold values from -2.5 to 2.5
- dt_bias: float32 [48], replicated, may hold values from -6.9 to -2.3
- a_log: float32 [48], replicated, may hold values from 0 to 2.7
- d_skip: float32 [48], replicated, may hold values from 0.5 to 1.5
- norm_gain: float32 [3072], replicated, may hold values from 0.5 to 1.5
- w_out: bfloat16 [3072, 1536], P('tensor', 'dp'), may hold values from -0.109375 to 0.109375
- gain_mid: float32 [1536], replicated, may hold values from 0.5 to 1.5
- router: bfloat16 [1536, 16], P(('dp', 'tensor')), may hold values from -0.078125 to 0.078125
- shared_gu: bfloat16 [1536, 2, 1024], P('dp', None, 'tensor'), may hold values from -0.15625 to 0.15625
- shared_down: bfloat16 [1024, 1536], P('tensor', 'dp'), may hold values from -0.25 to 0.25
- expert_gu: bfloat16 [16, 1536, 2, 512], P(None, 'dp', None, 'tensor'), may hold values from -0.15625 to 0.15625
- expert_down: bfloat16 [16, 512, 1536], P(None, 'tensor', 'dp'), may hold values from -0.5 to 0.5
- grad_out: bfloat16 [16384, 1536], P(('dp', 'tensor')), may hold values from -6 to 6
Outputs:
- output: bfloat16 [16384, 1536], P(('dp', 'tensor'))
- grad_tokens: bfloat16 [16384, 1536], P(('dp', 'tensor'))
- grad_gain_in: float32 [1536], replicated
- grad_w_zx: float32 [1536, 2, 3072], P('dp', None, 'tensor')
- grad_w_dt: float32 [1536, 48], P('dp', 'tensor')
- grad_w_bc: float32 [1536, 256], P(('dp', 'tensor'))
- grad_conv_w: float32 [4, 3328], replicated
- grad_conv_b: float32 [3328], replicated
- grad_dt_bias: float32 [48], replicated
- grad_a_log: float32 [48], replicated
- grad_d_skip: float32 [48], replicated
- grad_norm_gain: float32 [3072], replicated
- grad_w_out: float32 [3072, 1536], P('tensor', 'dp')
- grad_gain_mid: float32 [1536], replicated
- grad_router: float32 [1536, 16], P(('dp', 'tensor'))
- grad_shared_gu: float32 [1536, 2, 1024], P('dp', None, 'tensor')
- grad_shared_down: float32 [1024, 1536], P('tensor', 'dp')
- grad_expert_gu: float32 [16, 1536, 2, 512], P(None, 'dp', None, 'tensor')
- grad_expert_down: float32 [16, 512, 1536], P(None, 'tensor', 'dp')
Inputs may be any that keep to these rules, and one draw needn't show every extreme that they name: `routes`: each row names 6 different experts; among the 1024 rows of one sequence no expert is named by more than 416 rows, a bound that some block reaches.
All inputs are finite; a program needn't handle non-finite values.
Results may differ from a plain program's by a relative error of at most 0.01.
Values may be sent and summed in bfloat16 or wider, within the bound.
No kernel may reach another device: no remote copies, remote signals or barrier semaphores. Data moves between devices by JAX's collectives and lax.ppermute only.
A program may use at most 576 MiB of HBM per device.

v0:
```python
from functools import partial

import jax
import jax.numpy as jnp
from jax import lax
from jax.sharding import PartitionSpec as P

D = 1536
H = 48
P_SIZE = 64
EXPERTS = 16
BL = 128
SEQ = 1024
CAP = 416


eps = 1e-05
highest = lax.Precision.HIGHEST


def cast_value(v):
    return lax.optimization_barrier(v.astype(jnp.bfloat16)).astype(jnp.float32)


def value_rounder():

    def keep_value(v):
        return (cast_value(v), None)

    def pass_grad(kept, grad):
        return (grad,)

    wrapped = jax.custom_vjp(cast_value)
    wrapped.defvjp(keep_value, pass_grad)
    return wrapped


def grad_rounder():

    def same_value(v):
        return v

    def keep_same(v):
        return (v, None)

    def round_back(kept, grad):
        return (cast_value(grad),)

    wrapped = jax.custom_vjp(same_value)
    wrapped.defvjp(keep_same, round_back)
    return wrapped


def round_value(v):
    return value_rounder()(v)


def round_grad(v):
    return grad_rounder()(v)


def plain_dot(left_mat, right_mat):
    return jnp.dot(left_mat, right_mat, preferred_element_type=jnp.float32)


def exact_dot(left_mat, right_mat):
    return jnp.dot(left_mat, right_mat, precision=highest)


def rms_norm(values, gain_vec):
    return values * lax.rsqrt(jnp.mean(values * values, axis=-1, keepdims=True) + eps) * gain_vec


def causal_conv(signal, kernel, bias_vec):
    conv_width = kernel.shape[0]
    length = signal.shape[0]
    padded = jnp.pad(signal, ((conv_width - 1, 0), (0, 0)))
    summed = jnp.zeros_like(signal) + bias_vec
    for offset in range(conv_width):
        summed = summed + kernel[offset] * padded[offset : offset + length]
    return summed


def ssd_block(carry_state, block_in):
    inputs, b_proj, c_proj, decay_log = block_in
    length = inputs.shape[0]
    cum_log = jnp.cumsum(decay_log, axis=0)
    row_pos = lax.broadcasted_iota(jnp.int32, (length, length), 0)
    col_pos = lax.broadcasted_iota(jnp.int32, (length, length), 1)
    causal = (col_pos <= row_pos)[:, :, None]
    log_gap = jnp.where(causal, cum_log[:, None, :] - cum_log[None, :, :], 0.0)
    scores = jnp.dot(c_proj, b_proj.T, precision=highest)
    weights = jnp.where(causal, jnp.exp(log_gap), 0.0) * scores[:, :, None]
    within = jnp.einsum("tsh,shp->thp", weights, inputs, precision=highest)
    across = (
        jnp.einsum("tn,hnp->thp", c_proj, carry_state, precision=highest)
        * jnp.exp(cum_log)[:, :, None]
    )
    to_end = jnp.exp(cum_log[-1][None, :] - cum_log)
    carried = carry_state * jnp.exp(cum_log[-1])[:, None, None]
    new_state = carried + jnp.einsum(
        "sn,shp->hnp", b_proj, inputs * to_end[:, :, None], precision=highest
    )
    return (new_state, within + across)


def scan_heads(inputs, b_proj, c_proj, decay_log):
    length, head_count, head_size = inputs.shape
    block_count = length // BL
    blocks = (
        inputs.reshape(block_count, BL, head_count, head_size),
        b_proj.reshape(block_count, BL, -1),
        c_proj.reshape(block_count, BL, -1),
        decay_log.reshape(block_count, BL, head_count),
    )
    zero_state = jnp.zeros((head_count, b_proj.shape[1], head_size), jnp.float32)
    final_state, block_out = lax.scan(ssd_block, zero_state, blocks)
    return block_out.reshape(length, head_count, head_size)


def mixer_front(normed, zx_w, dt_w, bc_w, conv_k, conv_bias, dt_shift, decay_rate, skip_gain):
    local_width = zx_w.shape[2]
    head_count = dt_w.shape[1]
    state_size = bc_w.shape[1] // 2
    gate_z = round_grad(plain_dot(normed, zx_w[:, 0]))
    inner = round_grad(plain_dot(normed, zx_w[:, 1]))
    raw_dt = round_grad(plain_dot(normed, dt_w))
    proj_bc = exact_dot(normed, bc_w)
    activated = jax.nn.silu(
        causal_conv(jnp.concatenate([inner, proj_bc], axis=1), conv_k, conv_bias)
    )
    x_heads = activated[:, :local_width].reshape(-1, head_count, local_width // head_count)
    b_proj = activated[:, local_width : local_width + state_size]
    c_proj = activated[:, local_width + state_size :]
    step_size = jax.nn.softplus(raw_dt + dt_shift)
    decay_log = -step_size * jnp.exp(decay_rate)
    y_heads = scan_heads(x_heads * step_size[:, :, None], b_proj, c_proj, decay_log)
    y_heads = y_heads + skip_gain[None, :, None] * x_heads
    gated_out = y_heads.reshape(-1, local_width) * jax.nn.silu(gate_z)
    return (gated_out, jnp.sum(gated_out * gated_out, axis=1))


def mixer_rear(gated_out, summed, gain_vec, out_w, full_width):
    scaled = round_value(gated_out * lax.rsqrt(summed[:, None] / full_width + eps) * gain_vec)
    return plain_dot(scaled, out_w)


def slot_tables(routes):
    flat_ids = routes.reshape(-1)
    onehot = (flat_ids[:, None] == jnp.arange(EXPERTS, dtype=jnp.int32)[None, :]).astype(jnp.int32)
    before = jnp.cumsum(onehot, axis=0) - onehot
    place_in = jnp.sum(before * onehot, axis=1)
    slot_of = flat_ids * CAP + place_in
    token_of = jnp.arange(flat_ids.shape[0], dtype=jnp.int32) // routes.shape[1]
    slot_token = jnp.zeros((EXPERTS * CAP,), jnp.int32).at[slot_of].set(token_of)
    return (slot_of, slot_token)


def gate_values(normed, router_w, routes, slot_of):
    logits = exact_dot(normed, router_w)
    picked = jnp.take_along_axis(logits, routes, axis=1)
    exp_vals = jnp.exp(picked - jnp.max(picked, axis=1, keepdims=True))
    gates = exp_vals / jnp.sum(exp_vals, axis=1, keepdims=True)
    return jnp.zeros((EXPERTS * CAP,), jnp.float32).at[slot_of].set(gates.reshape(-1))


def swiglu_back(gate_pre, up_pre, d_hidden):
    sigmoid_g = jax.nn.sigmoid(gate_pre)
    d_up = d_hidden * gate_pre * sigmoid_g
    d_gate = d_hidden * up_pre * sigmoid_g * (1.0 + gate_pre * (1.0 - sigmoid_g))
    return jnp.stack([d_gate, d_up], axis=-2).astype(jnp.bfloat16)


def widen(local_part, my_index, full_size, axis_num):
    shape_full = local_part.shape[:axis_num] + (full_size,) + local_part.shape[axis_num + 1 :]
    zero_fill = jnp.zeros(shape_full, jnp.float32)
    return lax.dynamic_update_slice_in_dim(
        zero_fill, local_part, my_index * local_part.shape[axis_num], axis_num
    )


def whole_rows(values):
    return lax.all_gather(values, "tensor", axis=0, tiled=True)


def own_rows(values):
    return lax.psum_scatter(values, "tensor", scatter_dimension=0, tiled=True)


def head_total(values):
    return lax.psum(values, "tensor")


def dense_weights(w_zx, w_dt, w_out, shared_gu, shared_down):
    return (
        lax.all_gather(w_zx, "dp", axis=0, tiled=True),
        lax.all_gather(w_dt, "dp", axis=0, tiled=True),
        lax.all_gather(w_out, "dp", axis=1, tiled=True),
        lax.all_gather(shared_gu, "dp", axis=0, tiled=True),
        lax.all_gather(shared_down, "dp", axis=1, tiled=True),
    )


def routed_weights(expert_gu, expert_down):
    return (
        lax.all_gather(expert_gu, "dp", axis=1, tiled=True),
        lax.all_gather(expert_down, "dp", axis=2, tiled=True),
    )


def joint_weights(w_bc, router):
    return (
        lax.all_gather(w_bc, ("dp", "tensor"), axis=0, tiled=True),
        lax.all_gather(router, ("dp", "tensor"), axis=0, tiled=True),
    )


def shards(
    tokens,
    routes,
    gain_in,
    w_zx,
    w_dt,
    w_bc,
    conv_w,
    conv_b,
    dt_bias,
    a_log,
    d_skip,
    norm_gain,
    w_out,
    gain_mid,
    router,
    shared_gu,
    shared_down,
    expert_gu,
    expert_down,
    grad_out,
):
    splits = lax.axis_size("tensor")
    my_index = lax.axis_index("tensor")
    head_count = H // splits
    local_width = head_count * P_SIZE
    conv_k = jnp.concatenate(
        [
            lax.dynamic_slice_in_dim(conv_w, my_index * local_width, local_width, 1),
            conv_w[:, H * P_SIZE :],
        ],
        axis=1,
    )
    conv_bias = jnp.concatenate(
        [
            lax.dynamic_slice_in_dim(conv_b, my_index * local_width, local_width, 0),
            conv_b[H * P_SIZE :],
        ]
    )
    dt_shift = lax.dynamic_slice_in_dim(dt_bias, my_index * head_count, head_count, 0)
    decay_rate = lax.dynamic_slice_in_dim(a_log, my_index * head_count, head_count, 0)
    skip_gain = lax.dynamic_slice_in_dim(d_skip, my_index * head_count, head_count, 0)
    gain_loc = lax.dynamic_slice_in_dim(norm_gain, my_index * local_width, local_width, 0)
    local_args = (conv_k, conv_bias, dt_shift, decay_rate, skip_gain)
    rear = partial(mixer_rear, full_width=H * P_SIZE)
    resid_in = tokens.astype(jnp.float32)
    normed_piece, first_norm = jax.vjp(rms_norm, resid_in, gain_in)
    normed = whole_rows(normed_piece.astype(jnp.bfloat16))
    normed_wide = normed.astype(jnp.float32)
    zx_all, dt_all, out_all, sgu_all, sdown_all = dense_weights(
        w_zx, w_dt, w_out, shared_gu, shared_down
    )
    bc_all, router_all = joint_weights(w_bc, router)
    front_args = (
        normed_wide,
        zx_all.astype(jnp.float32),
        dt_all.astype(jnp.float32),
        bc_all.astype(jnp.float32),
    ) + local_args
    (gated_out, squares), front_pull = jax.vjp(mixer_front, *front_args)
    summed_sq = head_total(squares)
    mixed_part, rear_pull = jax.vjp(
        rear, gated_out, summed_sq, gain_loc, out_all.astype(jnp.float32)
    )
    resid = resid_in + own_rows(mixed_part)
    mid_piece, second_norm = jax.vjp(rms_norm, resid, gain_mid)
    mid_rows = whole_rows(mid_piece.astype(jnp.bfloat16))
    mid_wide = mid_rows.astype(jnp.float32)
    slot_of, slot_token = slot_tables(routes)
    token_table = slot_token.reshape(EXPERTS, CAP)
    gate_fn = partial(gate_values, routes=routes, slot_of=slot_of)
    slot_gate, gate_pull = jax.vjp(gate_fn, mid_wide, router_all.astype(jnp.float32))
    gate_table = slot_gate.reshape(EXPERTS, CAP)
    buffers = mid_rows[slot_token]
    egu_all, edown_all = routed_weights(expert_gu, expert_down)
    gate_up = jnp.einsum(
        "ecd,edkf->eckf",
        buffers.reshape(EXPERTS, CAP, D),
        egu_all,
        preferred_element_type=jnp.float32,
    )
    e_hidden = (jax.nn.silu(gate_up[:, :, 0]) * gate_up[:, :, 1]).astype(jnp.bfloat16)

    def combine(routed_rows, member):
        hidden_e, down_e, row_ids, weight = member
        expert_out = jnp.dot(hidden_e, down_e, preferred_element_type=jnp.float32)
        return (routed_rows.at[row_ids].add(expert_out * weight[:, None]), None)

    routed, _ = lax.scan(
        combine, jnp.zeros((SEQ, D), jnp.float32), (e_hidden, edown_all, token_table, gate_table)
    )
    shared_pre = jnp.dot(
        mid_rows, sgu_all.reshape(D, -1), preferred_element_type=jnp.float32
    ).reshape(SEQ, 2, -1)
    s_hidden = (jax.nn.silu(shared_pre[:, 0]) * shared_pre[:, 1]).astype(jnp.bfloat16)
    branch = routed + jnp.dot(s_hidden, sdown_all, preferred_element_type=jnp.float32)
    output = (resid + own_rows(branch)).astype(jnp.bfloat16)
    back_out = grad_out.astype(jnp.float32)
    back_rows = whole_rows(grad_out)
    zx_all, dt_all, out_all, sgu_all, sdown_all = dense_weights(
        w_zx, w_dt, w_out, shared_gu, shared_down
    )
    bc_all, router_all = joint_weights(w_bc, router)
    slot_gate, gate_pull = jax.vjp(gate_fn, mid_wide, router_all.astype(jnp.float32))
    egu_all, edown_all = routed_weights(expert_gu, expert_down)
    d_s_hidden = jnp.einsum("sd,fd->sf", back_rows, sdown_all, preferred_element_type=jnp.float32)
    grad_sdown = jnp.einsum("sf,sd->fd", s_hidden, back_rows, preferred_element_type=jnp.float32)
    d_shared = swiglu_back(shared_pre[:, 0], shared_pre[:, 1], d_s_hidden)
    grad_sgu = jnp.einsum("sd,skf->dkf", mid_rows, d_shared, preferred_element_type=jnp.float32)
    d_mid_shared = jnp.einsum("skf,dkf->sd", d_shared, sgu_all, preferred_element_type=jnp.float32)

    def expert_back(d_mid_acc, member):
        row_ids, weight, pre_act, down_e, gu_e = member
        in_rows = mid_rows[row_ids]
        cot_rows = back_rows[row_ids]
        hidden_e = (jax.nn.silu(pre_act[:, 0]) * pre_act[:, 1]).astype(jnp.bfloat16)
        expert_out = jnp.dot(hidden_e, down_e, preferred_element_type=jnp.float32)
        d_weight = jnp.sum(expert_out * cot_rows.astype(jnp.float32), axis=1)
        d_out = (weight[:, None] * cot_rows.astype(jnp.float32)).astype(jnp.bfloat16)
        d_hid = jnp.einsum("cd,fd->cf", d_out, down_e, preferred_element_type=jnp.float32)
        grad_down = jnp.einsum("cf,cd->fd", hidden_e, d_out, preferred_element_type=jnp.float32)
        d_pre = swiglu_back(pre_act[:, 0], pre_act[:, 1], d_hid)
        grad_gu = jnp.einsum("cd,ckf->dkf", in_rows, d_pre, preferred_element_type=jnp.float32)
        d_in = jnp.einsum("ckf,dkf->cd", d_pre, gu_e, preferred_element_type=jnp.float32)
        return (d_mid_acc.at[row_ids].add(d_in), (grad_gu, grad_down, d_weight))

    d_mid_routed, (egu_grads, edown_grads, d_slot_gate) = lax.scan(
        expert_back,
        jnp.zeros((SEQ, D), jnp.float32),
        (token_table, gate_table, gate_up, edown_all, egu_all),
    )
    d_slot_gate = d_slot_gate.reshape(-1)
    d_mid_gate, d_router_all = gate_pull(d_slot_gate)
    d_mid_piece = own_rows(d_mid_routed + d_mid_shared + d_mid_gate)
    d_resid_extra, grad_gain_mid = second_norm(d_mid_piece)
    d_resid = back_out + d_resid_extra
    d_mix = whole_rows(d_resid.astype(jnp.bfloat16))
    front_args = (
        normed_wide,
        zx_all.astype(jnp.float32),
        dt_all.astype(jnp.float32),
        bc_all.astype(jnp.float32),
    ) + local_args
    (gated_out, squares), front_pull = jax.vjp(mixer_front, *front_args)
    mixed_part, rear_pull = jax.vjp(
        rear, gated_out, summed_sq, gain_loc, out_all.astype(jnp.float32)
    )
    d_gated, d_summed, grad_gain_loc, grad_out_w = rear_pull(d_mix.astype(jnp.float32))
    d_summed = head_total(d_summed)
    (
        d_normed,
        grad_zx,
        grad_dt,
        grad_bc,
        grad_conv_k,
        grad_conv_bias,
        grad_dt_shift,
        grad_decay,
        grad_skip,
    ) = front_pull((d_gated, d_summed))
    d_in_piece = own_rows(d_normed)
    d_in_extra, grad_gain_in = first_norm(d_in_piece)
    grad_tokens = (d_resid + d_in_extra).astype(jnp.bfloat16)
    g_zx, g_dt, g_out, g_sgu, g_sdown = (
        lax.psum_scatter(grad_zx, "dp", scatter_dimension=0, tiled=True),
        lax.psum_scatter(grad_dt, "dp", scatter_dimension=0, tiled=True),
        lax.psum_scatter(grad_out_w, "dp", scatter_dimension=1, tiled=True),
        lax.psum_scatter(grad_sgu, "dp", scatter_dimension=0, tiled=True),
        lax.psum_scatter(grad_sdown, "dp", scatter_dimension=1, tiled=True),
    )
    g_bc, g_router = (
        lax.psum_scatter(grad_bc, ("dp", "tensor"), scatter_dimension=0, tiled=True),
        lax.psum_scatter(d_router_all, ("dp", "tensor"), scatter_dimension=0, tiled=True),
    )
    g_egu, g_edown = (
        lax.psum_scatter(egu_grads, "dp", scatter_dimension=1, tiled=True),
        lax.psum_scatter(edown_grads, "dp", scatter_dimension=2, tiled=True),
    )
    conv_full = jnp.concatenate(
        [
            widen(grad_conv_k[:, :local_width], my_index, H * P_SIZE, 1),
            grad_conv_k[:, local_width:],
        ],
        axis=1,
    )
    conv_b_full = jnp.concatenate(
        [widen(grad_conv_bias[:local_width], my_index, H * P_SIZE, 0), grad_conv_bias[local_width:]]
    )
    small_sums = lax.psum(
        (
            grad_gain_in,
            grad_gain_mid,
            conv_full,
            conv_b_full,
            widen(grad_dt_shift, my_index, H, 0),
            widen(grad_decay, my_index, H, 0),
            widen(grad_skip, my_index, H, 0),
            widen(grad_gain_loc, my_index, H * P_SIZE, 0),
        ),
        ("dp", "tensor"),
    )
    return (
        output,
        grad_tokens,
        small_sums[0],
        g_zx,
        g_dt,
        g_bc,
        small_sums[2],
        small_sums[3],
        small_sums[4],
        small_sums[5],
        small_sums[6],
        small_sums[7],
        g_out,
        small_sums[1],
        g_router,
        g_sgu,
        g_sdown,
        g_egu,
        g_edown,
    )


def solution(mesh):
    return jax.shard_map(
        shards,
        mesh=mesh,
        in_specs=(
            P(("dp", "tensor"), None),
            P("dp", None),
            P(),
            P("dp", None, "tensor"),
            P("dp", "tensor"),
            P(("dp", "tensor"), None),
            P(),
            P(),
            P(),
            P(),
            P(),
            P(),
            P("tensor", "dp"),
            P(),
            P(("dp", "tensor"), None),
            P("dp", None, "tensor"),
            P("tensor", "dp"),
            P(None, "dp", None, "tensor"),
            P(None, "tensor", "dp"),
            P(("dp", "tensor"), None),
        ),
        out_specs=(
            P(("dp", "tensor"), None),
            P(("dp", "tensor"), None),
            P(),
            P("dp", None, "tensor"),
            P("dp", "tensor"),
            P(("dp", "tensor"), None),
            P(),
            P(),
            P(),
            P(),
            P(),
            P(),
            P("tensor", "dp"),
            P(),
            P(("dp", "tensor"), None),
            P("dp", None, "tensor"),
            P("tensor", "dp"),
            P(None, "dp", None, "tensor"),
            P(None, "tensor", "dp"),
        ),
        check_vma=False,
    )
```

profile of v0, /device:TPU:1, one launch (start us, length us, event | category | flops | bytes accessed | tf_op | source)
XLA Modules:
  0.0 6108.5 jit_solution(3910447759484778267)
XLA Ops:
  107.1 49.5 all-gather.15.cloned.1.call-done
  214.3 174.6 %while.114 = (s32[]{:T(128)}, f32[24,128,64]{1,2,0:T(8,128)S(1)}, f32[8,128,24,64]{1,3,2,0:T(8,128)}, f32[8,128,128]{1,2,0:T(8,128)}, f32[8,128,128,24]{2,1,3,0:...) while((s32[]{:T(128)}, f32[24,128,64]{1,2,0:T(8,128)S(1)}, ...), condition=%wide.region_32.33_spmd.clone.clone, body=%wide.region_30.32_spmd.clone.clone.sunk | while | flops 936056832 | bytes 17725656 | solution.py:117
  392.3 76.4 %while.113 = (s32[]{:T(128)}, f32[24,128,64]{1,2,0:T(8,128)S(1)}, f32[8,128,24,64]{1,3,2,0:T(8,128)}, f32[8,128,24]{2,1,0:T(8,128)}, f32[8,128,24,64]{1,3,2,0:T(...) while((s32[]{:T(128)}, f32[24,128,64]{1,2,0:T(8,128)S(1)}, ...), condition=%wide.region_3.4_spmd.clone.clone, body=%wide.region_1.3_spmd.clone.clone.sunk | while | flops 934281216 | bytes 8487019 | solution.py:117
  715.0 76.3 %all-gather.23.cloned.1.call-done = bf16[16,256,1536]{1,0,2:T(8,128)(2,1)} async-done(((bf16[16,256,96]{1,0,2:T(8,128)(2,1)}), bf16[16,256,1536]{1,0,2:T(8,128)(2,1)}) %all-gather.23.cloned.1.call-update) | async-done | bytes 12582928 | tf_op jit(solution)/shard_map/all_gather | solution.py:207
  959.8 194.6 %all-gather.21.cloned.1.call-done = bf16[16,1536,2,256]{3,1,2,0:T(8,128)(2,1)} async-done(((bf16[16,96,2,256]{3,1,2,0:T(8,128)(2,1)}), bf16[16,1536,2,256]{3,1,2,0:T(8,128)(2,1)}) %all-gather.21.cloned.1.call-update) | async-done | bytes 25165840 | tf_op jit(solution)/shard_map/all_gather | solution.py:206
  1182.2 1868.8 %while.112 = (s32[]{:T(128)}, f32[1024,1536]{1,0:T(8,128)}, f32[16,1536,2,256]{3,0,2,1:T(8,128)}, f32[16,256,1536]{1,2,0:T(8,128)}, f32[16,416]{1,0:T(8,128)S(1)...) while((s32[]{:T(128)}, f32[1024,1536]{1,0:T(8,128)}, ...), condition=%wide.region_23.24_spmd, body=%wide.region_20.23_spmd.sunk | while | flops 2300208896 | bytes 47310156 | solution.py:344
  1223.8 69.2 %dynamic_update_slice.262 = f32[16,1536,2,256]{3,0,2,1:T(8,128)} dynamic-update-slice(f32[16,1536,2,256]{3,0,2,1:T(8,128)} %get-tuple-element.2752, f32[1,1536,2,256]{3,0,2,1:T(1,128)} %copy.475, s32[]{:T(128)S(6)} %copy.580, s32[]{:T(128)} %constant.311.clone.1..sunk, s32[]{:T(128)} %constant.311.clone.1..sunk, s32[]{:T(128)} %constant.311.clone.1..sunk) | dynamic-update-slice | bytes 6291460 | tf_op jit(solution)/shard_map/while/body/jit(dynamic_update_index_in_dim)/dynamic_update_slice | solution.py:344
  1340.6 69.2 %dynamic_update_slice.262 = f32[16,1536,2,256]{3,0,2,1:T(8,128)} dynamic-update-slice(f32[16,1536,2,256]{3,0,2,1:T(8,128)} %get-tuple-element.2752, f32[1,1536,2,256]{3,0,2,1:T(1,128)} %copy.475, s32[]{:T(128)S(6)} %copy.580, s32[]{:T(128)} %constant.311.clone.1..sunk, s32[]{:T(128)} %constant.311.clone.1..sunk, s32[]{:T(128)} %constant.311.clone.1..sunk) | dynamic-update-slice | bytes 6291460 | tf_op jit(solution)/shard_map/while/body/jit(dynamic_update_index_in_dim)/dynamic_update_slice | solution.py:344
  1457.4 69.2 %dynamic_update_slice.262 = f32[16,1536,2,256]{3,0,2,1:T(8,128)} dynamic-update-slice(f32[16,1536,2,256]{3,0,2,1:T(8,128)} %get-tuple-element.2752, f32[1,1536,2,256]{3,0,2,1:T(1,128)} %copy.475, s32[]{:T(128)S(6)} %copy.580, s32[]{:T(128)} %constant.311.clone.1..sunk, s32[]{:T(128)} %constant.311.clone.1..sunk, s32[]{:T(128)} %constant.311.clone.1..sunk) | dynamic-update-slice | bytes 6291460 | tf_op jit(solution)/shard_map/while/body/jit(dynamic_update_index_in_dim)/dynamic_update_slice | solution.py:344
  1574.3 69.2 %dynamic_update_slice.262 = f32[16,1536,2,256]{3,0,2,1:T(8,128)} dynamic-update-slice(f32[16,1536,2,256]{3,0,2,1:T(8,128)} %get-tuple-element.2752, f32[1,1536,2,256]{3,0,2,1:T(1,128)} %copy.475, s32[]{:T(128)S(6)} %copy.580, s32[]{:T(128)} %constant.311.clone.1..sunk, s32[]{:T(128)} %constant.311.clone.1..sunk, s32[]{:T(128)} %constant.311.clone.1..sunk) | dynamic-update-slice | bytes 6291460 | tf_op jit(solution)/shard_map/while/body/jit(dynamic_update_index_in_dim)/dynamic_update_slice | solution.py:344
  1691.1 69.2 %dynamic_update_slice.262 = f32[16,1536,2,256]{3,0,2,1:T(8,128)} dynamic-update-slice(f32[16,1536,2,256]{3,0,2,1:T(8,128)} %get-tuple-element.2752, f32[1,1536,2,256]{3,0,2,1:T(1,128)} %copy.475, s32[]{:T(128)S(6)} %copy.580, s32[]{:T(128)} %constant.311.clone.1..sunk, s32[]{:T(128)} %constant.311.clone.1..sunk, s32[]{:T(128)} %constant.311.clone.1..sunk) | dynamic-update-slice | bytes 6291460 | tf_op jit(solution)/shard_map/while/body/jit(dynamic_update_index_in_dim)/dynamic_update_slice | solution.py:344
  1807.9 69.2 %dynamic_update_slice.262 = f32[16,1536,2,256]{3,0,2,1:T(8,128)} dynamic-update-slice(f32[16,1536,2,256]{3,0,2,1:T(8,128)} %get-tuple-element.2752, f32[1,1536,2,256]{3,0,2,1:T(1,128)} %copy.475, s32[]{:T(128)S(6)} %copy.580, s32[]{:T(128)} %constant.311.clone.1..sunk, s32[]{:T(128)} %constant.311.clone.1..sunk, s32[]{:T(128)} %constant.311.clone.1..sunk) | dynamic-update-slice | bytes 6291460 | tf_op jit(solution)/shard_map/while/body/jit(dynamic_update_index_in_dim)/dynamic_update_slice | solution.py:344
  1924.7 69.2 %dynamic_update_slice.262 = f32[16,1536,2,256]{3,0,2,1:T(8,128)} dynamic-update-slice(f32[16,1536,2,256]{3,0,2,1:T(8,128)} %get-tuple-element.2752, f32[1,1536,2,256]{3,0,2,1:T(1,128)} %copy.475, s32[]{:T(128)S(6)} %copy.580, s32[]{:T(128)} %constant.311.clone.1..sunk, s32[]{:T(128)} %constant.311.clone.1..sunk, s32[]{:T(128)} %constant.311.clone.1..sunk) | dynamic-update-slice | bytes 6291460 | tf_op jit(solution)/shard_map/while/body/jit(dynamic_update_index_in_dim)/dynamic_update_slice | solution.py:344
  2041.5 69.2 %dynamic_update_slice.262 = f32[16,1536,2,256]{3,0,2,1:T(8,128)} dynamic-update-slice(f32[16,1536,2,256]{3,0,2,1:T(8,128)} %get-tuple-element.2752, f32[1,1536,2,256]{3,0,2,1:T(1,128)} %copy.475, s32[]{:T(128)S(6)} %copy.580, s32[]{:T(128)} %constant.311.clone.1..sunk, s32[]{:T(128)} %constant.311.clone.1..sunk, s32[]{:T(128)} %constant.311.clone.1..sunk) | dynamic-update-slice | bytes 6291460 | tf_op jit(solution)/shard_map/while/body/jit(dynamic_update_index_in_dim)/dynamic_update_slice | solution.py:344
  2158.3 69.2 %dynamic_update_slice.262 = f32[16,1536,2,256]{3,0,2,1:T(8,128)} dynamic-update-slice(f32[16,1536,2,256]{3,0,2,1:T(8,128)} %get-tuple-element.2752, f32[1,1536,2,256]{3,0,2,1:T(1,128)} %copy.475, s32[]{:T(128)S(6)} %copy.580, s32[]{:T(128)} %constant.311.clone.1..sunk, s32[]{:T(128)} %constant.311.clone.1..sunk, s32[]{:T(128)} %constant.311.clone.1..sunk) | dynamic-update-slice | bytes 6291460 | tf_op jit(solution)/shard_map/while/body/jit(dynamic_update_index_in_dim)/dynamic_update_slice | solution.py:344
  2275.1 69.2 %dynamic_update_slice.262 = f32[16,1536,2,256]{3,0,2,1:T(8,128)} dynamic-update-slice(f32[16,1536,2,256]{3,0,2,1:T(8,128)} %get-tuple-element.2752, f32[1,1536,2,256]{3,0,2,1:T(1,128)} %copy.475, s32[]{:T(128)S(6)} %copy.580, s32[]{:T(128)} %constant.311.clone.1..sunk, s32[]{:T(128)} %constant.311.clone.1..sunk, s32[]{:T(128)} %constant.311.clone.1..sunk) | dynamic-update-slice | bytes 6291460 | tf_op jit(solution)/shard_map/while/body/jit(dynamic_update_index_in_dim)/dynamic_update_slice | solution.py:344
  2391.8 69.2 %dynamic_update_slice.262 = f32[16,1536,2,256]{3,0,2,1:T(8,128)} dynamic-update-slice(f32[16,1536,2,256]{3,0,2,1:T(8,128)} %get-tuple-element.2752, f32[1,1536,2,256]{3,0,2,1:T(1,128)} %copy.475, s32[]{:T(128)S(6)} %copy.580, s32[]{:T(128)} %constant.311.clone.1..sunk, s32[]{:T(128)} %constant.311.clone.1..sunk, s32[]{:T(128)} %constant.311.clone.1..sunk) | dynamic-update-slice | bytes 6291460 | tf_op jit(solution)/shard_map/while/body/jit(dynamic_update_index_in_dim)/dynamic_update_slice | solution.py:344
  2508.6 69.2 %dynamic_update_slice.262 = f32[16,1536,2,256]{3,0,2,1:T(8,128)} dynamic-update-slice(f32[16,1536,2,256]{3,0,2,1:T(8,128)} %get-tuple-element.2752, f32[1,1536,2,256]{3,0,2,1:T(1,128)} %copy.475, s32[]{:T(128)S(6)} %copy.580, s32[]{:T(128)} %constant.311.clone.1..sunk, s32[]{:T(128)} %constant.311.clone.1..sunk, s32[]{:T(128)} %constant.311.clone.1..sunk) | dynamic-update-slice | bytes 6291460 | tf_op jit(solution)/shard_map/while/body/jit(dynamic_update_index_in_dim)/dynamic_update_slice | solution.py:344
  2625.4 69.2 %dynamic_update_slice.262 = f32[16,1536,2,256]{3,0,2,1:T(8,128)} dynamic-update-slice(f32[16,1536,2,256]{3,0,2,1:T(8,128)} %get-tuple-element.2752, f32[1,1536,2,256]{3,0,2,1:T(1,128)} %copy.475, s32[]{:T(128)S(6)} %copy.580, s32[]{:T(128)} %constant.311.clone.1..sunk, s32[]{:T(128)} %constant.311.clone.1..sunk, s32[]{:T(128)} %constant.311.clone.1..sunk) | dynamic-update-slice | bytes 6291460 | tf_op jit(solution)/shard_map/while/body/jit(dynamic_update_index_in_dim)/dynamic_update_slice | solution.py:344
  2742.1 69.2 %dynamic_update_slice.262 = f32[16,1536,2,256]{3,0,2,1:T(8,128)} dynamic-update-slice(f32[16,1536,2,256]{3,0,2,1:T(8,128)} %get-tuple-element.2752, f32[1,1536,2,256]{3,0,2,1:T(1,128)} %copy.475, s32[]{:T(128)S(6)} %copy.580, s32[]{:T(128)} %constant.311.clone.1..sunk, s32[]{:T(128)} %constant.311.clone.1..sunk, s32[]{:T(128)} %constant.311.clone.1..sunk) | dynamic-update-slice | bytes 6291460 | tf_op jit(solution)/shard_map/while/body/jit(dynamic_update_index_in_dim)/dynamic_update_slice | solution.py:344
  2858.9 69.2 %dynamic_update_slice.262 = f32[16,1536,2,256]{3,0,2,1:T(8,128)} dynamic-update-slice(f32[16,1536,2,256]{3,0,2,1:T(8,128)} %get-tuple-element.2752, f32[1,1536,2,256]{3,0,2,1:T(1,128)} %copy.475, s32[]{:T(128)S(6)} %copy.580, s32[]{:T(128)} %constant.311.clone.1..sunk, s32[]{:T(128)} %constant.311.clone.1..sunk, s32[]{:T(128)} %constant.311.clone.1..sunk) | dynamic-update-slice | bytes 6291460 | tf_op jit(solution)/shard_map/while/body/jit(dynamic_update_index_in_dim)/dynamic_update_slice | solution.py:344
  2975.7 69.2 %dynamic_update_slice.262 = f32[16,1536,2,256]{3,0,2,1:T(8,128)} dynamic-update-slice(f32[16,1536,2,256]{3,0,2,1:T(8,128)} %get-tuple-element.2752, f32[1,1536,2,256]{3,0,2,1:T(1,128)} %copy.475, s32[]{:T(128)S(6)} %copy.580, s32[]{:T(128)} %constant.311.clone.1..sunk, s32[]{:T(128)} %constant.311.clone.1..sunk, s32[]{:T(128)} %constant.311.clone.1..sunk) | dynamic-update-slice | bytes 6291460 | tf_op jit(solution)/shard_map/while/body/jit(dynamic_update_index_in_dim)/dynamic_update_slice | solution.py:344
  3215.8 239.7 %while.115 = (s32[]{:T(128)}, f32[24,128,64]{1,2,0:T(8,128)S(1)}, f32[8,128,24,64]{1,3,2,0:T(8,128)}, f32[8,128,128]{2,1,0:T(8,128)S(1)}, f32[8,128,128]{2,1,0:T...) while((s32[]{:T(128)}, f32[24,128,64]{1,2,0:T(8,128)S(1)}, ...), condition=%wide.region_44.45_spmd.clone.clone, body=%wide.region_35.44_spmd.clone.clone.sunk | while | flops 1868990464 | bytes 46328864 | solution.py:117
  3591.8 211.3 %while.111 = (s32[]{:T(128)}, f32[1024,1536]{1,0:T(8,128)}, s32[16,416]{1,0:T(8,128)}, bf16[16,416,256]{2,1,0:T(8,128)(2,1)}, bf16[16,256,1536]{2,1,0:T(8,128)(2,1)}, /*index=5*/f32[16,416]{1,0:T(8,128)}, s32[]{:T(128)}) while((s32[]{:T(128)}, f32[1024,1536]{1,0:T(8,128)}, s32[16,416]{1,0:T(8,128)}, bf16[16,416,256]{2,1,0:T(8,128)(2,1)}, ...), condition=%wide.region_18.19_spmd, body=%wide.region_16.18_spmd.sunk | while | flops 328434912 | bytes 11234141 | solution.py:306
  3899.6 125.7 %reduce-scatter.40.cloned.1.call-done = f32[96,24]{1,0:T(8,128)} async-done(((f32[1536,24]{1,0:T(8,128)}), f32[96,24]{1,0:T(8,128)}) %reduce-scatter.40.cloned.1.call-update) | async-done | bytes 9232
  4050.0 284.0 %reduce-scatter.26.cloned.1.call-done = f32[96,2,1536]{2,0,1:T(8,128)} async-done(((f32[1536,2,1536]{2,0,1:T(8,128)}), f32[96,2,1536]{2,0,1:T(8,128)}) %reduce-scatter.26.cloned.1.call-update) | async-done | bytes 1179664 | tf_op jit(solution)/shard_map/reduce_scatter | solution.py:382
  4337.2 702.5 %reduce-scatter.36.cloned.1.call-done = f32[16,96,2,256]{3,0,2,1:T(8,128)} async-done(((f32[16,1536,2,256]{3,0,2,1:T(8,128)}), f32[16,96,2,256]{3,0,2,1:T(8,128)}) %reduce-scatter.36.cloned.1.call-update) | async-done | bytes 3145744 | tf_op jit(solution)/shard_map/reduce_scatter | solution.py:393
  5045.6 128.0 %reduce-scatter.34.cloned.1.call-done = f32[512,96]{0,1:T(8,128)} async-done(((f32[512,1536]{0,1:T(8,128)}), f32[512,96]{0,1:T(8,128)}) %reduce-scatter.34.cloned.1.call-update) | async-done | bytes 196624 | tf_op jit(solution)/shard_map/reduce_scatter | solution.py:386
  5173.6 102.9 %reduce-scatter.28.cloned.1.call-done = f32[48,256]{1,0:T(8,128)} async-done(((f32[1536,256]{1,0:T(8,128)}), f32[48,256]{1,0:T(8,128)}) %reduce-scatter.28.cloned.1.call-update) | async-done | bytes 49168 | tf_op jit(solution)/shard_map/reduce_scatter | solution.py:389
  5276.5 266.4 %all-reduce.19.cloned.1.call-done = (f32[1536]{0:T(1024)}, f32[4,3328]{1,0:T(4,128)}, f32[3328]{0:T(1024)}, f32[48]{0:T(128)}, f32[48]{0:T(128)}, /*index=5*/f32[48]{0:T(128)}, f32[3072]{0:T(1024)}, f32[1536]{0:T(1024)}) async-done(((f32[1536]{0:T(1024)}, f32[4,3328]{1,0:T(4,128)}, f32[3328]{0:T(1024)}, f32[48]{0:T(128)}, f32[48]{0:T(128)}, /*index=5*/f32[48]{0:T(128)}, f32[3072]{0:T(1024)}, ...) | async-done | bytes 91728 | tf_op jit(solution)/shard_map/psum | solution.py:406
  5542.9 178.8 %reduce-scatter.30.cloned.1.call-done = f32[1536,96]{0,1:T(8,128)} async-done(((f32[1536,1536]{0,1:T(8,128)}), f32[1536,96]{0,1:T(8,128)}) %reduce-scatter.30.cloned.1.call-update) | async-done | bytes 589840 | tf_op jit(solution)/shard_map/reduce_scatter | solution.py:384
  5721.8 369.7 %reduce-scatter.38.cloned.1.call-done = f32[16,256,96]{1,2,0:T(8,128)} async-done(((f32[16,256,1536]{1,2,0:T(8,128)}), f32[16,256,96]{1,2,0:T(8,128)}) %reduce-scatter.38.cloned.1.call-update) | async-done | bytes 1572880 | tf_op jit(solution)/shard_map/reduce_scatter | solution.py:394
  (1400 shorter events, 2503.7 us)
Async XLA Ops:
  7.3 90.4 %all-gather.13.cloned.1.call-start = ((), (), s32[]{:S(2)}) async-start(), calls=%async_computation.13 | async-start | bytes 4718592 | tf_op jit(solution)/shard_map/all_gather | solution.py:183
  13.4 143.1 %all-gather.15.cloned.1.call-start = ((), (), s32[]{:S(2)}) async-start(), calls=%async_computation.14 | async-start | bytes 10027008 | tf_op jit(solution)/shard_map/all_gather | solution.py:196
  14.4 527.5 %all-gather.17.cloned.1.call-start = ((), (), s32[]{:S(2)}) async-start(), calls=%async_computation.15 | async-start | bytes 5013504 | tf_op jit(solution)/shard_map/all_gather | solution.py:198
  15.1 549.2 %reduce-scatter.18.cloned.1.call-start = ((), (), s32[]{:S(2)}) async-start(), calls=%async_computation.16 | async-start | bytes 9437184 | tf_op jit(solution)/shard_map/reduce_scatter | solution.py:187
  551.2 159.1 %all-gather.25.cloned.1.call-start = ((), (), s32[]{:S(2)}) async-start(), calls=%async_computation.20 | async-start | bytes 3342336 | tf_op jit(solution)/shard_map/all_gather | solution.py:199
  552.8 238.5 %all-gather.23.cloned.1.call-start = ((), (), s32[]{:S(2)}) async-start(), calls=%async_computation.19 | async-start | bytes 13369344 | tf_op jit(solution)/shard_map/all_gather | solution.py:207
  554.2 254.2 %all-gather.19.cloned.1.call-start = ((), (), s32[]{:S(2)}) async-start(), calls=%async_computation.17 | async-start | bytes 4718592 | tf_op jit(solution)/shard_map/all_gather | solution.py:183
  569.9 375.8 %all-gather.27.cloned.1.call-start = ((), (), s32[]{:S(2)}) async-start(), calls=%async_computation.21 | async-start | bytes 1671168 | tf_op jit(solution)/shard_map/all_gather | solution.py:200
  570.6 375.1 %all-gather.29.cloned.1.call-start = ((), (), s32[]{:S(2)}) async-start(), calls=%async_computation.23 | async-start | bytes 4718592 | tf_op jit(solution)/shard_map/all_gather | solution.py:183
  571.4 583.0 %all-gather.21.cloned.1.call-start = ((), (), s32[]{:S(2)}) async-start(), calls=%async_computation.18 | async-start | bytes 26738688 | tf_op jit(solution)/shard_map/all_gather | solution.py:206
  572.9 2569.4 %reduce-scatter.22.cloned.1.call-start = ((), (), s32[]{:S(2)}) async-start(), calls=%async_computation.24 | async-start | bytes 9437184 | tf_op jit(solution)/shard_map/reduce_scatter | solution.py:187
  580.9 127.4 %copy-start.67 = (s32[6144,1]{0,1:T(1,128)}, s32[6144,1]{0,1:T(1,128)S(1)}, u32[]{:S(2)}) copy-start(s32[6144,1]{0,1:T(1,128)S(1)} %compare_select_fusion.5) | copy-start | bytes 73732
  648.0 160.4 %copy-start.47 = (bf16[1536,16]{0,1:T(8,128)(2,1)}, bf16[1536,16]{0,1:T(8,128)(2,1)S(1)}, u32[]{:S(2)}) copy-start(bf16[1536,16]{0,1:T(8,128)(2,1)S(1)} %reshape.804) | copy-start | bytes 147460
  1182.2 1868.9 %copy-start.53 = (s32[6144]{0:T(1024)S(1)}, s32[6144]{0:T(1024)}, u32[]{:S(2)}) copy-start(s32[6144]{0:T(1024)} %copy-done.52) | copy-start | bytes 73732
  3128.7 33.3 all-gather.31.cloned.1.call-start
  3148.5 704.3 %reduce-scatter.24.cloned.1.call-start = ((), (), s32[]{:S(2)}) async-start(), calls=%async_computation.26 | async-start | bytes 9437184 | tf_op jit(solution)/shard_map/reduce_scatter | solution.py:187
  3567.0 300.0 %reduce-scatter.32.cloned.1.call-start = ((), (), s32[]{:S(2)}) async-start(), calls=%async_computation.30 | async-start | bytes 6684672 | tf_op jit(solution)/shard_map/reduce_scatter | solution.py:385
  3575.9 322.4 %reduce-scatter.42.cloned.1.call-start = ((), (), s32[]{:S(2)}) async-start(), calls=%async_computation.35 | async-start | bytes 811008
  3803.2 222.2 %reduce-scatter.40.cloned.1.call-start = ((), (), s32[]{:S(2)}) async-start(), calls=%async_computation.34 | async-start | bytes 835584
  3807.2 236.0 %reduce-scatter.20.cloned.1.call-start = ((), (), s32[]{:S(2)}) async-start(), calls=%async_computation.22 | async-start | bytes 9437184 | tf_op jit(solution)/shard_map/reduce_scatter | solution.py:187
  3814.5 519.5 %reduce-scatter.26.cloned.1.call-start = ((), (), s32[]{:S(2)}) async-start(), calls=%async_computation.27 | async-start | bytes 20054016 | tf_op jit(solution)/shard_map/reduce_scatter | solution.py:382
  3835.5 1204.2 %reduce-scatter.36.cloned.1.call-start = ((), (), s32[]{:S(2)}) async-start(), calls=%async_computation.32 | async-start | bytes 53477376 | tf_op jit(solution)/shard_map/reduce_scatter | solution.py:393
  3836.2 1337.4 %reduce-scatter.34.cloned.1.call-start = ((), (), s32[]{:S(2)}) async-start(), calls=%async_computation.31 | async-start | bytes 3342336 | tf_op jit(solution)/shard_map/reduce_scatter | solution.py:386
  3842.4 1434.2 %reduce-scatter.28.cloned.1.call-start = ((), (), s32[]{:S(2)}) async-start(), calls=%async_computation.28 | async-start | bytes 1622016 | tf_op jit(solution)/shard_map/reduce_scatter | solution.py:389
  3849.8 1693.1 %all-reduce.19.cloned.1.call-start = ((), (), s32[]{:S(2)}) async-start(), calls=%async_computation.36 | async-start | bytes 199680 | tf_op jit(solution)/shard_map/psum | solution.py:406
  3856.4 1865.4 %reduce-scatter.30.cloned.1.call-start = ((), (), s32[]{:S(2)}) async-start(), calls=%async_computation.29 | async-start | bytes 10027008 | tf_op jit(solution)/shard_map/reduce_scatter | solution.py:384
  3866.4 2225.1 %reduce-scatter.38.cloned.1.call-start = ((), (), s32[]{:S(2)}) async-start(), calls=%async_computation.33 | async-start | bytes 26738688 | tf_op jit(solution)/shard_map/reduce_scatter | solution.py:394
  3866.6 160.2 %copy-start.101 = (f32[512]{0:T(512)S(1)}, f32[512]{0:T(512)}, u32[]{:S(2)}) copy-start(f32[512]{0:T(512)} %copy-done.100) | copy-start | bytes 6148
  3866.6 176.6 %copy-start.6 = (f32[512,1536]{1,0:T(8,128)S(1)}, f32[512,1536]{1,0:T(8,128)}, u32[]{:S(2)}) copy-start(f32[512,1536]{1,0:T(8,128)} %copy-done.4) | copy-start | bytes 9437188
  3866.6 176.6 %copy-start.59 = (f32[1536]{0:T(1024)S(1)}, f32[1536]{0:T(1024)}, u32[]{:S(2)}) copy-start(f32[1536]{0:T(1024)} %param.43) | copy-start | bytes 18436
  3866.6 176.6 %copy-start.82 = (f32[512]{0:T(512)S(1)}, f32[512]{0:T(512)}, u32[]{:S(2)}) copy-start(f32[512]{0:T(512)} %copy-done.80) | copy-start | bytes 6148
  3866.6 176.6 %copy-start.99 = (f32[512]{0:T(512)S(1)}, f32[512]{0:T(512)}, u32[]{:S(2)}) copy-start(f32[512]{0:T(512)} %copy-done.98) | copy-start | bytes 6148
  (155 other events, 2834.5 us)
Sparse Core Ops, SparseCore 0:
  13.6 14.6 all-gather.12
  31.5 125.0 all-gather.14
  159.4 78.3 all-gather.16
  551.3 12.9 reduce-scatter.17
  567.7 68.8 all-gather.24
  640.2 151.0 all-gather.22
  793.5 11.0 all-gather.18
  807.8 57.6 all-gather.26
  867.1 12.2 all-gather.28
  882.8 271.5 all-gather.20
  3128.8 13.5 reduce-scatter.21
  3148.6 13.2 all-gather.30
  3567.1 15.6 reduce-scatter.23
  3588.7 145.6 reduce-scatter.31
  3803.3 94.8 reduce-scatter.41
  3904.1 121.2 reduce-scatter.39
  4027.6 15.5 reduce-scatter.19
  4048.8 285.1 reduce-scatter.25
  4339.9 699.6 reduce-scatter.35
  5045.8 127.7 reduce-scatter.33
  5180.3 96.1 reduce-scatter.27
  5285.3 257.6 all-reduce.18
  5550.5 171.1 reduce-scatter.29
  5728.9 362.5 reduce-scatter.37
where the time goes:
time: 6160 us; the launch traced here: 6110 us
  waiting for transfers between devices  2560 us (42%)
  local copies, waits for them, and re-layouts  1970 us (32%)
  matrix products  744 us (12%)
  other arithmetic  684 us (11%)
  blocking collectives  128 us (2%)
    dynamic_update_slice x48, local copies, waits for them, and re-layouts, shards(): lax.scan(expert_back, jnp.zeros((SEQ, D), jnp.float32), (token_table, gat...  1250 us
    reduce_scatter x1, waiting for transfers between devices, shards(): lax.psum_scatter(egu_grads, 'dp', scatter_dimension=1, tiled=True)  702 us
    reduce_scatter x1, waiting for transfers between devices, shards(): lax.psum_scatter(edown_grads, 'dp', scatter_dimension=2, tiled=True)  370 us
    reduce_scatter x1, waiting for transfers between devices, shards(): lax.psum_scatter(grad_zx, 'dp', scatter_dimension=0, tiled=True)  284 us
    psum x1, waiting for transfers between devices, shards(): lax.psum((grad_gain_in, grad_gain_mid, conv_full, conv_b_full, widen(grad...  266 us
    all_gather x1, waiting for transfers between devices, routed_weights(): lax.all_gather(expert_gu, 'dp', axis=1, tiled=True)  195 us
    reduce_scatter x1, waiting for transfers between devices, shards(): lax.psum_scatter(grad_out_w, 'dp', scatter_dimension=1, tiled=True)  179 us
    scatter-add x16, other arithmetic, expert_back(): return (d_mid_acc.at[row_ids].add(d_in), (grad_gu, grad_down, d_weight))  177 us
  transfers between devices with their start and end apart: 24, of which 16 were waited for; matrix products, arithmetic and copies ran while one was open for 16% of the time, Pallas kernels for 0%

commit v1 on v0

v1 whole, which is shorter than its diff:
```python
import functools

import jax
import jax.numpy as jnp
from jax import lax
from jax.experimental import pallas as pl
from jax.experimental.pallas import tpu as pltpu
from jax.sharding import PartitionSpec as P

F32 = jnp.float32
BF = jnp.bfloat16
EPS = 1e-05
H = 48
P_SIZE = 64
NS = 128
EXPERTS = 16
BL = 128
GROUP = 4
LANES = 128
VMEM = 60 * 1024 * 1024
highest = lax.Precision.HIGHEST


def nn(left, right):
    return lax.dot_general(left, right, (((1,), (0,)), ((), ())), preferred_element_type=F32)


def nt(left, right):
    return lax.dot_general(left, right, (((1,), (1,)), ((), ())), preferred_element_type=F32)


def tn(left, right, kind=F32):
    return lax.dot_general(left, right, (((0,), (0,)), ((), ())), preferred_element_type=kind)


def hop(values, bits):
    count = lax.axis_size("dp")
    return lax.ppermute(values, "dp", [(i, i ^ bits) for i in range(count)])


def next_line(values):
    count = lax.axis_size("dp")
    return lax.ppermute(values, "dp", [(i, (i + GROUP) % count) for i in range(count)])


def swap(values):
    return lax.ppermute(values, "tensor", [(0, 1), (1, 0)])


def pick(values, index, axis=0):
    return lax.dynamic_index_in_dim(values, index, axis, keepdims=False)


def in_order(mine, theirs, core):
    return jnp.where(
        core == 0, jnp.concatenate([mine, theirs]), jnp.concatenate([theirs, mine])
    )


def ring(block, lines):
    blocks = [block]
    for _ in range(lines - 1):
        blocks.append(next_line(blocks[-1]))
    return blocks


def gather_blocks(block, first, lines):
    own = jnp.stack(ring(block, lines))
    second = 3 - first
    near = hop(own, first)
    found = {0: own, first: near, second: hop(own, second), 3: hop(near, second)}
    return [found[k] for k in range(GROUP)]


def assemble(parts, targets):
    inner, height, width = parts[0].shape
    total = len(parts) * inner
    if height % 32:
        flat = jnp.concatenate(parts)
        source = jnp.zeros((total,), jnp.int32).at[targets].set(jnp.arange(total, dtype=jnp.int32))
        return flat[source].reshape(total * height, width)

    def body(target_ref, *refs):
        out_ref, sems = refs[-2], refs[-1]
        copies = []
        for i in range(len(parts)):
            for j in range(inner):
                number = i * inner + j
                start = pl.multiple_of(target_ref[number] * height, height)
                copies.append(
                    pltpu.make_async_copy(
                        refs[i].at[j], out_ref.at[pl.ds(start, height)], sems.at[number]
                    )
                )
        for copy in copies:
            copy.start()
        for copy in copies:
            copy.wait()

    return pl.pallas_call(
        body,
        out_shape=jax.ShapeDtypeStruct((total * height, width), parts[0].dtype),
        in_specs=[pl.BlockSpec(memory_space=pltpu.SMEM)]
        + [pl.BlockSpec(memory_space=pl.ANY)] * len(parts),
        out_specs=pl.BlockSpec(memory_space=pltpu.VMEM),
        scratch_shapes=[pltpu.SemaphoreType.DMA((total,))],
        compiler_params=pltpu.CompilerParams(vmem_limit_bytes=VMEM),
        cost_estimate=pl.CostEstimate(
            flops=0, bytes_accessed=4 * total * height * width, transcendentals=0
        ),
        name="assemble",
    )(targets, *parts)


def line_sum(blocks, line, lines):
    if lines == 1:
        return blocks[0].astype(F32)
    held = pick(blocks, lax.rem(line - 1 + lines, lines))
    for step in range(1, lines):
        came = next_line(held.astype(BF))
        mine = pick(blocks, lax.rem(line - 1 - step + 2 * lines, lines))
        held = came.astype(F32) + mine.astype(F32)
    return held


def block_sum(values, first, place, line, lines):
    rows, width = values.shape
    parts = values.reshape(lines, 2, 2, rows // (lines * GROUP), width)
    axes = {1: (2, lax.rem(place, 2)), 2: (1, place // 2)}
    axis, own = axes[first]
    sent = hop(pick(parts, 1 - own, axis).astype(BF), first)
    parts = pick(parts, own, axis).astype(F32) + sent.astype(F32)
    second = 3 - first
    own = axes[second][1]
    sent = hop(pick(parts, 1 - own, 1).astype(BF), second)
    parts = pick(parts, own, 1) + sent.astype(F32)
    return line_sum(parts, line, lines)


def share_group(piece):
    half = piece.shape[0] // 2
    along_x, along_y = hop(piece, 1), hop(piece, 2)
    across = jnp.concatenate([hop(along_x[:half], 2), hop(along_y[half:], 1)])
    return [piece, along_x, along_y, across]


def sum_group(parts):
    half = parts[3].shape[0] // 2
    over_x = hop(parts[3][:half].astype(BF), 1).astype(F32)
    over_y = hop(parts[3][half:].astype(BF), 2).astype(F32)
    to_y = jnp.concatenate([parts[2][:half] + over_x, parts[2][half:]])
    to_x = jnp.concatenate([parts[1][:half], parts[1][half:] + over_y])
    return (
        parts[0] + hop(to_x.astype(BF), 1).astype(F32) + hop(to_y.astype(BF), 2).astype(F32)
    )


def total_sum(values):
    values = values + swap(values)
    bits = 1
    while bits < lax.axis_size("dp"):
        values = values + hop(values, bits)
        bits *= 2
    return values


def sigmoid(values):
    return 1.0 / (1.0 + jnp.exp(-values))


def split_two(values):
    high = values.astype(BF)
    return high, (values - high.astype(F32)).astype(BF)


def spread_heads(values, spread):
    high, low = split_two(values)
    packed = high.astype(F32) + pltpu.roll(low.astype(F32), LANES // 2, 1)
    return nn(packed.astype(BF), spread)


def gather_heads(values, spread, heads_on):
    high, low = split_two(values)
    return jnp.where(heads_on, nt(high, spread) + nt(low, spread), 0.0)


def conv_rows(ext, kern, low, high, offset):
    summed = kern[4:5, low:high]
    for j in range(4):
        summed = summed + kern[j : j + 1, low:high] * ext[offset + j : offset + j + BL, low:high]
    return summed


def step_terms(raw, head_par, heads_on):
    shifted = raw + head_par[0:1]
    soft = jnp.maximum(shifted, 0.0) + jnp.log1p(jnp.exp(-jnp.abs(shifted)))
    step = jnp.where(heads_on, soft, 0.0)
    return shifted, step, -step * head_par[1:2]


def front_body(gate_ref, zi_ref, kern_ref, head_ref, spread_ref, y_ref, sq_ref, state_ref, ext, state):
    width = gate_ref.shape[1]
    first = pl.program_id(0) == 0

    @pl.when(first)
    def _():
        ext[0:8, :] = jnp.zeros((8, ext.shape[1]), F32)
        state[...] = jnp.zeros(state.shape, F32)

    @pl.when(jnp.logical_not(first))
    def _():
        ext[0:8, :] = ext[BL : BL + 8, :]

    ext[8 : BL + 8, :] = zi_ref[...]
    rows = lax.broadcasted_iota(jnp.int32, (BL, LANES), 0)
    cols = lax.broadcasted_iota(jnp.int32, (BL, LANES), 1)
    causal = cols <= rows
    heads_on = cols < width // P_SIZE
    spread = spread_ref[...]
    state_ref[0] = state[...]
    pre = conv_rows(ext, kern_ref, 0, width, 5)
    x = pre * sigmoid(pre)
    pre = conv_rows(ext, kern_ref, width + LANES, ext.shape[1], 5)
    maps = pre * sigmoid(pre)
    b, c = maps[:, :NS], maps[:, NS:]
    shifted, step, decay = step_terms(zi_ref[:, width : width + LANES], head_ref, heads_on)
    cum = jnp.dot(causal.astype(F32), decay, precision=highest, preferred_element_type=F32)
    cum_t = cum.T
    last = cum[BL - 1 : BL]
    scores = nt(c.astype(BF), b.astype(BF))
    u = x * spread_heads(step, spread)
    from_start = spread_heads(jnp.where(heads_on, jnp.exp(cum), 0.0), spread)
    to_end = spread_heads(jnp.where(heads_on, jnp.exp(last - cum), 0.0), spread)
    u_low = u.astype(BF)
    left = cols < P_SIZE
    within = []
    for pair in range(width // LANES):
        mats = []
        for head in (2 * pair, 2 * pair + 1):
            gap = cum[:, head : head + 1] - cum_t[head : head + 1, :]
            mats.append((jnp.where(causal, jnp.exp(gap), 0.0) * scores).astype(BF))
        cut = u_low[:, pair * LANES : (pair + 1) * LANES]
        zero = jnp.zeros_like(cut)
        stacked = jnp.concatenate([jnp.where(left, cut, zero), jnp.where(left, zero, cut)], axis=0)
        within.append(nn(jnp.concatenate(mats, axis=1), stacked))
    before = state[...]
    across = nn(c.astype(BF), before.astype(BF)) * from_start
    y = jnp.concatenate(within, axis=1) + across + kern_ref[5:6, :width] * x
    y_ref[...] = y
    gate = gate_ref[...]
    gated = y * gate * sigmoid(gate)
    sq_ref[...] = jnp.broadcast_to(jnp.sum(gated * gated, axis=1, keepdims=True), sq_ref.shape)
    grown = nn(b.T.astype(BF), (u * to_end).astype(BF))
    state[...] = before * from_start[BL - 1 : BL] + grown


def front_scan(gate, zi, kern, head_par, spread):
    length, width = gate.shape
    steps = length // BL
    return pl.pallas_call(
        front_body,
        grid=(steps,),
        out_shape=(
            jax.ShapeDtypeStruct((length, width), F32),
            jax.ShapeDtypeStruct((length, LANES), F32),
            jax.ShapeDtypeStruct((steps, NS, width), F32),
        ),
        in_specs=[
            pl.BlockSpec((BL, width), lambda i: (i, 0)),
            pl.BlockSpec((BL, zi.shape[1]), lambda i: (i, 0)),
            pl.BlockSpec(kern.shape, lambda i: (0, 0)),
            pl.BlockSpec(head_par.shape, lambda i: (0, 0)),
            pl.BlockSpec(spread.shape, lambda i: (0, 0)),
        ],
        out_specs=(
            pl.BlockSpec((BL, width), lambda i: (i, 0)),
            pl.BlockSpec((BL, LANES), lambda i: (i, 0)),
            pl.BlockSpec((1, NS, width), lambda i: (i, 0, 0)),
        ),
        scratch_shapes=[pltpu.VMEM((BL + 8, zi.shape[1]), F32), pltpu.VMEM((NS, width), F32)],
        compiler_params=pltpu.CompilerParams(
            dimension_semantics=("arbitrary",), vmem_limit_bytes=VMEM
        ),
        cost_estimate=pl.CostEstimate(
            flops=40_000_000_000, bytes_accessed=30_000_000, transcendentals=8_000_000
        ),
        name="front_scan",
    )(gate, zi, kern, head_par, spread)


def back_body(
    dsc_ref, y_ref, gate_ref, zi_ref, prev_ref, state_ref, rows_ref, kern_ref, head_ref, spread_ref,
    dz_ref, di_ref, par_ref, hg_ref, ext, ext_d, d_state,
):
    width = gate_ref.shape[1]
    wide = zi_ref.shape[1]
    number = pl.program_id(0)
    steps = pl.num_programs(0)

    @pl.when(number == 0)
    def _():
        ext_d[BL : BL + 8, :] = jnp.zeros((8, wide), F32)
        d_state[...] = jnp.zeros(d_state.shape, F32)
        par_ref[...] = jnp.zeros(par_ref.shape, F32)
        hg_ref[...] = jnp.zeros(hg_ref.shape, F32)

    @pl.when(number > 0)
    def _():
        ext_d[BL : BL + 8, :] = ext_d[0:8, :]

    ext[0:8, :] = jnp.where(number == steps - 1, 0.0, prev_ref[...])
    ext[8 : BL + 8, :] = zi_ref[...]
    rows = lax.broadcasted_iota(jnp.int32, (BL, LANES), 0)
    cols = lax.broadcasted_iota(jnp.int32, (BL, LANES), 1)
    upper = rows <= cols
    strict = rows < cols
    heads_on = cols < width // P_SIZE
    left = cols < P_SIZE
    spread = spread_ref[...]
    pre_x = conv_rows(ext, kern_ref, 0, width, 5)
    sig_x = sigmoid(pre_x)
    x = pre_x * sig_x
    pre_m = conv_rows(ext, kern_ref, width + LANES, wide, 5)
    sig_m = sigmoid(pre_m)
    maps = pre_m * sig_m
    b, c = maps[:, :NS], maps[:, NS:]
    b_low, c_low = b.astype(BF), c.astype(BF)
    shifted, step, decay = step_terms(zi_ref[:, width : width + LANES], head_ref, heads_on)
    cum = jnp.dot(
        (cols <= rows).astype(F32), decay, precision=highest, preferred_element_type=F32
    )
    cum_t = cum.T
    last = cum[BL - 1 : BL]
    step_wide = spread_heads(step, spread)
    from_start = spread_heads(jnp.where(heads_on, jnp.exp(cum), 0.0), spread)
    to_end = spread_heads(jnp.where(heads_on, jnp.exp(last - cum), 0.0), spread)
    whole = from_start[BL - 1 : BL]
    y, gate, d_scaled = y_ref[...], gate_ref[...], dsc_ref[...]
    sig_g = sigmoid(gate)
    silu_g = gate * sig_g
    gated = y * silu_g
    scale, pull = rows_ref[:, 0:1], rows_ref[:, 1:2]
    scaled_in = d_scaled * scale
    d_gated = scaled_in * kern_ref[6:7, :width] - gated * pull
    par_ref[6:7, :width] += jnp.sum(scaled_in * gated, axis=0, keepdims=True)
    d_y = d_gated * silu_g
    dz_ref[...] = (d_gated * y * sig_g * (1.0 + gate * (1.0 - sig_g))).astype(BF)
    par_ref[5:6, :width] += jnp.sum(d_y * x, axis=0, keepdims=True)
    u = x * step_wide
    u_low, dy_low = u.astype(BF), d_y.astype(BF)
    scores_t = nt(b_low, c_low)
    d_scores_t = jnp.zeros((BL, BL), F32)
    du_parts = []
    gap_rows = jnp.zeros((BL, LANES), F32)
    gap_cols = []
    for pair in range(width // LANES):
        lanes = slice(pair * LANES, (pair + 1) * LANES)
        cut_u, cut_d = u_low[:, lanes], dy_low[:, lanes]
        zero = jnp.zeros_like(cut_u)
        stack_u = jnp.concatenate([jnp.where(left, cut_u, zero), jnp.where(left, zero, cut_u)], axis=0)
        stack_d = jnp.concatenate([jnp.where(left, cut_d, zero), jnp.where(left, zero, cut_d)], axis=0)
        d_weights = nt(stack_u, cut_d)
        mats = []
        for place, head in enumerate((2 * pair, 2 * pair + 1)):
            gap = cum_t[head : head + 1, :] - cum[:, head : head + 1]
            decays = jnp.where(upper, jnp.exp(gap), 0.0)
            weight = decays * scores_t
            mats.append(weight.astype(BF))
            d_weight = d_weights[place * BL : (place + 1) * BL]
            d_scores_t = d_scores_t + decays * d_weight
            moved = jnp.where(strict, weight * d_weight, 0.0)
            gap_rows = jnp.where(cols == head, jnp.sum(moved, axis=1, keepdims=True), gap_rows)
            gap_cols.append(jnp.sum(moved, axis=0, keepdims=True))
        du_parts.append(nn(jnp.concatenate(mats, axis=1), stack_d))
    gap_cols.append(jnp.zeros((LANES - width // P_SIZE, BL), F32))
    gap_cols = jnp.concatenate(gap_cols, axis=0).T
    before, d_after = state_ref[0], d_state[...]
    before_low, d_after_low = before.astype(BF), d_after.astype(BF)
    dy_start = d_y * from_start
    dy_start_low = dy_start.astype(BF)
    reach = gather_heads(dy_start * nn(c_low, before_low), spread, heads_on)
    u_end = u * to_end
    d_from_state = nn(b_low, d_after_low)
    kept = gather_heads(u_end * d_from_state, spread, heads_on)
    carried = jnp.sum(before * d_after, axis=0, keepdims=True) * whole
    carried = gather_heads(jnp.broadcast_to(carried, (8, width)), spread, heads_on[:8])[0:1]
    d_c = nt(dy_start_low, before_low) + nn(d_scores_t.T.astype(BF), b_low)
    d_b = nt(u_end.astype(BF), d_after_low) + nn(d_scores_t.astype(BF), c_low)
    d_state[...] = d_after * whole + nn(c.T.astype(BF), dy_start_low)
    d_u = jnp.concatenate(du_parts, axis=1) + to_end * d_from_state
    d_decay = (
        jnp.dot(
            upper.astype(F32), reach + gap_cols - gap_rows, precision=highest,
            preferred_element_type=F32,
        )
        + jnp.dot(
            (cols < rows).astype(F32), kept, precision=highest, preferred_element_type=F32
        )
        + carried
    )
    d_step = gather_heads(x * d_u, spread, heads_on)
    rate = head_ref[1:2]
    d_raw = jnp.where(heads_on, (d_step - rate * d_decay) * sigmoid(shifted), 0.0)
    hg_ref[0:1, :] += jnp.sum(d_raw, axis=0, keepdims=True)
    hg_ref[1:2, :] += jnp.sum(jnp.where(heads_on, d_decay * decay, 0.0), axis=0, keepdims=True)
    d_x = step_wide * d_u + kern_ref[5:6, :width] * d_y
    ext_d[0:BL, :width] = d_x * sig_x * (1.0 + pre_x * (1.0 - sig_x))
    ext_d[0:BL, width : width + LANES] = jnp.zeros((BL, LANES), F32)
    ext_d[0:BL, width + LANES :] = (
        jnp.concatenate([d_b, d_c], axis=1) * sig_m * (1.0 + pre_m * (1.0 - sig_m))
    )
    for low, high in ((0, width), (width + LANES, wide)):
        d_act = ext_d[0:BL, low:high]
        d_in = jnp.zeros((BL, high - low), F32)
        for j in range(4):
            d_in = d_in + kern_ref[j : j + 1, low:high] * ext_d[3 - j : 3 - j + BL, low:high]
            par_ref[j : j + 1, low:high] += jnp.sum(
                d_act * ext[5 + j : 5 + j + BL, low:high], axis=0, keepdims=True
            )
        par_ref[4:5, low:high] += jnp.sum(d_act, axis=0, keepdims=True)
        di_ref[:, low:high] = d_in.astype(BF)
    di_ref[:, width : width + LANES] = d_raw.astype(BF)


def back_scan(d_scaled, y, gate, zi, states, row_par, kern, head_par, spread):
    length, width = gate.shape
    wide = zi.shape[1]
    steps = length // BL
    per = BL // 8

    def back(i):
        return (steps - 1 - i, 0)

    def fixed(i):
        return (0, 0)

    return pl.pallas_call(
        back_body,
        grid=(steps,),
        out_shape=(
            jax.ShapeDtypeStruct((length, width), BF),
            jax.ShapeDtypeStruct((length, wide), BF),
            jax.ShapeDtypeStruct((8, wide), F32),
            jax.ShapeDtypeStruct((8, LANES), F32),
        ),
        in_specs=[
            pl.BlockSpec((BL, width), back),
            pl.BlockSpec((BL, width), back),
            pl.BlockSpec((BL, width), back),
            pl.BlockSpec((BL, wide), back),
            pl.BlockSpec((8, wide), lambda i: (jnp.maximum((steps - 1 - i) * per - 1, 0), 0)),
            pl.BlockSpec((1, NS, width), lambda i: (steps - 1 - i, 0, 0)),
            pl.BlockSpec((BL, LANES), back),
            pl.BlockSpec(kern.shape, fixed),
            pl.BlockSpec(head_par.shape, fixed),
            pl.BlockSpec(spread.shape, fixed),
        ],
        out_specs=(
            pl.BlockSpec((BL, width), back),
            pl.BlockSpec((BL, wide), back),
            pl.BlockSpec((8, wide), fixed),
            pl.BlockSpec((8, LANES), fixed),
        ),
        scratch_shapes=[
            pltpu.VMEM((BL + 8, wide), F32),
            pltpu.VMEM((BL + 8, wide), F32),
            pltpu.VMEM((NS, width), F32),
        ],
        compiler_params=pltpu.CompilerParams(
            dimension_semantics=("arbitrary",), vmem_limit_bytes=VMEM
        ),
        cost_estimate=pl.CostEstimate(
            flops=80_000_000_000, bytes_accessed=60_000_000, transcendentals=12_000_000
        ),
        name="back_scan",
    )(d_scaled, y, gate, zi, zi, states, row_par, kern, head_par, spread)


def expert_body(hidden, units, x_ref, ym_ref, router_ref, w_ref, acts_ref, out_ref, dx_ref, dl_ref, w, sem):
    width = x_ref.shape[1]
    tile = x_ref.shape[0]

    @pl.when(pl.program_id(0) == 0)
    def _():
        copy = pltpu.make_async_copy(w_ref, w, sem)
        copy.start()
        copy.wait()

    lane = lax.broadcasted_iota(jnp.int32, (tile, LANES), 1)
    routed = ym_ref[:, width:].astype(F32) > 0.5
    logits = nn(x_ref[...], router_ref[...])
    top = jnp.max(jnp.where(routed, logits, -1e30), axis=1, keepdims=True)
    powers = jnp.where(routed, jnp.exp(jnp.where(routed, logits - top, 0.0)), 0.0)
    gates = powers / jnp.sum(powers, axis=1, keepdims=True)

    def hidden_part(start, size, gate):
        def columns(which):
            return pl.ds(pl.multiple_of(which * hidden + start, LANES), size)

        x = x_ref[...]
        pre = nn(x, w[:, columns(0)])
        up = nn(x, w[:, columns(1)])
        d_act = nn(ym_ref[:, :width], w[:, columns(2)])
        sig = sigmoid(pre)
        silu = pre * sig
        act = (silu * up).astype(BF).astype(F32)
        d_gate = jnp.sum(act * d_act, axis=1, keepdims=True)
        d_hid = d_act if gate is None else d_act * gate
        acts_ref[:, columns(0)] = (d_hid * up * sig * (1.0 + pre * (1.0 - sig))).astype(BF)
        acts_ref[:, columns(1)] = (d_hid * silu).astype(BF)
        acts_ref[:, columns(2)] = (act if gate is None else act * gate).astype(BF)
        return d_gate

    def one_expert(e, d_gates):
        gate = jnp.sum(jnp.where(lane == e, gates, 0.0), axis=1, keepdims=True)
        return jnp.where(lane == e, hidden_part(e * units, units, gate), d_gates)

    own = EXPERTS // GROUP
    d_gates = lax.fori_loop(0, own, one_expert, jnp.zeros((tile, LANES), F32))
    hidden_part(own * units, hidden - own * units, None)
    mean = jnp.sum(gates * d_gates, axis=1, keepdims=True)
    d_logits = (gates * (d_gates - mean)).astype(BF)
    dl_ref[...] = d_logits
    step = 256

    def one_slice(number, carry):
        rows = pl.ds(pl.multiple_of(number * step, step), step)
        out_ref[:, rows] = nt(acts_ref[:, 2 * hidden :], w[rows, 2 * hidden :]).astype(BF)
        dx_ref[:, rows] = (
            nt(acts_ref[:, : 2 * hidden], w[rows, : 2 * hidden]) + nt(d_logits, router_ref[rows, :])
        ).astype(BF)
        return carry

    lax.fori_loop(0, width // step, one_slice, 0)


def expert_rows(x, ym, router, w, units):
    rows, width = x.shape
    hidden = w.shape[1] // 3
    tile = min(512, rows)
    return pl.pallas_call(
        functools.partial(expert_body, hidden, units),
        grid=(rows // tile,),
        out_shape=(
            jax.ShapeDtypeStruct((rows, 3 * hidden), BF),
            jax.ShapeDtypeStruct((rows, width), BF),
            jax.ShapeDtypeStruct((rows, width), BF),
            jax.ShapeDtypeStruct((rows, LANES), BF),
        ),
        in_specs=[
            pl.BlockSpec((tile, width), lambda i: (i, 0)),
            pl.BlockSpec((tile, ym.shape[1]), lambda i: (i, 0)),
            pl.BlockSpec(router.shape, lambda i: (0, 0)),
            pl.BlockSpec(memory_space=pl.ANY),
        ],
        out_specs=(
            pl.BlockSpec((tile, 3 * hidden), lambda i: (i, 0)),
            pl.BlockSpec((tile, width), lambda i: (i, 0)),
            pl.BlockSpec((tile, width), lambda i: (i, 0)),
            pl.BlockSpec((tile, LANES), lambda i: (i, 0)),
        ),
        scratch_shapes=[pltpu.VMEM(w.shape, BF), pltpu.SemaphoreType.DMA],
        compiler_params=pltpu.CompilerParams(
            dimension_semantics=("arbitrary",), vmem_limit_bytes=VMEM
        ),
        cost_estimate=pl.CostEstimate(
            flops=4 * rows * width * 3 * hidden, bytes_accessed=30_000_000, transcendentals=0
        ),
        name="expert_rows",
    )(x, ym, router, w)


def norm_rows(values):
    return lax.rsqrt(jnp.mean(values * values, axis=-1, keepdims=True) + EPS)


def norm_back(d_rows, values, scale, gain):
    grad_gain = jnp.sum(d_rows * values * scale, axis=0)
    pulled = d_rows * gain
    mean = jnp.mean(values * pulled, axis=-1, keepdims=True)
    return scale * pulled - values * (scale * scale * scale) * mean, grad_gain


def shards(
    tokens, routes, gain_in, w_zx, w_dt, w_bc, conv_w, conv_b, dt_bias, a_log, d_skip, norm_gain,
    w_out, gain_mid, router, shared_gu, shared_down, expert_gu, expert_down, grad_out,
):
    core = lax.axis_index("tensor")
    me = lax.axis_index("dp")
    lines = lax.axis_size("dp") // GROUP
    line, place = me // GROUP, lax.rem(me, GROUP)
    piece, width_d = tokens.shape
    local = w_zx.shape[2]
    heads = w_dt.shape[1]
    units = expert_gu.shape[3]
    own = EXPERTS // GROUP
    inner_all = norm_gain.shape[0]
    height = w_zx.shape[0]

    lines_back = lax.rem(line - jnp.arange(lines, dtype=jnp.int32) + lines, lines)
    members = place ^ jnp.arange(GROUP, dtype=jnp.int32)
    mixer_order = (members[:, None] + GROUP * lines_back[None, :]).reshape(-1)
    expert_order = (members[None, :] + GROUP * lines_back[:, None]).reshape(-1)

    tokens_full = in_order(tokens, swap(tokens), core).astype(F32)
    joint = jnp.concatenate([w_bc, router], axis=1)
    joint = in_order(joint, swap(joint), core)
    bc_cols, router_cols = joint[:, : 2 * NS], joint[:, 2 * NS :]
    pad = jnp.zeros((height, LANES - heads - EXPERTS), BF)
    inner_block = jnp.concatenate([w_zx[:, 1], w_dt, router_cols, pad, bc_cols], axis=1)
    gate_w = assemble(gather_blocks(w_zx[:, 0], 1, lines), mixer_order)
    inner_w = assemble(gather_blocks(inner_block, 2, lines), mixer_order)
    out_w = assemble(gather_blocks(w_out.T, 1, lines), mixer_order)

    by_member = expert_gu.reshape(GROUP, own, height, 2, units).transpose(0, 2, 3, 1, 4)
    by_member = by_member.reshape(GROUP, height, 2, own * units)
    down_member = expert_down.reshape(GROUP, own, units, height).transpose(0, 3, 1, 2)
    down_member = down_member.reshape(GROUP, height, own * units)
    shared_units = shared_gu.shape[2] // GROUP
    sgu_member = shared_gu.reshape(height, 2, GROUP, shared_units).transpose(2, 0, 1, 3)
    sdown_member = shared_down.reshape(GROUP, shared_units, height).transpose(0, 2, 1)
    hidden = own * units + shared_units
    packed = jnp.concatenate(
        [
            by_member[:, :, 0], sgu_member[:, :, 0], by_member[:, :, 1], sgu_member[:, :, 1],
            down_member, sdown_member,
        ],
        axis=2,
    )
    group_block = jnp.stack(
        [pick(packed, members[0])] + [hop(pick(packed, members[k]), k) for k in range(1, GROUP)]
    )
    expert_w = assemble(ring(group_block, lines), expert_order)

    own_routes = lax.dynamic_slice_in_dim(routes, core * piece, piece, 0)
    lane = jnp.arange(LANES, dtype=jnp.int32)
    mask = jnp.any(own_routes[:, :, None] == lane[None, None, :], axis=1).astype(BF)
    back_rows = [
        jnp.concatenate([mine, swap(mine)])
        for mine in share_group(jnp.concatenate([grad_out, mask], axis=1))
    ]

    def own_mask(rows):
        marks = rows[:, width_d : width_d + EXPERTS]
        return jnp.pad(
            jnp.roll(marks, -own * place, axis=1), ((0, 0), (0, LANES - EXPERTS))
        )

    back_rows = [
        jnp.concatenate([rows[:, :width_d], own_mask(rows)], axis=1) for rows in back_rows
    ]

    cut = functools.partial(lax.dynamic_slice_in_dim, start_index=core * local, slice_size=local)
    cut_heads = functools.partial(lax.dynamic_slice_in_dim, start_index=core * heads, slice_size=heads)
    between = jnp.zeros((5, LANES), F32)
    conv_all = jnp.concatenate([conv_w, conv_b[None]])
    kern = jnp.concatenate([cut(conv_all, axis=1), between, conv_all[:, inner_all:]], axis=1)
    tail = jnp.zeros((1, kern.shape[1] - local), F32)
    skip_wide = jnp.repeat(cut_heads(d_skip, axis=0), P_SIZE)[None]
    gain_loc = cut(norm_gain, axis=0)
    kern = jnp.concatenate(
        [
            kern,
            jnp.concatenate([skip_wide, tail], axis=1),
            jnp.concatenate([gain_loc[None], tail], axis=1),
            jnp.zeros((1, kern.shape[1]), F32),
        ]
    )
    head_par = jnp.pad(
        jnp.stack([cut_heads(dt_bias, axis=0), jnp.exp(cut_heads(a_log, axis=0))]),
        ((0, 6), (0, LANES - heads)),
    )
    head_of = jnp.arange(local, dtype=jnp.int32) // P_SIZE
    half_lane = lax.rem(lane, LANES // 2)
    spread = (half_lane[:, None] == head_of[None, :]).astype(BF)

    normed = (tokens_full * norm_rows(tokens_full) * gain_in).astype(BF)
    gate = nn(normed, gate_w)
    zi = nn(normed, inner_w)
    y, squares, states = front_scan(gate, zi, kern, head_par, spread)
    squares = squares[:, 0:1]
    squares = squares + swap(squares)
    row_scale = lax.rsqrt(squares / inner_all + EPS)
    scaled = (y * gate * sigmoid(gate) * row_scale * gain_loc).astype(BF)
    mixed = nt(scaled, out_w)
    mixed_mine = lax.dynamic_slice_in_dim(mixed, core * piece, piece, 0)
    mixed_mine = mixed_mine + swap(lax.dynamic_slice_in_dim(mixed, (1 - core) * piece, piece, 0))
    resid_in = tokens.astype(F32)
    resid = resid_in + mixed_mine
    mid_scale = norm_rows(resid)
    mid = (resid * mid_scale * gain_mid).astype(BF)

    mid_rows = [jnp.concatenate([mine, swap(mine)]) for mine in share_group(mid)]
    router_all = inner_w[:, local + heads : local + heads + EXPERTS]
    router_own = jnp.pad(
        jnp.roll(router_all, -own * place, axis=1), ((0, 0), (0, LANES - EXPERTS))
    )
    done = [expert_rows(x, ym, router_own, expert_w, units) for x, ym in zip(mid_rows, back_rows)]

    def both_cores(rows):
        return rows[:piece].astype(F32) + swap(rows[piece:]).astype(F32)

    d_mid = sum_group([both_cores(item[2]) for item in done])
    branch = sum_group([both_cores(item[1]) for item in done])
    output = (resid + branch).astype(BF)
    x_all = jnp.concatenate(mid_rows)
    dy_all = jnp.concatenate([rows[:, :width_d] for rows in back_rows])
    acts = jnp.concatenate([item[0] for item in done])
    d_logits = jnp.concatenate([item[3] for item in done])
    grad_gu = tn(x_all, acts[:, : 2 * hidden], BF)
    grad_down = tn(dy_all, acts[:, 2 * hidden :], BF)
    grad_router = tn(x_all, d_logits)[:, :EXPERTS]
    grad_router = jnp.roll(grad_router, own * place, axis=1)

    def to_members(grad):
        summed = line_sum(grad.reshape(lines, GROUP, height, -1), line, lines)
        low = summed.astype(BF)
        came = [pick(summed, members[0])] + [
            hop(pick(low, members[k]), k).astype(F32) for k in range(1, GROUP)
        ]
        stacked = jnp.stack(came)
        return jnp.stack([pick(stacked, place ^ k) for k in range(GROUP)])

    g_gu = to_members(grad_gu).reshape(GROUP, height, 2, hidden)
    g_down = to_members(grad_down)
    routed = own * units
    g_egu = g_gu[..., :routed].reshape(GROUP, height, 2, own, units).transpose(0, 3, 1, 2, 4)
    g_egu = g_egu.reshape(EXPERTS, height, 2, units)
    g_edown = g_down[..., :routed].reshape(GROUP, height, own, units).transpose(0, 2, 3, 1)
    g_edown = g_edown.reshape(EXPERTS, units, height)
    g_sgu = g_gu[..., routed:].transpose(1, 2, 0, 3).reshape(height, 2, -1)
    g_sdown = g_down[..., routed:].transpose(0, 2, 1).reshape(-1, height)

    d_extra, grad_gain_mid = norm_back(d_mid, resid, mid_scale, gain_mid)
    d_resid = grad_out.astype(F32) + d_extra
    d_mix = d_resid.astype(BF)
    pulls = jnp.sum(d_mix.astype(F32) * (resid - resid_in), axis=1, keepdims=True)
    pulls = in_order(pulls, swap(pulls), core)
    d_mix = in_order(d_mix, swap(d_mix), core)
    row_par = jnp.concatenate(
        [row_scale, row_scale * row_scale * pulls / inner_all], axis=1
    )
    row_par = jnp.pad(row_par, ((0, 0), (0, LANES - 2)))
    d_scaled = nn(d_mix, out_w)
    grad_out_w = tn(d_mix, scaled, BF)
    dz, di, par_grads, head_grads = back_scan(
        d_scaled, y, gate, zi, states, row_par, kern, head_par, spread
    )
    d_normed = nt(dz, gate_w) + nt(di, inner_w)
    d_mine = lax.dynamic_slice_in_dim(d_normed, core * piece, piece, 0)
    d_mine = d_mine + swap(lax.dynamic_slice_in_dim(d_normed, (1 - core) * piece, piece, 0))
    d_extra, grad_gain_in = norm_back(d_mine, resid_in, norm_rows(resid_in), gain_in)
    grad_tokens = (d_resid + d_extra).astype(BF)

    grad_inner = tn(normed, di)
    grad_inner = lax.dynamic_update_slice(grad_inner, grad_router, (0, local + heads))
    g_out = block_sum(grad_out_w, 1, place, line, lines).T
    g_gate = block_sum(tn(normed, dz, BF), 2, place, line, lines)
    g_inner = block_sum(grad_inner.astype(BF), 1, place, line, lines)
    g_zx = jnp.stack([g_gate, g_inner[:, :local]], axis=1)
    g_dt = g_inner[:, local : local + heads]
    g_joint = jnp.concatenate(
        [g_inner[:, local + heads : local + heads + EXPERTS], g_inner[:, local + LANES :]], axis=1
    )
    joint_rows = height // 2
    g_joint = lax.dynamic_slice_in_dim(g_joint, core * joint_rows, joint_rows, 0) + swap(
        lax.dynamic_slice_in_dim(g_joint, (1 - core) * joint_rows, joint_rows, 0)
    )

    def widen(part, full):
        start = (0,) * (part.ndim - 1) + (core * part.shape[-1],)
        return lax.dynamic_update_slice(jnp.zeros(part.shape[:-1] + (full,), F32), part, start)

    conv_full = jnp.concatenate(
        [widen(par_grads[:5, :local], inner_all), par_grads[:5, local + LANES :]], axis=1
    )
    skip_loc = par_grads[5, :local].reshape(heads, P_SIZE).sum(axis=1)
    small = [
        grad_gain_in,
        grad_gain_mid,
        conv_full.reshape(-1),
        widen(head_grads[0, :heads], H),
        widen(head_grads[1, :heads], H),
        widen(skip_loc, H),
        widen(par_grads[6, :local], inner_all),
    ]
    flat = jnp.concatenate(small)
    count = -(-flat.shape[0] // 1024) * 1024
    flat = total_sum(jnp.pad(flat, (0, count - flat.shape[0])).reshape(-1, LANES)).reshape(-1)
    sums = []
    start = 0
    for item in small:
        sums.append(flat[start : start + item.shape[0]])
        start += item.shape[0]
    conv_sums = sums[2].reshape(5, -1)
    return (
        output, grad_tokens, sums[0], g_zx, g_dt, g_joint[:, EXPERTS:], conv_sums[:4],
        conv_sums[4], sums[3], sums[4], sums[5], sums[6], g_out, sums[1], g_joint[:, :EXPERTS],
        g_sgu, g_sdown, g_egu, g_edown,
    )


def solution(mesh):
    both = P(("dp", "tensor"), None)
    rows = P("dp", None, "tensor")
    cols = P("tensor", "dp")
    return jax.shard_map(
        shards,
        mesh=mesh,
        in_specs=(
            both, P("dp", None), P(), rows, P("dp", "tensor"), both, P(), P(), P(), P(), P(), P(),
            cols, P(), both, rows, cols, P(None, "dp", None, "tensor"), P(None, "tensor", "dp"),
            both,
        ),
        out_specs=(
            both, both, P(), rows, P("dp", "tensor"), both, P(), P(), P(), P(), P(), P(),
            cols, P(), both, rows, cols, P(None, "dp", None, "tensor"), P(None, "tensor", "dp"),
        ),
        check_vma=False,
    )
```

time: 6160 us -> 1390 us (0.23)
  waiting for transfers between devices: 2560 us -> 550 us
  local copies, waits for them, and re-layouts: 1970 us -> 160 us
  matrix products: 744 us -> 154 us
  other arithmetic: 684 us -> 137 us
  Pallas kernels: 0 us -> 269 us
  blocking collectives: 128 us -> 0 us
  starting transfers between devices: 1.95 us -> 98.7 us
    reduce_scatter x11 -> x0, waiting for transfers between devices: 1810 us -> none  [the longest x1 702 us: shards(): lax.psum_scatter(egu_grads, 'dp', scatter_dimension=1, tiled=True)]
    dynamic_update_slice x133 -> x6, local copies, waits for them, and re-layouts: 1280 us -> 8.04 us  [the longest x1 5.19 us: shards(): lax.dynamic_update_slice(grad_inner, grad_router, (0, local + heads))]
    dot_general x231 -> x12, matrix products: 723 us -> 154 us  [the longest x6 94.4 us: tn(): lax.dot_general(left, right, (((0,), (0,)), ((), ())), preferred_element_...]
    ppermute x0 -> x96, waiting for transfers between devices: none -> 550 us  [the longest x27 292 us: next_line(): lax.ppermute(values, 'dp', [(i, (i + GROUP) % count) for i in range(count)])]
    scatter-add x33 -> x0, other arithmetic: 370 us -> none  [the longest x16 177 us: expert_back(): return (d_mid_acc.at[row_ids].add(d_in), (grad_gu, grad_down, d_weight))]
    all_gather x10 -> x0, waiting for transfers between devices: 334 us -> none  [the longest x1 195 us: routed_weights(): lax.all_gather(expert_gu, 'dp', axis=1, tiled=True)]
    gather x46 -> x0, local copies, waits for them, and re-layouts: 315 us -> none  [the longest x16 105 us: expert_back(): cot_rows = back_rows[row_ids]]
    pallas_call x0 -> x10, Pallas kernels: none -> 269 us  [the longest x4 164 us: expert_rows(): pl.pallas_call(functools.partial(expert_body, hidden, units), grid=(rows...]
  transfers between devices with their start and end apart: 24 -> 96, of which waited for: 16 -> 39; matrix products, arithmetic and copies ran while one was open for 16% -> 32% of each run, Pallas kernels for 0% -> 20%
where the time goes in v1:
time: 1390 us; the launch traced here: 1380 us
  waiting for transfers between devices  550 us (40%)
  Pallas kernels  269 us (19%)
  local copies, waits for them, and re-layouts  160 us (12%)
  matrix products  154 us (11%)
  other arithmetic  137 us (10%)
  starting transfers between devices  98.7 us (7%)
    ppermute x27, waiting for transfers between devices, next_line(): lax.ppermute(values, 'dp', [(i, (i + GROUP) % count) for i in range(count)])  292 us
    ppermute x44, waiting for transfers between devices, hop(): return lax.ppermute(values, 'dp', [(i, i ^ bits) for i in range(count)])  257 us
    pallas_call x4, Pallas kernels, expert_rows(): pl.pallas_call(functools.partial(expert_body, hidden, units), grid=(rows...  164 us
    dot_general x6, matrix products, tn(): lax.dot_general(left, right, (((0,), (0,)), ((), ())), preferred_element_...  94.4 us
    unnamed x217, local copies, waits for them, and re-layouts  57.9 us
    pallas_call x1, Pallas kernels, back_scan(): pl.pallas_call(back_body, grid=(steps,), out_shape=(jax.ShapeDtypeStruct(...  56.2 us
    ppermute x25, starting transfers between devices, swap(): return lax.ppermute(values, 'tensor', [(0, 1), (1, 0)])  52.4 us
    ppermute x44, starting transfers between devices, hop(): return lax.ppermute(values, 'dp', [(i, i ^ bits) for i in range(count)])  39.3 us
  transfers between devices with their start and end apart: 96, of which 39 were waited for; matrix products, arithmetic and copies ran while one was open for 32% of the time, Pallas kernels for 20%

profile of v1, /device:TPU:1, one launch (start us, length us, event | category | flops | bytes accessed | tf_op | source)
XLA Modules:
  0.0 1379.9 jit_solution(15974746739190648314)
XLA Ops:
  118.9 21.3 %collective-permute-done.5.refs_2_ = bf16[4,96,1536]{2,1,0:T(8,128)(2,1)} collective-permute-done((bf16[4,96,1536]{2,1,0:T(8,128)(2,1)}, bf16[4,96,1536]{2,1,0:T(8,128)(2,1)}, u32[]{:S(2)}, u32[]{:S(2)}) %collective-permute-start.5) | collective-permute-done | bytes 1179680 | tf_op jit(solution)/shard_map/ppermute | solution.py:38
  142.3 23.1 %collective-permute-done.6.refs_3_ = bf16[4,96,1536]{2,1,0:T(8,128)(2,1)} collective-permute-done((bf16[4,96,1536]{2,1,0:T(8,128)(2,1)}, bf16[4,96,1536]{2,1,0:T(8,128)(2,1)}, u32[]{:S(2)}, u32[]{:S(2)}) %collective-permute-start.6) | collective-permute-done | bytes 1179680 | tf_op jit(solution)/shard_map/ppermute | solution.py:38
  171.9 11.1 fusion.89.gate_ref
  184.3 19.1 %collective-permute-done.13.refs_3_ = bf16[4,96,1920]{2,1,0:T(8,128)(2,1)} collective-permute-done((bf16[4,96,1920]{2,1,0:T(8,128)(2,1)}, bf16[4,96,1920]{2,1,0:T(8,128)(2,1)}, u32[]{:S(2)}, u32[]{:S(2)}) %collective-permute-start.13) | collective-permute-done | bytes 1474592 | tf_op jit(solution)/shard_map/ppermute | solution.py:38
  210.7 14.0 %fusion.87.zi_ref.prev_ref = f32[1024,1920]{1,0:T(8,128)} fusion(bf16[1536,1920]{1,0:T(8,128)(2,1)} %assemble.5, f32[1536]{0:T(1024)S(1)} %copy-done.61, f32[1024]{0:T(1024)S(1)} %add_rsqrt_fusion.1, bf16[512,1536]{1,0:T(8,128)(2,1)S(1)} %copy-done.4, bf16[512,1536]{1,0:T(8,128)(2,1)} %collective-permute-done, pred[]{:T(512)S(6)} %eq.44), kind=kOutput, calls=%fused_computation.314 | convolution fusion | flops 6060244992 | bytes 16918528 | tf_op jit(solution)/shard_map/dot_general | solution.py:25
  224.9 32.2 %collective-permute-done.18.refs_1_ = bf16[4,96,1536]{2,1,0:T(8,128)(2,1)} collective-permute-done((bf16[4,96,1536]{2,1,0:T(8,128)(2,1)}, bf16[4,96,1536]{2,1,0:T(8,128)(2,1)}, u32[]{:S(2)}, u32[]{:S(2)}) %collective-permute-start.18) | collective-permute-done | bytes 1179680 | tf_op jit(solution)/shard_map/ppermute | solution.py:38
  257.3 24.0 %front_scan.1 = (f32[1024,1536]{1,0:T(8,128)}, f32[1024,128]{1,0:T(8,128)}, f32[8,128,1536]{2,1,0:T(8,128)}) custom-call(f32[1024,1536]{1,0:T(8,128)} %fusion.89.gate_ref, f32[1024,1920]{1,0:T(8,128)} %fusion.87.zi_ref.prev_ref, f32[8,1920]{1,0:T(8,128)} %fusion.68.kern_ref, f32[8,128]{1,0:T(8,128)} %select_maximum_fusion.4.head_ref, ...), custom_call_target="tpu_custom_call" | custom-call | flops 40000000000 | bytes 30000000 | tf_op jit(solution)/shard_map/front_scan/pallas_call | solution.py:260
  330.4 23.0 %collective-permute-done.27.refs_1_ = bf16[4,96,3456]{2,1,0:T(8,128)(2,1)} collective-permute-done((bf16[4,96,3456]{2,1,0:T(8,128)(2,1)}, bf16[4,96,3456]{2,1,0:T(8,128)(2,1)}, u32[]{:S(2)}, u32[]{:S(2)}) %collective-permute-start.27) | collective-permute-done | bytes 2654240 | tf_op jit(solution)/shard_map/ppermute | solution.py:43
  367.1 46.0 %collective-permute-done.28.refs_2_ = bf16[4,96,3456]{2,1,0:T(8,128)(2,1)S(1)} collective-permute-done((bf16[4,96,3456]{2,1,0:T(8,128)(2,1)}, bf16[4,96,3456]{2,1,0:T(8,128)(2,1)S(1)}, u32[]{:S(2)}, u32[]{:S(2)}) %collective-permute-start.28) | collective-permute-done | bytes 2654240 | tf_op jit(solution)/shard_map/ppermute | solution.py:43
  433.5 38.4 %collective-permute-done.29.refs_3_ = bf16[4,96,3456]{2,1,0:T(8,128)(2,1)} collective-permute-done((bf16[4,96,3456]{2,1,0:T(8,128)(2,1)S(1)}, bf16[4,96,3456]{2,1,0:T(8,128)(2,1)}, u32[]{:S(2)}, u32[]{:S(2)}) %collective-permute-start.29) | collective-permute-done | bytes 2654240 | tf_op jit(solution)/shard_map/ppermute | solution.py:43
  491.5 41.2 %expert_rows.4 = (bf16[1024,3456]{1,0:T(8,128)(2,1)}, bf16[1024,1536]{1,0:T(8,128)(2,1)}, bf16[1024,1536]{1,0:T(8,128)(2,1)}, bf16[1024,128]{1,0:T(8,128)(2,1)}) custom-call(bf16[1024,1536]{1,0:T(8,128)(2,1)} %pad_maximum_fusion.3.x_ref, bf16[1024,1664]{1,0:T(8,128)(2,1)} %fusion.20.ym_ref, bf16[1536,128]{1,0:T(8,128)(2,1)} %pad.33.router_ref, ...), custom_call_target="tpu_custom_call" | custom-call | flops 21743271936 | bytes 30000000 | tf_op jit(solution)/shard_map/expert_rows/pallas_call | solution.py:541
  551.6 40.7 %expert_rows.7 = (bf16[1024,3456]{1,0:T(8,128)(2,1)}, bf16[1024,1536]{1,0:T(8,128)(2,1)}, bf16[1024,1536]{1,0:T(8,128)(2,1)}, bf16[1024,128]{1,0:T(8,128)(2,1)}) custom-call(bf16[1024,1536]{1,0:T(8,128)(2,1)} %pad_maximum_fusion.6.x_ref, bf16[1024,1664]{1,0:T(8,128)(2,1)} %fusion.23.ym_ref, bf16[1536,128]{1,0:T(8,128)(2,1)} %pad.33.router_ref, ...), custom_call_target="tpu_custom_call" | custom-call | flops 21743271936 | bytes 30000000 | tf_op jit(solution)/shard_map/expert_rows/pallas_call | solution.py:541
  600.1 41.0 %expert_rows.5 = (bf16[1024,3456]{1,0:T(8,128)(2,1)}, bf16[1024,1536]{1,0:T(8,128)(2,1)}, bf16[1024,1536]{1,0:T(8,128)(2,1)}, bf16[1024,128]{1,0:T(8,128)(2,1)}) custom-call(bf16[1024,1536]{1,0:T(8,128)(2,1)} %pad_maximum_fusion.4.x_ref, bf16[1024,1664]{1,0:T(8,128)(2,1)} %fusion.21.ym_ref, bf16[1536,128]{1,0:T(8,128)(2,1)} %pad.33.router_ref, ...), custom_call_target="tpu_custom_call" | custom-call | flops 21743271936 | bytes 30000000 | tf_op jit(solution)/shard_map/expert_rows/pallas_call | solution.py:541
  667.4 40.7 %expert_rows.6 = (bf16[1024,3456]{1,0:T(8,128)(2,1)}, bf16[1024,1536]{1,0:T(8,128)(2,1)}, bf16[1024,1536]{1,0:T(8,128)(2,1)}, bf16[1024,128]{1,0:T(8,128)(2,1)}) custom-call(bf16[1024,1536]{1,0:T(8,128)(2,1)} %pad_maximum_fusion.5.x_ref, bf16[1024,1664]{1,0:T(8,128)(2,1)} %fusion.22.ym_ref, bf16[1536,128]{1,0:T(8,128)(2,1)} %pad.33.router_ref, ...), custom_call_target="tpu_custom_call" | custom-call | flops 21743271936 | bytes 30000000 | tf_op jit(solution)/shard_map/expert_rows/pallas_call | solution.py:541
  714.7 22.5 %fusion.2 = bf16[1536,1152]{1,0:T(8,128)(2,1)} fusion(bf16[1024,1536]{1,0:T(8,128)(2,1)} %copy-done.16, bf16[1024,1536]{1,0:T(8,128)(2,1)S(1)} %copy-done.14, bf16[1024,1536]{1,0:T(8,128)(2,1)} %copy-done.15, bf16[1024,1536]{1,0:T(8,128)(2,1)S(1)} %copy-done.12, bf16[4096,3456]{1,0:T(8,128)(2,1)} %constant_dynamic-update-slice_fusion.17), kind=kOutput, calls=%fused_computation.2 | convolution fusion | flops 14545846272 | bytes 25559040 | tf_op jit(solution)/shard_map/dot_general | solution.py:33
  739.9 38.9 %fusion = bf16[1536,2304]{1,0:T(8,128)(2,1)} fusion(bf16[4096,1536]{1,0:T(8,128)(2,1)} %constant_dynamic-update-slice_fusion.8, bf16[4096,3456]{1,0:T(8,128)(2,1)} %constant_dynamic-update-slice_fusion.17), kind=kOutput, calls=%fused_computation | convolution fusion | flops 28991029248 | bytes 38535168 | tf_op jit(solution)/shard_map/dot_general | solution.py:33
  802.8 17.9 %collective-permute-done.90 = bf16[4,96,1152]{2,1,0:T(8,128)(2,1)S(1)} collective-permute-done((bf16[4,96,1152]{2,1,0:T(8,128)(2,1)S(1)}, bf16[4,96,1152]{2,1,0:T(8,128)(2,1)S(1)}, u32[]{:S(2)}, u32[]{:S(2)}) %collective-permute-start.90) | collective-permute-done | bytes 884768 | tf_op jit(solution)/shard_map/ppermute | solution.py:43
  823.4 56.8 %collective-permute-done.91 = bf16[4,96,1152]{2,1,0:T(8,128)(2,1)S(1)} collective-permute-done((bf16[4,96,1152]{2,1,0:T(8,128)(2,1)S(1)}, bf16[4,96,1152]{2,1,0:T(8,128)(2,1)S(1)}, u32[]{:S(2)}, u32[]{:S(2)}) %collective-permute-start.91) | collective-permute-done | bytes 884768 | tf_op jit(solution)/shard_map/ppermute | solution.py:43
  882.5 14.5 %collective-permute-done.58 = bf16[256,1536]{1,0:T(8,128)(2,1)S(1)} collective-permute-done((bf16[256,1536]{1,0:T(8,128)(2,1)S(1)}, bf16[256,1536]{1,0:T(8,128)(2,1)S(1)}, u32[]{:S(2)}, u32[]{:S(2)}) %collective-permute-start.58) | collective-permute-done | bytes 786464 | tf_op jit(solution)/shard_map/ppermute | solution.py:38
  897.5 15.4 %collective-permute-done.50 = bf16[256,1536]{1,0:T(8,128)(2,1)S(1)} collective-permute-done((bf16[256,1536]{1,0:T(8,128)(2,1)S(1)}, bf16[256,1536]{1,0:T(8,128)(2,1)S(1)}, u32[]{:S(2)}, u32[]{:S(2)}) %collective-permute-start.50) | collective-permute-done | bytes 786464 | tf_op jit(solution)/shard_map/ppermute | solution.py:38
  915.3 16.5 %collective-permute-done.92 = bf16[4,96,1152]{2,1,0:T(8,128)(2,1)S(1)} collective-permute-done((bf16[4,96,1152]{2,1,0:T(8,128)(2,1)S(1)}, bf16[4,96,1152]{2,1,0:T(8,128)(2,1)S(1)}, u32[]{:S(2)}, u32[]{:S(2)}) %collective-permute-start.92) | collective-permute-done | bytes 884768 | tf_op jit(solution)/shard_map/ppermute | solution.py:43
  959.1 10.6 collective-permute-done.85
  971.8 13.7 collective-permute-done.56
  989.1 30.0 %collective-permute-done.46 = bf16[512,1536]{1,0:T(8,128)(2,1)S(1)} collective-permute-done((bf16[512,1536]{1,0:T(8,128)(2,1)S(1)}, bf16[512,1536]{1,0:T(8,128)(2,1)S(1)}, u32[]{:S(2)}, u32[]{:S(2)}) %collective-permute-start.46) | collective-permute-done | bytes 1572896 | tf_op jit(solution)/shard_map/ppermute | solution.py:38
  1041.8 12.2 fusion.57.dsc_ref
  1054.0 56.2 %back_scan.1 = (bf16[1024,1536]{1,0:T(8,128)(2,1)}, bf16[1024,1920]{1,0:T(8,128)(2,1)}, f32[8,1920]{1,0:T(8,128)}, f32[8,128]{1,0:T(8,128)}) custom-call(f32[1024,1536]{1,0:T(8,128)} %fusion.57.dsc_ref, f32[1024,1536]{1,0:T(8,128)} %get-tuple-element.43.y_ref, f32[1024,1536]{1,0:T(8,128)} %fusion.89.gate_ref, f32[1024,1920]{1,0:T(8,128)} %fusion.87.zi_ref.prev_ref, ...), custom_call_target="tpu_custom_call" | custom-call | flops 80000000000 | bytes 60000000 | tf_op jit(solution)/shard_map/back_scan/pallas_call | solution.py:437
  1156.8 10.7 fusion.83
  1227.2 24.0 %collective-permute-done.73 = bf16[4,2,96,1920]{3,2,1,0:T(8,128)(2,1)} collective-permute-done((bf16[4,2,96,1920]{3,2,1,0:T(8,128)(2,1)}, bf16[4,2,96,1920]{3,2,1,0:T(8,128)(2,1)}, u32[]{:S(2)}, u32[]{:S(2)}) %collective-permute-start.73) | collective-permute-done | bytes 2949152 | tf_op jit(solution)/shard_map/ppermute | solution.py:38
  1257.6 20.9 %collective-permute-done.64 = f32[184,128]{1,0:T(8,128)S(1)} collective-permute-done((f32[184,128]{1,0:T(8,128)S(1)}, f32[184,128]{1,0:T(8,128)S(1)}, u32[]{:S(2)}, u32[]{:S(2)}) %collective-permute-start.64) | collective-permute-done | bytes 94240 | tf_op jit(solution)/shard_map/ppermute | solution.py:38
  1332.1 10.6 collective-permute-done.76
  1342.9 13.3 collective-permute-done.77
  1356.5 19.0 %collective-permute-start.78 = (f32[48,272]{1,0:T(8,128)S(1)}, f32[48,272]{1,0:T(8,128)S(1)}, u32[]{:S(2)}, u32[]{:S(2)}) collective-permute-start(f32[48,272]{1,0:T(8,128)S(1)} %fusion.65), channel_id=1, source_target_pairs={{0,1},{1,0},{2,3},{3,2},{4,5},{5,4},{6,7},{7,6},{8,9},{9,8},{10,11... | collective-permute-start | bytes 156680 | tf_op jit(solution)/shard_map/ppermute | solution.py:47
  (630 shorter events, 549.6 us)
Async XLA Ops:
  3.1 82.8 %collective-permute-start.15 = (bf16[96,1536]{1,0:T(8,128)(2,1)}, bf16[96,1536]{1,0:T(8,128)(2,1)}, u32[]{:S(2)}, u32[]{:S(2)}) collective-permute-start(bf16[96,1536]{1,0:T(8,128)(2,1)} %bitcast.319), channel_id=1, source_target_pairs={{0,8},{2,10},{4,12},{6,14},{8,16},{10,18},{12,20},{14,22},{16,24},... | collective-permute-start | bytes 884744 | tf_op jit(solution)/shard_map/ppermute | solution.py:43
  10.3 97.3 %collective-permute-start = (bf16[512,1536]{1,0:T(8,128)(2,1)S(1)}, bf16[512,1536]{1,0:T(8,128)(2,1)}, u32[]{:S(2)}, u32[]{:S(2)}) collective-permute-start(bf16[512,1536]{1,0:T(8,128)(2,1)S(1)} %copy-done.4), channel_id=1, source_target_pairs={{0,1},{1,0},{2,3},{3,2},{4,5},{5,4},{6,7},{7,6},{8,9},{9,8},{10,11... | collective-permute-start | bytes 4718600 | tf_op jit(solution)/shard_map/ppermute | solution.py:47
  99.9 65.5 %collective-permute-start.6 = (bf16[4,96,1536]{2,1,0:T(8,128)(2,1)}, bf16[4,96,1536]{2,1,0:T(8,128)(2,1)}, u32[]{:S(2)}, u32[]{:S(2)}) collective-permute-start(bf16[4,96,1536]{2,1,0:T(8,128)(2,1)} %collective-permute-done.4.refs_1_), channel_id=1, source_target_pairs={{0,4},{2,6},{4,0},{6,2},{8,12},{10,14},{12,8},{14,10},{16,20},{18,... | collective-permute-start | bytes 3538952 | tf_op jit(solution)/shard_map/ppermute | solution.py:38
  104.1 186.5 %collective-permute-start.33 = (bf16[512,1664]{1,0:T(8,128)(2,1)}, bf16[512,1664]{1,0:T(8,128)(2,1)}, u32[]{:S(2)}, u32[]{:S(2)}) collective-permute-start(bf16[512,1664]{1,0:T(8,128)(2,1)} %pad_maximum_fusion.10), channel_id=1, source_target_pairs={{0,2},{2,0},{4,6},{6,4},{8,10},{10,8},{12,14},{14,12},{16,18},{18,... | collective-permute-start | bytes 5111816 | tf_op jit(solution)/shard_map/ppermute | solution.py:38
  107.6 75.5 %collective-permute-start.11 = (bf16[4,96,1920]{2,1,0:T(8,128)(2,1)}, bf16[4,96,1920]{2,1,0:T(8,128)(2,1)}, u32[]{:S(2)}, u32[]{:S(2)}) collective-permute-start(bf16[4,96,1920]{2,1,0:T(8,128)(2,1)} %pad_maximum_fusion.20.refs_0_), channel_id=1, source_target_pairs={{0,2},{2,0},{4,6},{6,4},{8,10},{10,8},{12,14},{14,12},{16,18},{18,... | collective-permute-start | bytes 4423688 | tf_op jit(solution)/shard_map/ppermute | solution.py:38
  114.9 88.5 %collective-permute-start.13 = (bf16[4,96,1920]{2,1,0:T(8,128)(2,1)}, bf16[4,96,1920]{2,1,0:T(8,128)(2,1)}, u32[]{:S(2)}, u32[]{:S(2)}) collective-permute-start(bf16[4,96,1920]{2,1,0:T(8,128)(2,1)} %collective-permute-done.12.refs_2_), channel_id=1, source_target_pairs={{0,2},{2,0},{4,6},{6,4},{8,10},{10,8},{12,14},{14,12},{16,18},{18,... | collective-permute-start | bytes 4423688 | tf_op jit(solution)/shard_map/ppermute | solution.py:38
  140.2 84.5 %collective-permute-start.26 = (bf16[96,3456]{1,0:T(8,128)(2,1)}, bf16[96,3456]{1,0:T(8,128)(2,1)}, u32[]{:S(2)}, u32[]{:S(2)}) collective-permute-start(bf16[96,3456]{1,0:T(8,128)(2,1)} %get-tuple-element.194), channel_id=1, source_target_pairs={{0,6},{2,4},{4,2},{6,0},{8,14},{10,12},{12,10},{14,8},{16,22},{18,... | collective-permute-start | bytes 1990664 | tf_op jit(solution)/shard_map/ppermute | solution.py:38
  165.4 115.9 %collective-permute-start.25 = (bf16[96,3456]{1,0:T(8,128)(2,1)}, bf16[96,3456]{1,0:T(8,128)(2,1)}, u32[]{:S(2)}, u32[]{:S(2)}) collective-permute-start(bf16[96,3456]{1,0:T(8,128)(2,1)} %get-tuple-element.195), channel_id=1, source_target_pairs={{0,4},{2,6},{4,0},{6,2},{8,12},{10,14},{12,8},{14,10},{16,20},{18,... | collective-permute-start | bytes 1990664 | tf_op jit(solution)/shard_map/ppermute | solution.py:38
  183.1 99.6 %collective-permute-start.24 = (bf16[96,3456]{1,0:T(8,128)(2,1)}, bf16[96,3456]{1,0:T(8,128)(2,1)}, u32[]{:S(2)}, u32[]{:S(2)}) collective-permute-start(bf16[96,3456]{1,0:T(8,128)(2,1)} %get-tuple-element.196), channel_id=1, source_target_pairs={{0,2},{2,0},{4,6},{6,4},{8,10},{10,8},{12,14},{14,12},{16,18},{18,... | collective-permute-start | bytes 1990664 | tf_op jit(solution)/shard_map/ppermute | solution.py:38
  224.7 68.0 %collective-permute-start.19 = (bf16[4,96,1536]{2,1,0:T(8,128)(2,1)}, bf16[4,96,1536]{2,1,0:T(8,128)(2,1)}, u32[]{:S(2)}, u32[]{:S(2)}) collective-permute-start(bf16[4,96,1536]{2,1,0:T(8,128)(2,1)} %pad_maximum_fusion.22.refs_0_), channel_id=1, source_target_pairs={{0,4},{2,6},{4,0},{6,2},{8,12},{10,14},{12,8},{14,10},{16,20},{18,... | collective-permute-start | bytes 3538952 | tf_op jit(solution)/shard_map/ppermute | solution.py:38
  292.7 63.2 %collective-permute-start.40 = (bf16[256,1664]{1,0:T(8,128)(2,1)}, bf16[256,1664]{1,0:T(8,128)(2,1)}, u32[]{:S(2)}, u32[]{:S(2)}) collective-permute-start(bf16[256,1664]{1,0:T(8,128)(2,1)} %slice.393), channel_id=1, source_target_pairs={{0,4},{2,6},{4,0},{6,2},{8,12},{10,14},{12,8},{14,10},{16,20},{18,... | collective-permute-start | bytes 2555912 | tf_op jit(solution)/shard_map/ppermute | solution.py:38
  315.3 97.9 %collective-permute-start.21 = (f32[512,1536]{1,0:T(8,128)}, f32[512,1536]{1,0:T(8,128)}, u32[]{:S(2)}, u32[]{:S(2)}) collective-permute-start(f32[512,1536]{1,0:T(8,128)} %constant_dynamic-slice_fusion.15), channel_id=1, source_target_pairs={{0,1},{1,0},{2,3},{3,2},{4,5},{5,4},{6,7},{7,6},{8,9},{9,8},{10,11... | collective-permute-start | bytes 9437192 | tf_op jit(solution)/shard_map/ppermute | solution.py:47
  364.0 66.3 %collective-permute-start.43 = (bf16[512,1664]{1,0:T(8,128)(2,1)S(1)}, bf16[512,1664]{1,0:T(8,128)(2,1)S(1)}, u32[]{:S(2)}, u32[]{:S(2)}) collective-permute-start(bf16[512,1664]{1,0:T(8,128)(2,1)S(1)} %pad_maximum_fusion.11), channel_id=1, source_target_pairs={{0,1},{1,0},{2,3},{3,2},{4,5},{5,4},{6,7},{7,6},{8,9},{9,8},{10,11... | collective-permute-start | bytes 5111816 | tf_op jit(solution)/shard_map/ppermute | solution.py:47
  419.7 63.1 %collective-permute-start.31 = (bf16[512,1536]{1,0:T(8,128)(2,1)}, bf16[512,1536]{1,0:T(8,128)(2,1)S(1)}, u32[]{:S(2)}, u32[]{:S(2)}) collective-permute-start(bf16[512,1536]{1,0:T(8,128)(2,1)} %get-tuple-element.174), channel_id=1, source_target_pairs={{0,2},{2,0},{4,6},{6,4},{8,10},{10,8},{12,14},{14,12},{16,18},{18,... | collective-permute-start | bytes 4718600 | tf_op jit(solution)/shard_map/ppermute | solution.py:38
  420.9 66.8 %collective-permute-start.22 = (bf16[512,1536]{1,0:T(8,128)(2,1)}, bf16[512,1536]{1,0:T(8,128)(2,1)}, u32[]{:S(2)}, u32[]{:S(2)}) collective-permute-start(bf16[512,1536]{1,0:T(8,128)(2,1)} %get-tuple-element.174), channel_id=1, source_target_pairs={{0,1},{1,0},{2,3},{3,2},{4,5},{5,4},{6,7},{7,6},{8,9},{9,8},{10,11... | collective-permute-start | bytes 4718600 | tf_op jit(solution)/shard_map/ppermute | solution.py:47
  481.6 63.8 %collective-permute-start.38 = (bf16[256,1536]{1,0:T(8,128)(2,1)}, bf16[256,1536]{1,0:T(8,128)(2,1)S(1)}, u32[]{:S(2)}, u32[]{:S(2)}) collective-permute-start(bf16[256,1536]{1,0:T(8,128)(2,1)} %slice.392), channel_id=1, source_target_pairs={{0,2},{2,0},{4,6},{6,4},{8,10},{10,8},{12,14},{14,12},{16,18},{18,... | collective-permute-start | bytes 2359304 | tf_op jit(solution)/shard_map/ppermute | solution.py:38
  484.0 64.3 %collective-permute-start.47 = (bf16[512,1536]{1,0:T(8,128)(2,1)S(1)}, bf16[512,1536]{1,0:T(8,128)(2,1)}, u32[]{:S(2)}, u32[]{:S(2)}) collective-permute-start(bf16[512,1536]{1,0:T(8,128)(2,1)S(1)} %collective-permute-done.37), channel_id=1, source_target_pairs={{0,1},{1,0},{2,3},{3,2},{4,5},{5,4},{6,7},{7,6},{8,9},{9,8},{10,11... | collective-permute-start | bytes 4718600 | tf_op jit(solution)/shard_map/ppermute | solution.py:47
  536.8 421.0 %collective-permute-start.52 = (bf16[512,1536]{1,0:T(8,128)(2,1)}, bf16[512,1536]{1,0:T(8,128)(2,1)}, u32[]{:S(2)}, u32[]{:S(2)}) collective-permute-start(bf16[512,1536]{1,0:T(8,128)(2,1)} %slice.332), channel_id=1, source_target_pairs={{0,1},{1,0},{2,3},{3,2},{4,5},{5,4},{6,7},{7,6},{8,9},{9,8},{10,11... | collective-permute-start | bytes 4718600 | tf_op jit(solution)/shard_map/ppermute | solution.py:47
  536.8 452.3 %collective-permute-start.30 = (bf16[512,1536]{1,0:T(8,128)(2,1)}, bf16[512,1536]{1,0:T(8,128)(2,1)}, u32[]{:S(2)}, u32[]{:S(2)}) collective-permute-start(bf16[512,1536]{1,0:T(8,128)(2,1)} %slice.308), channel_id=1, source_target_pairs={{0,1},{1,0},{2,3},{3,2},{4,5},{5,4},{6,7},{7,6},{8,9},{9,8},{10,11... | collective-permute-start | bytes 4718600 | tf_op jit(solution)/shard_map/ppermute | solution.py:47
  547.8 116.1 %collective-permute-start.39 = (bf16[512,1536]{1,0:T(8,128)(2,1)}, bf16[512,1536]{1,0:T(8,128)(2,1)}, u32[]{:S(2)}, u32[]{:S(2)}) collective-permute-start(bf16[512,1536]{1,0:T(8,128)(2,1)} %pad_maximum_fusion.15), channel_id=1, source_target_pairs={{0,1},{1,0},{2,3},{3,2},{4,5},{5,4},{6,7},{7,6},{8,9},{9,8},{10,11... | collective-permute-start | bytes 4718600 | tf_op jit(solution)/shard_map/ppermute | solution.py:47
  596.4 196.9 %collective-permute-start.57 = (bf16[512,1536]{1,0:T(8,128)(2,1)}, bf16[512,1536]{1,0:T(8,128)(2,1)}, u32[]{:S(2)}, u32[]{:S(2)}) collective-permute-start(bf16[512,1536]{1,0:T(8,128)(2,1)} %slice.341), channel_id=1, source_target_pairs={{0,1},{1,0},{2,3},{3,2},{4,5},{5,4},{6,7},{7,6},{8,9},{9,8},{10,11... | collective-permute-start | bytes 4718600 | tf_op jit(solution)/shard_map/ppermute | solution.py:47
  596.4 199.6 %collective-permute-start.49 = (bf16[512,1536]{1,0:T(8,128)(2,1)}, bf16[512,1536]{1,0:T(8,128)(2,1)}, u32[]{:S(2)}, u32[]{:S(2)}) collective-permute-start(bf16[512,1536]{1,0:T(8,128)(2,1)} %slice.327), channel_id=1, source_target_pairs={{0,1},{1,0},{2,3},{3,2},{4,5},{5,4},{6,7},{7,6},{8,9},{9,8},{10,11... | collective-permute-start | bytes 4718600 | tf_op jit(solution)/shard_map/ppermute | solution.py:47
  663.9 134.3 %collective-permute-start.53 = (bf16[512,1536]{1,0:T(8,128)(2,1)}, bf16[512,1536]{1,0:T(8,128)(2,1)}, u32[]{:S(2)}, u32[]{:S(2)}) collective-permute-start(bf16[512,1536]{1,0:T(8,128)(2,1)} %slice.334), channel_id=1, source_target_pairs={{0,1},{1,0},{2,3},{3,2},{4,5},{5,4},{6,7},{7,6},{8,9},{9,8},{10,11... | collective-permute-start | bytes 4718600 | tf_op jit(solution)/shard_map/ppermute | solution.py:47
  821.6 91.7 %collective-permute-start.55 = (bf16[256,1536]{1,0:T(8,128)(2,1)S(1)}, bf16[256,1536]{1,0:T(8,128)(2,1)S(1)}, u32[]{:S(2)}, u32[]{:S(2)}) collective-permute-start(bf16[256,1536]{1,0:T(8,128)(2,1)S(1)} %get-tuple-element.204), channel_id=1, source_target_pairs={{0,4},{2,6},{4,0},{6,2},{8,12},{10,14},{12,8},{14,10},{16,20},{18,... | collective-permute-start | bytes 2359304 | tf_op jit(solution)/shard_map/ppermute | solution.py:38
  971.7 63.0 %collective-permute-start.86 = (bf16[4,96,2304]{2,1,0:T(8,128)(2,1)}, bf16[4,96,2304]{2,1,0:T(8,128)(2,1)}, u32[]{:S(2)}, u32[]{:S(2)}) collective-permute-start(bf16[4,96,2304]{2,1,0:T(8,128)(2,1)} %fusion.18), channel_id=1, source_target_pairs={{0,8},{2,10},{4,12},{6,14},{8,16},{10,18},{12,20},{14,22},{16,24},... | collective-permute-start | bytes 5308424 | tf_op jit(solution)/shard_map/ppermute | solution.py:43
  1038.2 143.5 %collective-permute-start.87 = (bf16[96,2304]{1,0:T(8,128)(2,1)}, bf16[96,2304]{1,0:T(8,128)(2,1)}, u32[]{:S(2)}, u32[]{:S(2)}) collective-permute-start(bf16[96,2304]{1,0:T(8,128)(2,1)} %get-tuple-element.201), channel_id=1, source_target_pairs={{0,2},{2,0},{4,6},{6,4},{8,10},{10,8},{12,14},{14,12},{16,18},{18,... | collective-permute-start | bytes 1327112 | tf_op jit(solution)/shard_map/ppermute | solution.py:38
  1038.5 144.8 %collective-permute-start.89 = (bf16[96,2304]{1,0:T(8,128)(2,1)}, bf16[96,2304]{1,0:T(8,128)(2,1)}, u32[]{:S(2)}, u32[]{:S(2)}) collective-permute-start(bf16[96,2304]{1,0:T(8,128)(2,1)} %get-tuple-element.202), channel_id=1, source_target_pairs={{0,6},{2,4},{4,2},{6,0},{8,14},{10,12},{12,10},{14,8},{16,22},{18,... | collective-permute-start | bytes 1327112 | tf_op jit(solution)/shard_map/ppermute | solution.py:38
  1040.7 145.8 %collective-permute-start.88 = (bf16[96,2304]{1,0:T(8,128)(2,1)}, bf16[96,2304]{1,0:T(8,128)(2,1)}, u32[]{:S(2)}, u32[]{:S(2)}) collective-permute-start(bf16[96,2304]{1,0:T(8,128)(2,1)} %get-tuple-element.203), channel_id=1, source_target_pairs={{0,4},{2,6},{4,0},{6,2},{8,12},{10,14},{12,8},{14,10},{16,20},{18,... | collective-permute-start | bytes 1327112 | tf_op jit(solution)/shard_map/ppermute | solution.py:38
  1136.1 73.7 %collective-permute-start.79 = (bf16[4,2,96,1536]{3,2,0,1:T(8,128)(2,1)}, bf16[4,2,96,1536]{3,2,0,1:T(8,128)(2,1)}, u32[]{:S(2)}, u32[]{:S(2)}) collective-permute-start(bf16[4,2,96,1536]{3,2,0,1:T(8,128)(2,1)} %bitcast.263), channel_id=1, source_target_pairs={{0,2},{2,0},{4,6},{6,4},{8,10},{10,8},{12,14},{14,12},{16,18},{18,... | collective-permute-start | bytes 7077896 | tf_op jit(solution)/shard_map/ppermute | solution.py:38
  1181.7 69.5 %collective-permute-start.73 = (bf16[4,2,96,1920]{3,2,1,0:T(8,128)(2,1)}, bf16[4,2,96,1920]{3,2,1,0:T(8,128)(2,1)}, u32[]{:S(2)}, u32[]{:S(2)}) collective-permute-start(bf16[4,2,96,1920]{3,2,1,0:T(8,128)(2,1)} %dynamic-slice_bitcast_fusion), channel_id=1, source_target_pairs={{0,2},{2,0},{4,6},{6,4},{8,10},{10,8},{12,14},{14,12},{16,18},{18,... | collective-permute-start | bytes 8847368 | tf_op jit(solution)/shard_map/ppermute | solution.py:38
  1212.5 82.7 %collective-permute-start.80 = (bf16[4,96,1536]{2,1,0:T(8,128)(2,1)S(1)}, bf16[4,96,1536]{2,1,0:T(8,128)(2,1)}, u32[]{:S(2)}, u32[]{:S(2)}) collective-permute-start(bf16[4,96,1536]{2,1,0:T(8,128)(2,1)S(1)} %fusion.43), channel_id=1, source_target_pairs={{0,4},{2,6},{4,0},{6,2},{8,12},{10,14},{12,8},{14,10},{16,20},{18,... | collective-permute-start | bytes 3538952 | tf_op jit(solution)/shard_map/ppermute | solution.py:38
  1221.1 76.1 %collective-permute-start.69 = (bf16[4,96,1536]{2,1,0:T(8,128)(2,1)}, bf16[4,96,1536]{2,1,0:T(8,128)(2,1)}, u32[]{:S(2)}, u32[]{:S(2)}) collective-permute-start(bf16[4,96,1536]{2,1,0:T(8,128)(2,1)} %fusion.42), channel_id=1, source_target_pairs={{0,2},{2,0},{4,6},{6,4},{8,10},{10,8},{12,14},{14,12},{16,18},{18,... | collective-permute-start | bytes 3538952 | tf_op jit(solution)/shard_map/ppermute | solution.py:38
  (159 other events, 3564.5 us)

commit v2 on v1

v2 whole, which is shorter than its diff:
```python
import functools

import jax
import jax.numpy as jnp
from jax import lax
from jax.experimental import pallas as pl
from jax.experimental.pallas import tpu as pltpu
from jax.sharding import PartitionSpec as P

F32 = jnp.float32
BF = jnp.bfloat16
EPS = 1e-05
H = 48
P_SIZE = 64
NS = 128
EXPERTS = 16
BL = 128
GROUP = 4
LANES = 128
VMEM = 60 * 1024 * 1024
SMALL = pl.CostEstimate(flops=1000, bytes_accessed=1000, transcendentals=0)
highest = lax.Precision.HIGHEST


def nn(left, right):
    return lax.dot_general(left, right, (((1,), (0,)), ((), ())), preferred_element_type=F32)


def nt(left, right):
    return lax.dot_general(left, right, (((1,), (1,)), ((), ())), preferred_element_type=F32)


def tn(left, right, kind=F32):
    return lax.dot_general(left, right, (((0,), (0,)), ((), ())), preferred_element_type=kind)


def hop(values, bits):
    count = lax.axis_size("dp")
    return lax.ppermute(values, "dp", [(i, i ^ bits) for i in range(count)])


def next_line(values):
    count = lax.axis_size("dp")
    return lax.ppermute(values, "dp", [(i, (i + GROUP) % count) for i in range(count)])


def swap(values):
    return lax.ppermute(values, "tensor", [(0, 1), (1, 0)])


def pick(values, index, axis=0):
    return lax.dynamic_index_in_dim(values, index, axis, keepdims=False)


def in_order(mine, theirs, core):
    return jnp.where(
        core == 0, jnp.concatenate([mine, theirs]), jnp.concatenate([theirs, mine])
    )


def tie(values, *others):
    flat, tree = jax.tree.flatten(values)
    held = lax.optimization_barrier((flat, others))
    return jax.tree.unflatten(tree, held[0])


class Order:
    def __init__(self):
        self.marks = self.last = ()

    def __call__(self, values):
        return tie(values, *self.marks)

    def set(self, *marks):
        self.marks, self.last = marks + self.last, marks

    def take(self, *values):
        values = self(values)
        self.set(*values)
        return values if len(values) > 1 else values[0]


def ring_on(blocks, order, low, high, lines):
    for _ in range(low, min(high, lines)):
        blocks.append(order(next_line(blocks[-1])))


def pieces_of(parts, targets, cut):
    inner, height, width = parts[0].shape
    starts = [0] * len(parts)
    if cut:
        starts[-1] = cut
    if height % 32 == 0:
        return parts, starts, targets
    if cut:
        parts = parts[:3] + [jnp.concatenate(parts[3:], axis=-1)]
    flat = jnp.concatenate(parts)
    total = flat.shape[0]
    source = jnp.zeros((total,), jnp.int32)
    source = source.at[targets[:total]].set(jnp.arange(total, dtype=jnp.int32))
    whole = flat[source].reshape(1, total * height, width)
    return [whole], [0], jnp.zeros((1,), jnp.int32)


def load_pieces(target_ref, part_refs, starts, held, base, sems):
    copies = []
    for ref, start in zip(part_refs, starts):
        inner, height, width = ref.shape
        for j in range(inner):
            row = pl.multiple_of(target_ref[len(copies)] * height, height)
            copies.append(
                pltpu.make_async_copy(
                    ref.at[j],
                    held.at[pl.ds(row, height), base + start : base + start + width],
                    sems.at[len(copies)],
                )
            )
    return copies


def run_copies(copies):
    for copy in copies:
        copy.start()
    for copy in copies:
        copy.wait()


def norm_rows(values):
    return lax.rsqrt(jnp.mean(values * values, axis=-1, keepdims=True) + EPS)


def sigmoid(values):
    return 1.0 / (1.0 + jnp.exp(-values))


def split_two(values):
    high = values.astype(BF)
    return high, (values - high.astype(F32)).astype(BF)


def spread_heads(values, spread):
    high, low = split_two(values)
    packed = high.astype(F32) + pltpu.roll(low.astype(F32), LANES // 2, 1)
    return nn(packed.astype(BF), spread)


def gather_heads(values, spread, heads_on):
    high, low = split_two(values)
    return jnp.where(heads_on, nt(high, spread) + nt(low, spread), 0.0)


def conv_rows(ext, kern, low, high, offset):
    summed = kern[4:5, low:high]
    for j in range(4):
        summed = summed + kern[j : j + 1, low:high] * ext[offset + j : offset + j + BL, low:high]
    return summed


def step_terms(raw, head_par, heads_on):
    shifted = raw + head_par[0:1]
    soft = jnp.maximum(shifted, 0.0) + jnp.log1p(jnp.exp(-jnp.abs(shifted)))
    step = jnp.where(heads_on, soft, 0.0)
    return shifted, step, -step * head_par[1:2]


def front_body(zi_ref, kern_ref, head_ref, spread_ref, y_ref, state_ref, ext, state):
    width = y_ref.shape[1]
    first = pl.program_id(0) == 0

    @pl.when(first)
    def _():
        ext[0:8, :] = jnp.zeros((8, ext.shape[1]), F32)
        state[...] = jnp.zeros(state.shape, F32)

    @pl.when(jnp.logical_not(first))
    def _():
        ext[0:8, :] = ext[BL : BL + 8, :]

    ext[8 : BL + 8, :] = zi_ref[...]
    rows = lax.broadcasted_iota(jnp.int32, (BL, LANES), 0)
    cols = lax.broadcasted_iota(jnp.int32, (BL, LANES), 1)
    causal = cols <= rows
    heads_on = cols < width // P_SIZE
    spread = spread_ref[...]
    state_ref[0] = state[...]
    pre = conv_rows(ext, kern_ref, 0, width, 5)
    x = pre * sigmoid(pre)
    pre = conv_rows(ext, kern_ref, width + LANES, ext.shape[1], 5)
    maps = pre * sigmoid(pre)
    b, c = maps[:, :NS], maps[:, NS:]
    shifted, step, decay = step_terms(zi_ref[:, width : width + LANES], head_ref, heads_on)
    cum = jnp.dot(causal.astype(F32), decay, precision=highest, preferred_element_type=F32)
    cum_t = cum.T
    last = cum[BL - 1 : BL]
    scores = nt(c.astype(BF), b.astype(BF))
    u = x * spread_heads(step, spread)
    from_start = spread_heads(jnp.where(heads_on, jnp.exp(cum), 0.0), spread)
    to_end = spread_heads(jnp.where(heads_on, jnp.exp(last - cum), 0.0), spread)
    u_low = u.astype(BF)
    left = cols < P_SIZE
    within = []
    for pair in range(width // LANES):
        mats = []
        for head in (2 * pair, 2 * pair + 1):
            gap = cum[:, head : head + 1] - cum_t[head : head + 1, :]
            mats.append((jnp.where(causal, jnp.exp(gap), 0.0) * scores).astype(BF))
        cut = u_low[:, pair * LANES : (pair + 1) * LANES]
        zero = jnp.zeros_like(cut)
        stacked = jnp.concatenate([jnp.where(left, cut, zero), jnp.where(left, zero, cut)], axis=0)
        within.append(nn(jnp.concatenate(mats, axis=1), stacked))
    before = state[...]
    across = nn(c.astype(BF), before.astype(BF)) * from_start
    y_ref[...] = jnp.concatenate(within, axis=1) + across + kern_ref[5:6, :width] * x
    grown = nn(b.T.astype(BF), (u * to_end).astype(BF))
    state[...] = before * from_start[BL - 1 : BL] + grown


def front_scan(zi, kern, head_par, spread):
    length, width = zi.shape[0], spread.shape[1]
    steps = length // BL
    return pl.pallas_call(
        front_body,
        grid=(steps,),
        out_shape=(
            jax.ShapeDtypeStruct((length, width), F32),
            jax.ShapeDtypeStruct((steps, NS, width), F32),
        ),
        in_specs=[
            pl.BlockSpec((BL, zi.shape[1]), lambda i: (i, 0)),
            pl.BlockSpec(kern.shape, lambda i: (0, 0)),
            pl.BlockSpec(head_par.shape, lambda i: (0, 0)),
            pl.BlockSpec(spread.shape, lambda i: (0, 0)),
        ],
        out_specs=(
            pl.BlockSpec((BL, width), lambda i: (i, 0)),
            pl.BlockSpec((1, NS, width), lambda i: (i, 0, 0)),
        ),
        scratch_shapes=[pltpu.VMEM((BL + 8, zi.shape[1]), F32), pltpu.VMEM((NS, width), F32)],
        compiler_params=pltpu.CompilerParams(
            dimension_semantics=("arbitrary",), vmem_limit_bytes=VMEM
        ),
        cost_estimate=SMALL,
        name="front_scan",
    )(zi, kern, head_par, spread)


def back_body(
    dy_ref, zi_ref, prev_ref, state_ref, kern_ref, head_ref, spread_ref,
    dia_ref, dib_ref, par_ref, hg_ref, ext, ext_d, d_state,
):
    width = dy_ref.shape[1]
    wide = zi_ref.shape[1]
    cut_at = dia_ref.shape[1]
    number = pl.program_id(0)
    steps = pl.num_programs(0)

    @pl.when(number == 0)
    def _():
        ext_d[BL : BL + 8, :] = jnp.zeros((8, wide), F32)
        d_state[...] = jnp.zeros(d_state.shape, F32)
        par_ref[...] = jnp.zeros(par_ref.shape, F32)
        hg_ref[...] = jnp.zeros(hg_ref.shape, F32)

    @pl.when(number > 0)
    def _():
        ext_d[BL : BL + 8, :] = ext_d[0:8, :]

    ext[0:8, :] = jnp.where(number == steps - 1, 0.0, prev_ref[...])
    ext[8 : BL + 8, :] = zi_ref[...]
    rows = lax.broadcasted_iota(jnp.int32, (BL, LANES), 0)
    cols = lax.broadcasted_iota(jnp.int32, (BL, LANES), 1)
    upper = rows <= cols
    strict = rows < cols
    heads_on = cols < width // P_SIZE
    left = cols < P_SIZE
    spread = spread_ref[...]
    pre_x = conv_rows(ext, kern_ref, 0, width, 5)
    sig_x = sigmoid(pre_x)
    x = pre_x * sig_x
    pre_m = conv_rows(ext, kern_ref, width + LANES, wide, 5)
    sig_m = sigmoid(pre_m)
    maps = pre_m * sig_m
    b, c = maps[:, :NS], maps[:, NS:]
    b_low, c_low = b.astype(BF), c.astype(BF)
    shifted, step, decay = step_terms(zi_ref[:, width : width + LANES], head_ref, heads_on)
    cum = jnp.dot(
        (cols <= rows).astype(F32), decay, precision=highest, preferred_element_type=F32
    )
    cum_t = cum.T
    last = cum[BL - 1 : BL]
    step_wide = spread_heads(step, spread)
    from_start = spread_heads(jnp.where(heads_on, jnp.exp(cum), 0.0), spread)
    to_end = spread_heads(jnp.where(heads_on, jnp.exp(last - cum), 0.0), spread)
    whole = from_start[BL - 1 : BL]
    d_y = dy_ref[...]
    par_ref[5:6, :width] += jnp.sum(d_y * x, axis=0, keepdims=True)
    u = x * step_wide
    u_low, dy_low = u.astype(BF), d_y.astype(BF)
    scores_t = nt(b_low, c_low)
    d_scores_t = jnp.zeros((BL, BL), F32)
    du_parts = []
    gap_rows = jnp.zeros((BL, LANES), F32)
    gap_cols = []
    for pair in range(width // LANES):
        lanes = slice(pair * LANES, (pair + 1) * LANES)
        cut_u, cut_d = u_low[:, lanes], dy_low[:, lanes]
        zero = jnp.zeros_like(cut_u)
        stack_u = jnp.concatenate([jnp.where(left, cut_u, zero), jnp.where(left, zero, cut_u)], axis=0)
        stack_d = jnp.concatenate([jnp.where(left, cut_d, zero), jnp.where(left, zero, cut_d)], axis=0)
        d_weights = nt(stack_u, cut_d)
        mats = []
        for place, head in enumerate((2 * pair, 2 * pair + 1)):
            gap = cum_t[head : head + 1, :] - cum[:, head : head + 1]
            decays = jnp.where(upper, jnp.exp(gap), 0.0)
            weight = decays * scores_t
            mats.append(weight.astype(BF))
            d_weight = d_weights[place * BL : (place + 1) * BL]
            d_scores_t = d_scores_t + decays * d_weight
            moved = jnp.where(strict, weight * d_weight, 0.0)
            gap_rows = jnp.where(cols == head, jnp.sum(moved, axis=1, keepdims=True), gap_rows)
            gap_cols.append(jnp.sum(moved, axis=0, keepdims=True))
        du_parts.append(nn(jnp.concatenate(mats, axis=1), stack_d))
    gap_cols.append(jnp.zeros((LANES - width // P_SIZE, BL), F32))
    gap_cols = jnp.concatenate(gap_cols, axis=0).T
    before, d_after = state_ref[0], d_state[...]
    before_low, d_after_low = before.astype(BF), d_after.astype(BF)
    dy_start = d_y * from_start
    dy_start_low = dy_start.astype(BF)
    reach = gather_heads(dy_start * nn(c_low, before_low), spread, heads_on)
    u_end = u * to_end
    d_from_state = nn(b_low, d_after_low)
    kept = gather_heads(u_end * d_from_state, spread, heads_on)
    carried = jnp.sum(before * d_after, axis=0, keepdims=True) * whole
    carried = gather_heads(jnp.broadcast_to(carried, (8, width)), spread, heads_on[:8])[0:1]
    d_c = nt(dy_start_low, before_low) + nn(d_scores_t.T.astype(BF), b_low)
    d_b = nt(u_end.astype(BF), d_after_low) + nn(d_scores_t.astype(BF), c_low)
    d_state[...] = d_after * whole + nn(c.T.astype(BF), dy_start_low)
    d_u = jnp.concatenate(du_parts, axis=1) + to_end * d_from_state
    d_decay = (
        jnp.dot(
            upper.astype(F32), reach + gap_cols - gap_rows, precision=highest,
            preferred_element_type=F32,
        )
        + jnp.dot(
            (cols < rows).astype(F32), kept, precision=highest, preferred_element_type=F32
        )
        + carried
    )
    d_step = gather_heads(x * d_u, spread, heads_on)
    rate = head_ref[1:2]
    d_raw = jnp.where(heads_on, (d_step - rate * d_decay) * sigmoid(shifted), 0.0)
    hg_ref[0:1, :] += jnp.sum(d_raw, axis=0, keepdims=True)
    hg_ref[1:2, :] += jnp.sum(jnp.where(heads_on, d_decay * decay, 0.0), axis=0, keepdims=True)
    d_x = step_wide * d_u + kern_ref[5:6, :width] * d_y
    ext_d[0:BL, :width] = d_x * sig_x * (1.0 + pre_x * (1.0 - sig_x))
    ext_d[0:BL, width : width + LANES] = jnp.zeros((BL, LANES), F32)
    ext_d[0:BL, width + LANES :] = (
        jnp.concatenate([d_b, d_c], axis=1) * sig_m * (1.0 + pre_m * (1.0 - sig_m))
    )
    for low, high in ((0, cut_at), (cut_at, width), (width + LANES, wide)):
        d_act = ext_d[0:BL, low:high]
        d_in = jnp.zeros((BL, high - low), F32)
        for j in range(4):
            d_in = d_in + kern_ref[j : j + 1, low:high] * ext_d[3 - j : 3 - j + BL, low:high]
            par_ref[j : j + 1, low:high] += jnp.sum(
                d_act * ext[5 + j : 5 + j + BL, low:high], axis=0, keepdims=True
            )
        par_ref[4:5, low:high] += jnp.sum(d_act, axis=0, keepdims=True)
        if low < cut_at:
            dia_ref[...] = d_in.astype(BF)
        else:
            dib_ref[:, low - cut_at : high - cut_at] = d_in.astype(BF)
    dib_ref[:, width - cut_at : width - cut_at + LANES] = d_raw.astype(BF)


def back_scan(d_y, zi, states, kern, head_par, spread, cut_at):
    length, width = d_y.shape
    wide = zi.shape[1]
    steps = length // BL
    per = BL // 8

    def back(i):
        return (steps - 1 - i, 0)

    def fixed(i):
        return (0, 0)

    return pl.pallas_call(
        back_body,
        grid=(steps,),
        out_shape=(
            jax.ShapeDtypeStruct((length, cut_at), BF),
            jax.ShapeDtypeStruct((length, wide - cut_at), BF),
            jax.ShapeDtypeStruct((8, wide), F32),
            jax.ShapeDtypeStruct((8, LANES), F32),
        ),
        in_specs=[
            pl.BlockSpec((BL, width), back),
            pl.BlockSpec((BL, wide), back),
            pl.BlockSpec((8, wide), lambda i: (jnp.maximum((steps - 1 - i) * per - 1, 0), 0)),
            pl.BlockSpec((1, NS, width), lambda i: (steps - 1 - i, 0, 0)),
            pl.BlockSpec(kern.shape, fixed),
            pl.BlockSpec(head_par.shape, fixed),
            pl.BlockSpec(spread.shape, fixed),
        ],
        out_specs=(
            pl.BlockSpec((BL, cut_at), back),
            pl.BlockSpec((BL, wide - cut_at), back),
            pl.BlockSpec((8, wide), fixed),
            pl.BlockSpec((8, LANES), fixed),
        ),
        scratch_shapes=[
            pltpu.VMEM((BL + 8, wide), F32),
            pltpu.VMEM((BL + 8, wide), F32),
            pltpu.VMEM((NS, width), F32),
        ],
        compiler_params=pltpu.CompilerParams(
            dimension_semantics=("arbitrary",), vmem_limit_bytes=VMEM
        ),
        cost_estimate=SMALL,
        name="back_scan",
    )(d_y, zi, zi, states, kern, head_par, spread)


def small_call(body, outs, args, name, scalars=0):
    vmem, smem = pl.BlockSpec(memory_space=pltpu.VMEM), pl.BlockSpec(memory_space=pltpu.SMEM)
    return pl.pallas_call(
        body,
        out_shape=tuple(jax.ShapeDtypeStruct(shape, kind) for shape, kind in outs),
        in_specs=[smem] * scalars + [vmem] * (len(args) - scalars),
        out_specs=tuple(vmem for _ in outs),
        compiler_params=pltpu.CompilerParams(vmem_limit_bytes=VMEM),
        cost_estimate=SMALL,
        name=name,
    )(*args)


def stack_columns(blocks, start, width):
    height = blocks[0].shape[0]

    def body(*refs):
        for number, ref in enumerate(refs[:-1]):
            refs[-1][number] = ref[:, start : start + width]

    shape = (len(blocks), height, width)
    return small_call(body, [(shape, blocks[0].dtype)], blocks, "stack_columns")[0]


def stack_pairs(first, second):
    height, low = first[0].shape
    high = second[0].shape[1]

    def body(*refs):
        for number in range(len(first)):
            refs[-1][number, :, :low] = refs[number][...]
            refs[-1][number, :, low:] = refs[len(first) + number][...]

    shape = (len(first), height, low + high)
    return small_call(body, [(shape, first[0].dtype)], [*first, *second], "stack_pairs")[0]


def cut_columns(values, start, width):
    def body(values_ref, out_ref):
        out_ref[...] = values_ref[:, :, start : start + width]

    return small_call(
        body, [(values.shape[:2] + (width,), values.dtype)], [values], "cut_columns"
    )[0]


def cut_rows_of(values, start, rows):
    def body(values_ref, out_ref):
        out_ref[...] = values_ref[start : start + rows]

    return small_call(body, [((rows, values.shape[1]), values.dtype)], [values], "cut_rows")[0]


def pair_rows(pairs, core):
    def body(core_ref, *refs):
        for number in range(len(pairs)):
            mine_ref, other_ref = refs[2 * number : 2 * number + 2]
            out_ref = refs[2 * len(pairs) + number]
            out_ref[core_ref[0]] = mine_ref[...]
            out_ref[1 - core_ref[0]] = other_ref[...]

    outs = [((2,) + mine.shape, mine.dtype) for mine, _ in pairs]
    args = [core] + [item for pair in pairs for item in pair]
    done = small_call(body, outs, args, "pair_rows", 1)
    return [item.reshape(-1, item.shape[2]) for item in done]


def add_blocks(groups, height, count, kind, where, name):
    total = sum(width for width, _, _ in groups)
    flat = [(width, item) for width, items, _ in groups for item in items]
    overs = []
    for _, _, over in groups:
        if over is not None and not any(over[0] is array for array in overs):
            overs.append(over[0])

    if height % 32:
        columns = []
        for width, items, over in groups:
            term = 0.0
            for array, number, spot in items:
                part = array[:, number * width : (number + 1) * width].reshape(-1, height, width)
                picked = [pick(part, spot(i, where)) for i in range(count)]
                term = term + jnp.concatenate(picked).astype(F32)
            if over is not None:
                term = term + over[0][:, over[1] : over[1] + width].astype(F32)
            columns.append(term)
        return jnp.concatenate(columns, axis=1).astype(kind)

    def body(where_ref, *refs):
        item_refs = refs[: len(flat)]
        over_refs = refs[len(flat) : len(flat) + len(overs)]
        out_ref, sems = refs[len(flat) + len(overs)], refs[-1]
        helds = refs[len(flat) + len(overs) + 1 : -1]
        copies = []
        for row, (ref, held, (width, (_, number, spot))) in enumerate(zip(item_refs, helds, flat)):
            for i in range(count):
                start = pl.multiple_of(spot(i, where_ref) * height, height)
                copies.append(
                    pltpu.make_async_copy(
                        ref.at[pl.ds(start, height), number * width : (number + 1) * width],
                        held.at[i * height : (i + 1) * height],
                        sems.at[row, i],
                    )
                )
        run_copies(copies)
        at = start = 0
        for width, items, over in groups:
            term = helds[at][...]
            if len(items) > 1 or over is not None:
                term = term.astype(F32)
            for held in helds[at + 1 : at + len(items)]:
                term = term + held[...].astype(F32)
            if over is not None:
                (number,) = [i for i, array in enumerate(overs) if array is over[0]]
                term = term + over_refs[number][:, over[1] : over[1] + width].astype(F32)
            out_ref[:, start : start + width] = term.astype(kind)
            at += len(items)
            start += width

    vmem, any_ref = pl.BlockSpec(memory_space=pltpu.VMEM), pl.BlockSpec(memory_space=pl.ANY)
    return pl.pallas_call(
        body,
        out_shape=jax.ShapeDtypeStruct((count * height, total), kind),
        in_specs=[pl.BlockSpec(memory_space=pltpu.SMEM)]
        + [any_ref] * len(flat)
        + [vmem] * len(overs),
        out_specs=vmem,
        scratch_shapes=[
            pltpu.VMEM((count * height, width), item[0].dtype) for width, item in flat
        ]
        + [pltpu.SemaphoreType.DMA((len(flat), count))],
        compiler_params=pltpu.CompilerParams(vmem_limit_bytes=VMEM),
        cost_estimate=SMALL,
        name=name,
    )(where, *[item[0] for _, item in flat], *overs)


class Plane:
    def __init__(self, values, bits, where, lines):
        self.values, self.bits, self.where, self.lines = values, bits, where, lines
        self.height = values[0][0].shape[0] // (lines * GROUP)
        self.came = self.came_last = None

    def _spot(self, i, first, second):
        x, y = (first, second) if self.bits == 1 else (second, first)
        return i * GROUP + y * 2 + x

    def _own(self, where, axis):
        return lax.rem(where[0], 2) if axis == 1 else where[0] // 2

    def start(self, order):
        def spot(i, where):
            return self._spot(i // 2, 1 - self._own(where, self.bits), i % 2)

        groups = [
            (width, [(order(array), number, spot)], None) for array, number, width in self.values
        ]
        return add_blocks(groups, self.height, 2 * self.lines, BF, self.where, "plane_start")

    def _groups(self, keep, line_at, last):
        def which(where):
            own = self._own(where, 3 - self.bits)
            return own if keep else 1 - own

        def in_came(i, where):
            return 2 * line_at(i, where) + which(where)

        def in_values(i, where):
            return self._spot(line_at(i, where), self._own(where, self.bits), which(where))

        width = sum(item[2] for item in self.values)
        groups = []
        start = 0
        for array, number, wide in self.values:
            items = [(array, number, in_values), (self.came, start, in_came)]
            if last:
                items.append((self.came_last, start, line_at))
            groups.append((wide, items, None))
            start += 1
        return groups

    def turn(self):
        return add_blocks(
            self._groups(False, lambda i, where: i, False), self.height, self.lines, BF,
            self.where, "plane_turn",
        )

    def groups(self, line_at):
        return self._groups(True, line_at, True)


class LineSums:
    def __init__(self, parts, order, lines, height, where):
        self.parts, self.order, self.lines = parts, order, lines
        self.height, self.where = height, where
        self.steps, self.final, self.names = {}, {}, []
        self.sent = None

    def _step(self, names, overs, kind):
        groups = []
        for name in names:
            back = self.steps[name] + 1

            def line_at(i, spots, back=back):
                return lax.rem(spots[1] - back + 2 * self.lines, self.lines)

            over = overs.get(name)
            start = 0
            for width, items, _ in self.parts[name](line_at):
                groups.append((width, items, None if over is None else (over[0], over[1] + start)))
                start += width
        return add_blocks(groups, self.height, 1, kind, self.where, "line_step")

    def _send(self, names, overs):
        self.names = names
        self.sent = self._step(names, overs, BF) if names else None

    def start(self, *names):
        for name in names:
            self.steps[name] = 0
        self._send(list(names), {})

    def run(self, count, *new):
        for number in range(count):
            joining = list(new) if number + 1 == count else []
            overs = {}
            if self.names:
                came = self.order(next_line(self.sent))
                start = 0
                for name in self.names:
                    overs[name] = (came, start)
                    start += sum(width for width, _, _ in self.parts[name](None))
                    self.steps[name] += 1
                    if self.steps[name] + 1 == self.lines:
                        self.final[name] = self._step([name], overs, F32)
            staying = [name for name in self.names if name not in self.final]
            for name in joining:
                self.steps[name] = 0
            if staying or joining or self.names:
                self._send(staying + joining, overs)


def member_pieces(gu, down, where, height):
    wide, narrow = gu.shape[1], down.shape[1]

    def spot_of(k, spots):
        bit_0 = lax.rem(spots[0] + k % 2, 2)
        return bit_0 + 2 * lax.rem(spots[0] // 2 + k // 2, 2)

    if height % 32:
        return [
            jnp.concatenate(
                [pick(item.reshape(GROUP, height, -1), spot_of(k, where)) for item in (gu, down)],
                axis=1,
            ).astype(BF)
            for k in range(GROUP)
        ]

    def body(where_ref, gu_ref, down_ref, *out_refs):
        for k, out_ref in enumerate(out_refs):
            rows = pl.ds(pl.multiple_of(spot_of(k, where_ref) * height, height), height)
            out_ref[:, :wide] = gu_ref[rows, :].astype(BF)
            out_ref[:, wide:] = down_ref[rows, :].astype(BF)

    return list(
        small_call(
            body, [((height, wide + narrow), BF)] * GROUP, [where, gu, down], "member_pieces", 1
        )
    )


def gathered_call(body, tile, row_args, fixed_args, matrices, shift, outs, name):
    depth = sum(part.shape[0] * part.shape[1] for part in matrices[0][0][:4])
    widths = [parts[0].shape[2] for parts, _, _ in matrices]
    counts = [len(parts) for parts, _, _ in matrices]
    targets = matrices[0][2]
    rows = row_args[0].shape[0]
    steps = rows // tile
    row_count, fixed_count = len(row_args), len(fixed_args)

    def whole(*refs):
        order_ref = refs[0]
        at = 2
        row_refs = refs[at : at + row_count]
        at += row_count
        fixed_refs = refs[at : at + fixed_count]
        at += fixed_count
        part_refs = refs[at : at + sum(counts)]
        at += sum(counts)
        out_refs = refs[at : at + len(outs)]
        held, sems = refs[-2], refs[-1]

        @pl.when(pl.program_id(0) == 0)
        def _():
            copies = []
            used = base = 0
            for number, (count, width) in enumerate(zip(counts, widths)):
                copies += load_pieces(
                    order_ref, part_refs[used : used + count], matrices[number][1], held, base,
                    sems.at[number],
                )
                used += count
                base += width
            run_copies(copies)

        body(row_refs, fixed_refs, held, out_refs, pl.program_id(0))

    def rows_map(i, order_ref, shift_ref):
        return (lax.rem(i + shift_ref[0], steps), 0)

    def fixed_map(i, order_ref, shift_ref):
        return (0, 0)

    def low_map(i, order_ref, shift_ref):
        return (jnp.minimum(i, steps // 2 - 1), 0)

    def high_map(i, order_ref, shift_ref):
        return (jnp.maximum(i - steps // 2, 0), 0)

    maps = {"rows": rows_map, "low": low_map, "high": high_map}

    def out_spec(shape, kind):
        if kind == "one":
            return pl.BlockSpec(shape, fixed_map)
        return pl.BlockSpec((tile, shape[1]), maps[kind])

    return pl.pallas_call(
        whole,
        grid_spec=pltpu.PrefetchScalarGridSpec(
            num_scalar_prefetch=2,
            grid=(steps,),
            in_specs=[pl.BlockSpec((tile, arg.shape[1]), rows_map) for arg in row_args]
            + [pl.BlockSpec(arg.shape, fixed_map) for arg in fixed_args]
            + [pl.BlockSpec(memory_space=pl.ANY)] * sum(counts),
            out_specs=tuple(out_spec(shape, kind) for shape, _, kind in outs),
            scratch_shapes=[
                pltpu.VMEM((depth, sum(widths)), BF),
                pltpu.SemaphoreType.DMA((len(matrices), targets.shape[0])),
            ],
        ),
        out_shape=tuple(jax.ShapeDtypeStruct(shape, kind) for shape, kind, _ in outs),
        compiler_params=pltpu.CompilerParams(
            dimension_semantics=("arbitrary",), vmem_limit_bytes=VMEM
        ),
        cost_estimate=SMALL,
        name=name,
    )(targets, shift, *row_args, *fixed_args, *[part for parts, _, _ in matrices for part in parts])


NO_SHIFT = (0,)


def inner_product(normed, matrix, small):
    rows, depth = normed.shape
    width = matrix[0][0].shape[2]

    def body(row_refs, fixed_refs, held, out_refs, number):
        out_refs[0][...] = nn(row_refs[0][...], held[...])

        @pl.when(number == 0)
        def _():
            out_refs[1][...] = held[:, small : small + LANES]

    return gathered_call(
        body, 256, [normed], [], [matrix], jnp.array(NO_SHIFT, jnp.int32),
        [((rows, width), F32, "rows"), ((depth, LANES), BF, "one")], "inner_product",
    )


def gate_product(normed, y, matrix):
    rows, width = y.shape

    def body(row_refs, fixed_refs, held, out_refs, number):
        gate = nn(row_refs[0][...], held[...])
        out_refs[0][...] = gate
        gated = row_refs[1][...] * gate * sigmoid(gate)
        total = jnp.sum(gated * gated, axis=1, keepdims=True)
        out_refs[1][...] = jnp.broadcast_to(total, out_refs[1].shape)

    return gathered_call(
        body, 256, [normed, y], [], [matrix], jnp.array(NO_SHIFT, jnp.int32),
        [((rows, width), F32, "rows"), ((rows, LANES), F32, "rows")], "gate_product",
    )


def row_scales(squares_ref, others_ref, width):
    return lax.rsqrt((squares_ref[:, 0:1] + others_ref[:, 0:1]) / width + EPS)


def split_rows(value, number, steps, low_ref, high_ref):
    @pl.when(number < steps // 2)
    def _():
        low_ref[...] = value

    @pl.when(number >= steps // 2)
    def _():
        high_ref[...] = value


def mixed_product(y, gate, squares, others, kern, matrix, shift, inner_all):
    rows, width = y.shape
    depth = sum(part.shape[0] * part.shape[1] for part in matrix[0][:4])
    tile = 256

    def body(row_refs, fixed_refs, held, out_refs, number):
        gate_now = row_refs[1][...]
        scale = row_scales(row_refs[2], row_refs[3], inner_all)
        scaled = row_refs[0][...] * gate_now * sigmoid(gate_now) * scale
        scaled = (scaled * fixed_refs[0][6:7, :width]).astype(BF)
        out_refs[0][...] = scaled
        mixed = nt(scaled, held[...])
        split_rows(mixed, number, rows // tile, out_refs[1], out_refs[2])

    return gathered_call(
        body, tile, [y, gate, squares, others], [kern], [matrix], shift,
        [
            ((rows, width), BF, "rows"), ((rows // 2, depth), F32, "low"),
            ((rows // 2, depth), F32, "high"),
        ],
        "mixed_product",
    )


def gate_back(d_mix, y, gate, squares, others, pulls, kern, matrix, cut_at, inner_all):
    rows, width = y.shape

    def body(row_refs, fixed_refs, held, out_refs, number):
        d_scaled = nn(row_refs[0][...], held[...])
        y_now, gate_now = row_refs[1][...], row_refs[2][...]
        scale = row_scales(row_refs[3], row_refs[4], inner_all)
        pull = scale * scale * row_refs[5][:, 0:1] / inner_all
        sig = sigmoid(gate_now)
        silu = gate_now * sig
        gated = y_now * silu
        scaled_in = d_scaled * scale
        d_gated = scaled_in * fixed_refs[0][6:7, :width] - gated * pull

        @pl.when(number == 0)
        def _():
            out_refs[3][...] = jnp.zeros(out_refs[3].shape, F32)

        out_refs[3][0:1, :] += jnp.sum(scaled_in * gated, axis=0, keepdims=True)
        out_refs[0][...] = d_gated * silu
        d_gate = (d_gated * y_now * sig * (1.0 + gate_now * (1.0 - sig))).astype(BF)
        out_refs[1][...] = d_gate[:, :cut_at]
        out_refs[2][...] = d_gate[:, cut_at:]

    return gathered_call(
        body, 256, [d_mix, y, gate, squares, others, pulls], [kern], [matrix],
        jnp.array(NO_SHIFT, jnp.int32),
        [
            ((rows, width), F32, "rows"), ((rows, cut_at), BF, "rows"),
            ((rows, width - cut_at), BF, "rows"), ((8, width), F32, "one"),
        ],
        "gate_back",
    )


def normed_back(grads, matrices, shift):
    rows = grads[0].shape[0]
    widths = [grad.shape[1] for grad in grads]
    depth = sum(part.shape[0] * part.shape[1] for part in matrices[0][0][:4])
    tile = 256

    def body(row_refs, fixed_refs, held, out_refs, number):
        total = None
        start = 0
        for ref, width in zip(row_refs, widths):
            term = nt(ref[...], held[:, start : start + width])
            total = term if total is None else total + term
            start += width
        split_rows(total, number, rows // tile, out_refs[0], out_refs[1])

    return gathered_call(
        body, tile, grads, [], matrices, shift,
        [((rows // 2, depth), F32, "low"), ((rows // 2, depth), F32, "high")], "normed_back",
    )


def rows_call(body, tile, row_args, fixed_args, outs, name):
    arrays = [arg if isinstance(arg, tuple) else (arg, None) for arg in row_args]
    rows = arrays[0][0].shape[-2]

    def spec(array, number):
        if number is None:
            return pl.BlockSpec((tile, array.shape[1]), lambda i: (i, 0))
        return pl.BlockSpec((None, tile, array.shape[2]), lambda i: (number, i, 0))

    return pl.pallas_call(
        body,
        grid=(rows // tile,),
        out_shape=tuple(jax.ShapeDtypeStruct(shape, kind) for shape, kind, _ in outs),
        in_specs=[spec(*item) for item in arrays]
        + [pl.BlockSpec(arg.shape, lambda i: (0, 0)) for arg in fixed_args],
        out_specs=tuple(
            pl.BlockSpec(shape, lambda i: (0, 0))
            if one
            else pl.BlockSpec((tile, shape[1]), lambda i: (i, 0))
            for shape, _, one in outs
        ),
        compiler_params=pltpu.CompilerParams(
            dimension_semantics=("arbitrary",), vmem_limit_bytes=VMEM
        ),
        cost_estimate=SMALL,
        name=name,
    )(*[array for array, _ in arrays], *fixed_args)


def columns_call(body, row_args, outs, name):
    arrays = [arg if isinstance(arg, tuple) else (arg, None) for arg in row_args]
    width = arrays[0][0].shape[-1]
    tile = width // 2

    def spec(array, number):
        if number is None:
            return pl.BlockSpec((array.shape[0], tile), lambda i: (0, i))
        return pl.BlockSpec((None, array.shape[1], tile), lambda i: (number, 0, i))

    return pl.pallas_call(
        body,
        grid=(width // tile,),
        out_shape=tuple(jax.ShapeDtypeStruct(shape, BF) for shape in outs),
        in_specs=[spec(*item) for item in arrays],
        out_specs=tuple(pl.BlockSpec((shape[0], tile), lambda i: (0, i)) for shape in outs),
        compiler_params=pltpu.CompilerParams(
            dimension_semantics=("arbitrary",), vmem_limit_bytes=VMEM
        ),
        cost_estimate=SMALL,
        name=name,
    )(*[array for array, _ in arrays])


def normed_rows(tokens, others, gain, core):
    rows, width = tokens.shape
    tile = 128

    def body(core_ref, mine_ref, other_ref, gain_ref, out_ref):
        for ref, spot in ((mine_ref, core_ref[0]), (other_ref, 1 - core_ref[0])):
            values = ref[...].astype(F32)
            out_ref[spot] = (values * norm_rows(values) * gain_ref[...]).astype(BF)

    by_rows = pl.BlockSpec((tile, width), lambda i: (i, 0))
    return pl.pallas_call(
        body,
        grid=(rows // tile,),
        out_shape=jax.ShapeDtypeStruct((2, rows, width), BF),
        in_specs=[
            pl.BlockSpec(memory_space=pltpu.SMEM), by_rows, by_rows,
            pl.BlockSpec((1, width), lambda i: (0, 0)),
        ],
        out_specs=pl.BlockSpec((2, tile, width), lambda i: (0, i, 0)),
        compiler_params=pltpu.CompilerParams(
            dimension_semantics=("arbitrary",), vmem_limit_bytes=VMEM
        ),
        cost_estimate=SMALL,
        name="normed_rows",
    )(core, tokens, others, gain).reshape(2 * rows, width)


def marked_rows(grad_out, routes, first_lane):
    rows, width = grad_out.shape

    def body(grad_ref, routes_ref, out_ref):
        out_ref[:, :width] = grad_ref[...]
        lane = lax.broadcasted_iota(jnp.int32, (grad_ref.shape[0], LANES), 1)
        marks = jnp.zeros(lane.shape, F32)
        for number in range(routes_ref.shape[1]):
            marks = jnp.where(lane == routes_ref[:, number : number + 1] + first_lane, 1.0, marks)
        out_ref[:, width:] = marks.astype(BF)

    return rows_call(
        body, 256, [grad_out, routes], [], [((rows, width + LANES), BF, False)], "marked_rows"
    )[0]


def mid_rows_of(mixed, others, tokens, gain):
    rows, width = tokens.shape

    def body(mixed_ref, other_ref, tokens_ref, gain_ref, resid_ref, mid_ref):
        resid = tokens_ref[...].astype(F32) + mixed_ref[...] + other_ref[...]
        resid_ref[...] = resid
        mid_ref[...] = (resid * norm_rows(resid) * gain_ref[...]).astype(BF)

    return rows_call(
        body, 256, [mixed, others, tokens], [gain],
        [((rows, width), F32, False), ((rows, width), BF, False)], "mid_rows",
    )


def across_sum(mine, came, number):
    _, rows, width = mine.shape
    cut = rows // 2

    def body(mine_ref, came_ref, low_ref, high_ref):
        total = (mine_ref[...].astype(F32) + came_ref[...].astype(F32)).astype(BF)
        low_ref[...] = total[:cut]
        high_ref[...] = total[cut:]

    return columns_call(
        body, [(mine, number), (came, number)], [(cut, width)] * 2, "across_sum"
    )


def side_sums(mine, came, over_x, over_y):
    _, rows, width = mine.shape
    cut = rows // 2

    def body(mine_x, came_x, mine_y, came_y, over_x_ref, over_y_ref, x_ref, y_ref):
        to_x = mine_x[...].astype(F32) + came_x[...].astype(F32)
        x_ref[:cut] = to_x[:cut].astype(BF)
        x_ref[cut:] = (to_x[cut:] + over_y_ref[...].astype(F32)).astype(BF)
        to_y = mine_y[...].astype(F32) + came_y[...].astype(F32)
        y_ref[:cut] = (to_y[:cut] + over_x_ref[...].astype(F32)).astype(BF)
        y_ref[cut:] = to_y[cut:].astype(BF)

    return columns_call(
        body, [(mine, 0), (came, 0), (mine, 1), (came, 1), over_x, over_y],
        [(rows, width)] * 2, "side_sums",
    )


def own_sum(mine_ref, came_ref, x_ref, y_ref):
    return (
        mine_ref[...].astype(F32) + came_ref[...].astype(F32)
        + x_ref[...].astype(F32) + y_ref[...].astype(F32)
    )


def norm_back(d_rows, values, gain, grad_ref):
    scale = norm_rows(values)

    @pl.when(pl.program_id(0) == 0)
    def _():
        grad_ref[...] = jnp.zeros(grad_ref.shape, F32)

    grad_ref[0:1, :] += jnp.sum(d_rows * values * scale, axis=0, keepdims=True)
    pulled = d_rows * gain
    mean = jnp.mean(values * pulled, axis=-1, keepdims=True)
    return scale * pulled - values * (scale * scale * scale) * mean


def resid_back(mine, came, from_x, from_y, resid, tokens, grad_out, gain):
    rows, width = tokens.shape

    def body(
        mine_ref, came_ref, x_ref, y_ref, resid_ref, tokens_ref, grad_ref, gain_ref,
        d_resid_ref, d_mix_ref, pulls_ref, gain_grad_ref,
    ):
        resid_now = resid_ref[...]
        d_mid = own_sum(mine_ref, came_ref, x_ref, y_ref)
        d_extra = norm_back(d_mid, resid_now, gain_ref[...], gain_grad_ref)
        d_resid = grad_ref[...].astype(F32) + d_extra
        d_resid_ref[...] = d_resid
        d_mix = d_resid.astype(BF)
        d_mix_ref[...] = d_mix
        mixed = resid_now - tokens_ref[...].astype(F32)
        pull = jnp.sum(d_mix.astype(F32) * mixed, axis=1, keepdims=True)
        pulls_ref[...] = jnp.broadcast_to(pull, pulls_ref.shape)

    return rows_call(
        body, 256, [(mine, 0), (came, 0), from_x, from_y, resid, tokens, grad_out], [gain],
        [
            ((rows, width), F32, False), ((rows, width), BF, False),
            ((rows, LANES), F32, False), ((8, width), F32, True),
        ],
        "resid_back",
    )


def output_rows(mine, came, from_x, from_y, resid):
    def body(mine_ref, came_ref, x_ref, y_ref, resid_ref, out_ref):
        out_ref[...] = (resid_ref[...] + own_sum(mine_ref, came_ref, x_ref, y_ref)).astype(BF)

    return rows_call(
        body, 256, [(mine, 0), (came, 0), from_x, from_y, resid], [], [(resid.shape, BF, False)],
        "output_rows",
    )[0]


def tokens_back(mine, came, tokens, d_resid, gain):
    rows, width = tokens.shape

    def body(mine_ref, came_ref, tokens_ref, d_resid_ref, gain_ref, out_ref, gain_grad_ref):
        d_rows = mine_ref[...] + came_ref[...]
        d_extra = norm_back(d_rows, tokens_ref[...].astype(F32), gain_ref[...], gain_grad_ref)
        out_ref[...] = (d_resid_ref[...] + d_extra).astype(BF)

    return rows_call(
        body, 256, [mine, came, tokens, d_resid], [gain],
        [((rows, width), BF, False), ((8, width), F32, True)], "tokens_back",
    )


def pack_small(par_grads, head_grads, gain_grads, mid_gains, in_gains, spread, core, local, heads):
    width_d = in_gains.shape[1]
    both = 2 * local
    rest = par_grads.shape[1] - local - LANES

    def body(core_ref, par_ref, head_ref, gain_ref, mid_ref, in_ref, spread_ref, out_ref):
        out_ref[...] = jnp.zeros(out_ref.shape, F32)
        spot = pl.ds(pl.multiple_of(core_ref[0] * local, LANES), local)
        out_ref[0:5, spot] = par_ref[0:5, :local]
        out_ref[0:5, both:] = par_ref[0:5, local + LANES :]
        out_ref[5:6, spot] = gain_ref[0:1, :]
        out_ref[6:7, :width_d] = in_ref[0:1, :]
        out_ref[6:7, width_d : 2 * width_d] = mid_ref[0:1, :]
        lane = lax.broadcasted_iota(jnp.int32, (8, LANES), 1)
        skip = gather_heads(par_ref[:, :local], spread_ref[...], lane < heads)
        for number, row in enumerate((head_ref[0:1], head_ref[1:2], skip[5:6])):
            start = pl.multiple_of((2 * number + core_ref[0]) * LANES, LANES)
            out_ref[7:8, pl.ds(start, LANES)] = row

    return small_call(
        body, [((8, both + rest), F32)],
        [core, par_grads, head_grads, gain_grads, mid_gains, in_gains, spread], "pack_small", 1,
    )[0]


def unpack_experts(came, place, units, shared_units):
    height, width = came[0].shape
    hidden = width // 3
    own = EXPERTS // GROUP

    def body(place_ref, *refs):
        came_refs, (gu_ref, down_ref, sgu_ref, sdown_ref) = refs[:GROUP], refs[GROUP:]
        for k in range(GROUP):
            bit_0 = lax.rem(place_ref[0] + k % 2, 2)
            bit_1 = lax.rem(place_ref[0] // 2 + k // 2, 2)
            member = bit_0 + 2 * bit_1
            for e in range(own):
                expert = member * own + e
                for j in range(2):
                    start = j * hidden + e * units
                    gu_ref[expert, :, j, :] = came_refs[k][:, start : start + units].astype(F32)
                start = 2 * hidden + e * units
                down_ref[expert] = came_refs[k][:, start : start + units].astype(F32).T
            spot = pl.ds(pl.multiple_of(member * shared_units, shared_units), shared_units)
            for j in range(2):
                start = j * hidden + own * units
                sgu_ref[:, j, spot] = came_refs[k][:, start : start + shared_units].astype(F32)
            start = 2 * hidden + own * units
            sdown_ref[spot, :] = came_refs[k][:, start : start + shared_units].astype(F32).T

    return pl.pallas_call(
        body,
        out_shape=(
            jax.ShapeDtypeStruct((EXPERTS, height, 2, units), F32),
            jax.ShapeDtypeStruct((EXPERTS, units, height), F32),
            jax.ShapeDtypeStruct((height, 2, GROUP * shared_units), F32),
            jax.ShapeDtypeStruct((GROUP * shared_units, height), F32),
        ),
        in_specs=[pl.BlockSpec(memory_space=pltpu.SMEM)]
        + [pl.BlockSpec(memory_space=pltpu.VMEM)] * GROUP,
        out_specs=(pl.BlockSpec(memory_space=pltpu.VMEM),) * 4,
        compiler_params=pltpu.CompilerParams(vmem_limit_bytes=VMEM),
        cost_estimate=SMALL,
        name="unpack_experts",
    )(place, *came)


def expert_body(plan, *refs):
    own, units, shared, counts, part_count, aliased = plan
    hidden = own * units + shared
    refs = list(refs)

    def take(number):
        out = refs[:number]
        del refs[:number]
        return out

    order_ref, base_ref = take(2)
    x_pieces = [take(number) for number in counts]
    ym_pieces = [take(number) for number in counts]
    count = len(counts)
    (router_ref,) = take(1)
    part_refs = take(part_count)
    take(aliased)
    x_out, dy_out, gu_ref, down_ref = take(4)
    out_mine, out_other, dx_mine, dx_other = take(4)
    w, sems, x_held, ym_held, row_sems = refs
    step = pl.program_id(0)
    width = router_ref.shape[0]

    def fetch(number):
        slot = number % 2
        copies = []
        for which, (parts, target) in enumerate(
            ((x_pieces[number], x_held), (ym_pieces[number], ym_held))
        ):
            start = 0
            for half, ref in enumerate(parts):
                rows = ref.shape[0]
                copies.append(
                    pltpu.make_async_copy(
                        ref, target.at[slot, start : start + rows], row_sems.at[which, slot, half]
                    )
                )
                start += rows
        return copies

    @pl.when(step == 0)
    def _():
        loads = load_pieces(order_ref, part_refs, [0] * part_count, w, 0, sems)
        for copy in fetch(0) + loads:
            copy.start()
        for copy in loads:
            copy.wait()

    for number in range(count):

        @pl.when(step == number)
        def _():
            if number + 1 < count:
                for copy in fetch(number + 1):
                    copy.start()
            for copy in fetch(number):
                copy.wait()

    slot = lax.rem(step, 2)
    x_now, ym_now = x_held.at[slot], ym_held.at[slot]
    x_out[...] = x_now[...]
    dy_out[...] = ym_now[:, :width]
    tile = x_now.shape[0]
    lane = lax.broadcasted_iota(jnp.int32, (tile, LANES), 1)
    routed = ym_now[:, width:].astype(F32) > 0.5
    logits = nn(x_now[...], router_ref[...])
    top = jnp.max(jnp.where(routed, logits, -1e30), axis=1, keepdims=True)
    powers = jnp.where(routed, jnp.exp(jnp.where(routed, logits - top, 0.0)), 0.0)
    gates = powers / jnp.sum(powers, axis=1, keepdims=True)
    d_gates = jnp.zeros((tile, LANES), F32)
    parts = [(e * units, units, e) for e in range(own)] + [(own * units, shared, None)]
    for start, size, expert in parts:
        cols = [slice(k * hidden + start, k * hidden + start + size) for k in range(3)]
        pre = nn(x_now[...], w[:, cols[0]])
        up = nn(x_now[...], w[:, cols[1]])
        d_act = nn(ym_now[:, :width], w[:, cols[2]])
        sig = sigmoid(pre)
        silu = pre * sig
        act = (silu * up).astype(BF).astype(F32)
        if expert is not None:
            here = lane == base_ref[0] + expert
            gate = jnp.sum(jnp.where(here, gates, 0.0), axis=1, keepdims=True)
            d_gate = jnp.sum(act * d_act, axis=1, keepdims=True)
            d_gates = jnp.where(here, d_gate, d_gates)
            d_act = d_act * gate
            act = act * gate
        gu_ref[:, cols[0]] = (d_act * up * sig * (1.0 + pre * (1.0 - sig))).astype(BF)
        gu_ref[:, cols[1]] = (d_act * silu).astype(BF)
        down_ref[:, start : start + size] = act.astype(BF)
    mean = jnp.sum(gates * d_gates, axis=1, keepdims=True)
    d_logits = (gates * (d_gates - mean)).astype(BF)
    gu_ref[:, 2 * hidden :] = d_logits
    cut = 256

    def results(out_ref, dx_ref):
        for number in range(width // cut):
            rows = slice(number * cut, (number + 1) * cut)
            out_ref[0, :, rows] = nt(down_ref[...], w[rows, 2 * hidden :]).astype(BF)
            d_x = nt(gu_ref[:, : 2 * hidden], w[rows, : 2 * hidden])
            dx_ref[0, :, rows] = (d_x + nt(d_logits, router_ref[rows, :])).astype(BF)

    @pl.when(slot == 0)
    def _():
        results(out_mine, dx_mine)

    @pl.when(slot == 1)
    def _():
        results(out_other, dx_other)


def expert_rows(members, x_pieces, ym_pieces, held, base, router, parts, targets, units, shared):
    low, count = members[0], len(members)
    width = router.shape[0]
    x_pieces = [item if isinstance(item, tuple) else (item,) for item in x_pieces]
    ym_pieces = [item if isinstance(item, tuple) else (item,) for item in ym_pieces]
    tile = sum(part.shape[0] for part in x_pieces[0])
    counts = [len(item) for item in x_pieces]
    rows = 2 * GROUP * tile
    steps = 2 * count
    own = EXPERTS // GROUP
    hidden = own * units + shared

    def like(columns):
        spec = pl.BlockSpec((tile, columns), lambda i: (i + 2 * low, 0))
        return jax.ShapeDtypeStruct((rows, columns), BF), spec

    result = (
        jax.ShapeDtypeStruct((count, tile, width), BF),
        pl.BlockSpec((1, tile, width), lambda i: (i // 2, 0, 0)),
    )
    outs = [like(width), like(width), like(2 * hidden + LANES), like(hidden)] + [result] * 4
    any_ref = pl.BlockSpec(memory_space=pl.ANY)
    flat = [part for item in x_pieces + ym_pieces for part in item]
    args = [targets, base, *flat, router, *parts, *held]
    specs = [pl.BlockSpec(memory_space=pltpu.SMEM)] * 2 + [any_ref] * len(flat)
    specs += [pl.BlockSpec(router.shape, lambda i: (0, 0))]
    specs += [any_ref] * (len(parts) + len(held))
    aliases = {len(args) - len(held) + i: i for i in range(len(held))}
    done = pl.pallas_call(
        functools.partial(
            expert_body, (own, units, shared, counts, len(parts), len(held))
        ),
        grid=(steps,),
        out_shape=tuple(shape for shape, _ in outs),
        in_specs=specs,
        out_specs=tuple(spec for _, spec in outs),
        scratch_shapes=[
            pltpu.VMEM((width, 3 * hidden), BF), pltpu.SemaphoreType.DMA((targets.shape[0],)),
            pltpu.VMEM((2, tile, width), BF), pltpu.VMEM((2, tile, width + LANES), BF),
            pltpu.SemaphoreType.DMA((2, 2, 2)),
        ],
        input_output_aliases=aliases,
        compiler_params=pltpu.CompilerParams(
            dimension_semantics=("arbitrary",), vmem_limit_bytes=VMEM
        ),
        cost_estimate=SMALL,
        name="expert_rows",
    )(*args)
    return list(done[:4]), list(done[4:])


def shards(
    tokens, routes, gain_in, w_zx, w_dt, w_bc, conv_w, conv_b, dt_bias, a_log, d_skip, norm_gain,
    w_out, gain_mid, router, shared_gu, shared_down, expert_gu, expert_down, grad_out,
):
    core = lax.axis_index("tensor")
    me = lax.axis_index("dp")
    lines = lax.axis_size("dp") // GROUP
    line, place = me // GROUP, lax.rem(me, GROUP)
    piece, width_d = tokens.shape
    local = w_zx.shape[2]
    heads = w_dt.shape[1]
    units = expert_gu.shape[3]
    own = EXPERTS // GROUP
    inner_all = norm_gain.shape[0]
    height = w_zx.shape[0]
    cut_in, cut_gate = 2 * local // 3, local // 2
    third = (lines - 1 + 2) // 3
    place_now = place.reshape(1)
    where = jnp.stack([place, line]).astype(jnp.int32)
    base = (heads + own * place).reshape(1)
    tiles = 4
    mine_last = (tiles // 2 * (1 - core)).reshape(1).astype(jnp.int32)

    lines_back = lax.rem(line - jnp.arange(lines, dtype=jnp.int32) + lines, lines)
    members = place ^ jnp.arange(GROUP, dtype=jnp.int32)
    pieces = jnp.concatenate([members, members[3:]])
    mixer_targets = (pieces[:, None] + GROUP * lines_back[None, :]).reshape(-1)
    expert_targets = (members[None, :] + GROUP * lines_back[:, None]).reshape(-1)
    order = Order()

    core_now = core.reshape(1)
    gain_in, gain_mid = gain_in[None], gain_mid[None]
    joint = jnp.concatenate([w_bc, router], axis=1)
    joint_came = swap(joint)
    ring_a = [w_zx[:, 1, :cut_in]]
    tokens_other = swap(tokens)
    order.set(ring_a[0], joint)
    joint = in_order(joint, order(joint_came), core)
    bc_cols, router_cols = joint[:, : 2 * NS], joint[:, 2 * NS :]
    pad = jnp.zeros((height, LANES - heads - EXPERTS), BF)
    ring_b = [jnp.concatenate([w_zx[:, 1, cut_in:], w_dt, router_cols, pad, bc_cols], axis=1)]
    order.set(
        ring_b[0], gain_in, gain_mid, where, base, mine_last, place_now, core_now, mixer_targets,
        expert_targets,
    )
    shared_units = shared_gu.shape[2] // GROUP
    hidden = own * units + shared_units
    gu = order(expert_gu).reshape(GROUP, own, height, 2, units).transpose(0, 2, 3, 1, 4)
    gu = gu.reshape(GROUP, height, 2, own * units)
    order.set(gu)
    ring_on(ring_a, order, 1, 1 + third, lines)
    ring_on(ring_b, order, 1, 1 + third, lines)
    order.set(ring_a[-1], ring_b[-1])
    down = order(expert_down).reshape(GROUP, own, units, height).transpose(0, 3, 1, 2)
    down = down.reshape(GROUP, height, own * units)
    sgu = order(shared_gu).reshape(height, 2, GROUP, shared_units).transpose(2, 0, 1, 3)
    sdown = order(shared_down).reshape(GROUP, shared_units, height).transpose(0, 2, 1)
    order.set(down, sgu, sdown)
    ring_on(ring_a, order, 1 + third, 1 + 2 * third, lines)
    ring_on(ring_b, order, 1 + third, 1 + 2 * third, lines)
    order.set(ring_a[-1], ring_b[-1])
    gu, sgu, down, sdown = order((gu, sgu, down, sdown))
    packed = jnp.concatenate([gu[:, :, 0], sgu[:, :, 0], gu[:, :, 1], sgu[:, :, 1], down, sdown], axis=2)
    to_send = [pick(packed, members[k]) for k in range(GROUP)]
    order.set(*to_send)
    came = to_send[:1] + [hop(to_send[k], k) for k in range(1, GROUP)]
    lane = jnp.arange(LANES, dtype=jnp.int32)
    cut = functools.partial(lax.dynamic_slice_in_dim, start_index=core * local, slice_size=local)
    cut_heads = functools.partial(lax.dynamic_slice_in_dim, start_index=core * heads, slice_size=heads)
    conv_w, conv_b, norm_gain, routes = order((conv_w, conv_b, norm_gain, routes))
    conv_all = jnp.concatenate([conv_w, conv_b[None]])
    kern = jnp.concatenate(
        [cut(conv_all, axis=1), jnp.zeros((5, LANES), F32), conv_all[:, inner_all:]], axis=1
    )
    tail = jnp.zeros((1, kern.shape[1] - local), F32)
    skip_wide = jnp.repeat(cut_heads(d_skip, axis=0), P_SIZE)[None]
    kern = jnp.concatenate(
        [
            kern,
            jnp.concatenate([skip_wide, tail], axis=1),
            jnp.concatenate([cut(norm_gain, axis=0)[None], tail], axis=1),
            jnp.zeros((1, kern.shape[1]), F32),
        ]
    )
    head_par = jnp.pad(
        jnp.stack([cut_heads(dt_bias, axis=0), jnp.exp(cut_heads(a_log, axis=0))]),
        ((0, 6), (0, LANES - heads)),
    )
    head_of = jnp.arange(local, dtype=jnp.int32) // P_SIZE
    spread = (lax.rem(lane, LANES // 2)[:, None] == head_of[None, :]).astype(BF)
    own_routes = lax.dynamic_slice_in_dim(routes, core * piece, piece, 0)
    go_ring = [order(jnp.concatenate([w_zx[:, 0], w_out.T], axis=1))]
    order.set(kern, head_par, spread, own_routes, go_ring[0])
    ring_on(ring_a, order, 1 + 2 * third, lines, lines)
    ring_on(ring_b, order, 1 + 2 * third, lines, lines)
    order.set(ring_a[-1], ring_b[-1])

    def matrix(parts, cut_at):
        return pieces_of(parts, mixer_targets, cut_at)

    def along_both(stacked):
        return [stacked, hop(stacked, 1), hop(stacked, 2)]

    def across_halves(parts, cut_at):
        width = parts[0].shape[2]
        low, high = cut_columns(parts[1], 0, cut_at), cut_columns(parts[2], cut_at, width - cut_at)
        order.set(low, high)
        return parts + [hop(low, 2), hop(high, 1)]

    tokens_other = order.take(tokens_other)
    in_stack = stack_pairs(ring_a, ring_b)
    marked = marked_rows(order(grad_out), own_routes, heads)
    order.set(in_stack, marked)
    ring_on(go_ring, order, 1, 1 + third, lines)
    order.set(go_ring[-1])
    in_w = along_both(order(in_stack))
    came = order.take(*came)
    expert_ring = [stack_columns(came, 0, 3 * hidden)]
    normed = normed_rows(order(tokens), tokens_other, gain_in, core_now)
    order.set(normed, expert_ring[0])
    ring_on(go_ring, order, 1 + third, 1 + 2 * third, lines)
    order.set(go_ring[-1])
    marked_other = swap(order(marked))
    in_w = list(order.take(*in_w))
    marked_other = order.take(marked_other)
    in_w = across_halves(in_w, cut_in)
    ring_on(go_ring, order, 1 + 2 * third, lines, lines)
    order.set(go_ring[-1])
    gate_stack = stack_columns(go_ring, 0, local)
    expert_ring[0] = order(expert_ring[0])
    in_w = order.take(*in_w, gate_stack)
    gate_stack, in_w = in_w[-1], list(in_w[:-1])

    gate_w = along_both(gate_stack)
    in_matrix = matrix(in_w, cut_in)
    zi, router_w = inner_product(order(normed), in_matrix, local)
    y, states = front_scan(zi, kern, head_par, spread)
    order.set(y)
    gate_w = list(order.take(*gate_w))
    gate_w = across_halves(gate_w, cut_gate)
    out_stack = stack_columns(order(go_ring), local, width_d)
    order.set(out_stack)
    ring_on(expert_ring, order, 1, 1 + third, lines)
    order.set(expert_ring[-1])
    gate_w = list(order.take(*gate_w))
    out_w = along_both(order(out_stack))
    gate_matrix = matrix(gate_w, cut_gate)
    gate, squares = gate_product(order(normed), y, gate_matrix)
    order.set(gate)
    squares_other = order.take(swap(squares))
    out_w = list(order.take(*out_w))
    out_w = across_halves(out_w, cut_gate)
    out_w = list(order.take(*out_w))
    ring_on(expert_ring, order, 1 + third, 1 + 2 * third, lines)
    order.set(expert_ring[-1])
    marked_sent = order(marked)
    marked_x, marked_y = hop(marked_sent, 1), hop(marked_sent, 2)
    out_matrix = matrix(out_w, cut_gate)
    scaled, mixed_sent, mixed_mine = mixed_product(
        order(y), gate, squares, squares_other, kern, out_matrix, mine_last, inner_all
    )
    order.set(mixed_mine)
    marked_x, marked_y = order.take(marked_x, marked_y)
    half_rows = piece // 2

    def halves_of(from_x, from_y):
        return cut_rows_of(from_x, 0, half_rows), cut_rows_of(from_y, half_rows, half_rows)

    def across(halves):
        return hop(halves[0], 2), hop(halves[1], 1)

    marked_halves = halves_of(marked_x, marked_y)
    order.set(*marked_halves)
    ring_on(expert_ring, order, 1 + 2 * third, lines, lines)
    order.set(expert_ring[-1])
    mixed_came = order.take(swap(order(mixed_sent)))
    resid, mid = mid_rows_of(mixed_mine, mixed_came, tokens, gain_mid)
    order.set(mid)

    mid_x, mid_y = hop(mid, 1), hop(mid, 2)
    mid_other = order.take(swap(mid))
    marked_swap_x, marked_swap_y = swap(order(marked_x)), swap(order(marked_y))
    parts, _, expert_order = pieces_of(expert_ring, expert_targets, 0)
    common = (base, router_w, parts, expert_order, units, shared_units)
    kept, result_0 = expert_rows(
        [0], [order(mid), mid_other], [marked, marked_other], [], *common
    )
    order.set(result_0[0])
    mid_x, mid_y, marked_swap_x, marked_swap_y = order.take(
        mid_x, mid_y, marked_swap_x, marked_swap_y
    )
    mid_swap_x, mid_swap_y = order.take(swap(mid_x), swap(mid_y))
    mid_halves = halves_of(mid_x, mid_y)
    order.set(*mid_halves, mid_swap_x, mid_swap_y)
    mid_d, marked_d = across(order(mid_halves)), across(order(marked_halves))
    kept, result = expert_rows(
        [1, 2], order([mid_x, mid_swap_x, mid_y, mid_swap_y]),
        [marked_x, marked_swap_x, marked_y, marked_swap_y], kept, *common,
    )
    order.set(result[0])
    mid_d = order.take(*mid_d)
    marked_d = order.take(*marked_d)
    mid_d_other = order.take(*[swap(item) for item in mid_d])
    marked_d_other = order.take(*[swap(item) for item in marked_d])
    d_others, d_other_0 = swap(order(result[3])), swap(order(result_0[3]))
    kept, result_3 = expert_rows(
        [3], [order(mid_d), mid_d_other], [marked_d, marked_d_other], kept, *common
    )
    order.set(result_3[0])
    x_all, dy_all, gu, down = kept
    d_others, d_other_0 = order.take(d_others, d_other_0)
    d_other_3 = order.take(swap(result_3[3]))
    over_low, over_high = across_sum(result_3[2], d_other_3, 0)
    order.set(over_low)
    d_over = hop(over_low, 1), hop(over_high, 2)
    out_others = swap(order(result_3[1])), swap(order(result[1])), swap(order(result_0[1]))

    grad_down = tn(order(dy_all), down, BF)
    order.set(grad_down)
    d_over = order.take(*d_over)
    out_other_3, out_others, out_other_0 = order.take(*out_others)
    to_x, to_y = side_sums(result[2], d_others, *d_over)
    order.set(to_x)
    arrays = {}

    def whole_block(name, width):
        return lambda line_at: [(width, [(arrays[name], 0, line_at)], None)]

    sums = LineSums(
        {"gu": whole_block("gu", 2 * hidden), "down": whole_block("down", hidden)},
        order, lines, GROUP * height, where,
    )
    arrays["down"] = grad_down
    arrays["gu"] = None
    sums.start("down")
    d_came = hop(to_x, 1), hop(to_y, 2)
    out_over = across_sum(result_3[0], order(out_other_3), 0)
    order.set(out_over[0], sums.sent)
    out_over = hop(out_over[0], 1), hop(out_over[1], 2)
    grad_gu = tn(order(x_all), gu, BF)
    order.set(grad_gu)
    arrays["gu"] = grad_gu
    sums.run(third, "gu")
    order.set(sums.sent)
    d_came = order.take(*d_came)
    out_over = order.take(*out_over)
    out_sums = side_sums(result[0], out_others, *out_over)
    order.set(out_sums[0])
    out_came = hop(out_sums[0], 1), hop(out_sums[1], 2)

    d_resid, d_mix_mine, pulls, mid_gains = resid_back(
        result_0[2], d_other_0, *d_came, order(resid), tokens, grad_out, gain_mid
    )
    order.set(d_mix_mine)
    d_mix_came, pulls_came = order.take(swap(d_mix_mine), swap(pulls))
    d_mix, pulls = pair_rows([(d_mix_mine, order(d_mix_came)), (pulls, pulls_came)], core_now)
    order.set(d_mix)
    d_y, dz_a, dz_b, gain_grads = gate_back(
        order(d_mix), y, gate, squares, squares_other, pulls, kern, out_matrix, cut_gate, inner_all
    )
    order.set(d_y)
    out_came = order.take(*out_came)

    def hop_first(pair):
        sent = [item.start(order) for item in pair]
        order.set(*sent)
        for item, values in zip(pair, sent):
            item.came = hop(values, item.bits)

    def hop_second(pair):
        for item in pair:
            item.came = order(item.came)
        sent = [item.turn() for item in pair]
        order.set(*sent)
        for item, values in zip(pair, sent):
            item.came_last = hop(values, 3 - item.bits)

    def all_came(pair):
        for item in pair:
            item.came_last = order(item.came_last)
        order.set(*[item.came_last for item in pair])

    grad_out_w = tn(order(d_mix), scaled, BF)
    normed_now = order(normed)
    grad_gate_a, grad_gate_b = tn(normed_now, dz_a, BF), tn(normed_now, dz_b, BF)
    order.set(grad_gate_a, grad_gate_b, grad_out_w)
    og_pair = [
        Plane([(grad_out_w, 0, cut_gate), (grad_gate_a, 0, cut_gate)], 1, where, lines),
        Plane([(grad_out_w, 1, cut_gate), (grad_gate_b, 0, cut_gate)], 2, where, lines),
    ]
    hop_first(og_pair)
    sums.run(third)
    order.set(sums.sent)
    di_a, di_b, par_grads, head_grads = back_scan(
        order(d_y), zi, states, kern, head_par, spread, cut_in
    )
    order.set(di_a)
    hop_second(og_pair)
    grad_in_a = tn(order(normed), di_a, BF)
    start = local - cut_in
    grad_router = jnp.pad(
        order(grad_gu[:, 2 * hidden :]).astype(F32),
        ((0, 0), (start, di_b.shape[1] - start - LANES)),
    )
    grad_in_b = (tn(order(normed), di_b) + grad_router).astype(BF)
    order.set(grad_in_a, grad_in_b)
    sums.run(third)
    order.set(sums.sent)
    all_came(og_pair)
    in_pair = [
        Plane([(grad_in_a, 0, cut_in)], 1, where, lines),
        Plane([(grad_in_b, 0, grad_in_b.shape[1])], 2, where, lines),
    ]
    hop_first(in_pair)
    d_sent, d_mine = normed_back(
        order([dz_a, dz_b, di_a, di_b]), [gate_matrix, in_matrix], mine_last
    )
    order.set(d_mine)

    def pair_groups(pair):
        return lambda line_at: [group for item in pair for group in item.groups(line_at)]

    rest = LineSums(
        {"og": pair_groups(og_pair), "in": pair_groups(in_pair)}, order, lines, height, where
    )
    hop_second(in_pair)
    sums.run(third)
    order.set(sums.final["gu"])
    rest.start("og")
    order.set(rest.sent)
    to_send = member_pieces(sums.final["gu"], sums.final["down"], where, height)
    order.set(*to_send)
    all_came(in_pair)
    came = to_send[:1] + [hop(order(to_send[k]), k) for k in range(1, GROUP)]
    rest.run(third)
    order.set(rest.sent)
    d_other = order.take(swap(order(d_sent)))
    grad_tokens, in_gains = tokens_back(d_mine, d_other, tokens, d_resid, gain_in)
    order.set(grad_tokens)
    small = pack_small(
        par_grads, head_grads, gain_grads, mid_gains, in_gains, spread, core_now, local, heads
    )
    order.set(small)
    rest.run(third, "in")
    order.set(rest.sent)
    small = order.take(small + order(swap(small)))
    output = output_rows(order(result_0[0]), out_other_0, *out_came, resid)
    order.set(output)
    small = order.take(small + order(hop(small, 1)))
    rest.run(third)
    order.set(rest.sent)
    came = list(order.take(*came))
    g_egu, g_edown, g_sgu, g_sdown = unpack_experts(came, place_now, units, shared_units)
    order.set(g_edown)
    rest.run(third)
    order.set(rest.sent)
    bits = 2
    while bits < lines * GROUP:
        small = order.take(small + order(hop(small, bits)))
        bits *= 2
    rest.run(third)
    og_held, g_inner = rest.final["og"], rest.final["in"]
    quarters = [og_held[:, i * cut_gate : (i + 1) * cut_gate] for i in range(4)]
    g_out = jnp.concatenate([quarters[0], quarters[2]], axis=1).T
    g_gate = jnp.concatenate([quarters[1], quarters[3]], axis=1)
    g_zx = jnp.stack([g_gate, g_inner[:, :local]], axis=1)
    g_dt = g_inner[:, local : local + heads]
    g_joint = jnp.concatenate(
        [g_inner[:, local + heads : local + heads + EXPERTS], g_inner[:, local + LANES :]], axis=1
    )
    joint_rows = height // 2
    g_joint = lax.dynamic_slice_in_dim(g_joint, core * joint_rows, joint_rows, 0) + swap(
        lax.dynamic_slice_in_dim(g_joint, (1 - core) * joint_rows, joint_rows, 0)
    )

    def of_heads(number):
        return jnp.concatenate(
            [
                small[7, (2 * number + which) * LANES : (2 * number + which) * LANES + heads]
                for which in range(2)
            ]
        )

    return (
        output, grad_tokens, small[6, :width_d], g_zx, g_dt, g_joint[:, EXPERTS:], small[:4],
        small[4], of_heads(0), of_heads(1), of_heads(2), small[5, :inner_all], g_out,
        small[6, width_d : 2 * width_d], g_joint[:, :EXPERTS], g_sgu, g_sdown, g_egu, g_edown,
    )


def solution(mesh):
    both = P(("dp", "tensor"), None)
    rows = P("dp", None, "tensor")
    cols = P("tensor", "dp")
    return jax.shard_map(
        shards,
        mesh=mesh,
        in_specs=(
            both, P("dp", None), P(), rows, P("dp", "tensor"), both, P(), P(), P(), P(), P(), P(),
            cols, P(), both, rows, cols, P(None, "dp", None, "tensor"), P(None, "tensor", "dp"),
            both,
        ),
        out_specs=(
            both, both, P(), rows, P("dp", "tensor"), both, P(), P(), P(), P(), P(), P(),
            cols, P(), both, rows, cols, P(None, "dp", None, "tensor"), P(None, "tensor", "dp"),
        ),
        check_vma=False,
    )
```

time: 1390 us -> 970 us (0.70)
  waiting for transfers between devices: 550 us -> 217 us
  Pallas kernels: 269 us -> 486 us
  other arithmetic: 137 us -> 10.2 us
  local copies, waits for them, and re-layouts: 160 us -> 51.1 us
  matrix products: 154 us -> 92.8 us
    ppermute x27 -> x21, waiting for transfers between devices: 292 us -> 42.7 us  [next_line(): lax.ppermute(values, 'dp', [(i, (i + GROUP) % count) for i in range(count)])]
    pallas_call x8 -> x57, Pallas kernels: 189 us -> 413 us  [the longest x3 151 us: expert_rows(): pl.pallas_call(functools.partial(expert_body, (own, units, shared, counts...]
    ppermute x44 -> x46, waiting for transfers between devices: 257 us -> 148 us  [hop(): return lax.ppermute(values, 'dp', [(i, i ^ bits) for i in range(count)])]
    dot_general x6 -> x0, matrix products: 60 us -> none  [the longest x3 37.3 us: nn(): lax.dot_general(left, right, (((1,), (0,)), ((), ())), preferred_element_...]
    unnamed x217 -> x163, local copies, waits for them, and re-layouts: 57.9 us -> 29.9 us
    concatenate x25 -> x5, other arithmetic: 32 us -> 4.29 us  [the longest x1 1.82 us: shards(): go_ring = [order(jnp.concatenate([w_zx[:, 0], w_out.T], axis=1))]]
    another operation x21 -> x1, other arithmetic: 27.1 us -> 0.58 us  [shards(): where = jnp.stack([place, line]).astype(jnp.int32)]
    ppermute x25, waiting for transfers between devices: 0.29 us -> 26.1 us  [swap(): return lax.ppermute(values, 'tensor', [(0, 1), (1, 0)])]
  transfers between devices with their start and end apart: 96 -> 92, of which waited for: 39 -> 40; matrix products, arithmetic and copies ran while one was open for 32% -> 13% of each run, Pallas kernels for 20% -> 47%
where the time goes in v2:
time: 970 us; the launch traced here: 959 us
  Pallas kernels  486 us (50%)
  waiting for transfers between devices  217 us (22%)
  matrix products  92.8 us (10%)
  starting transfers between devices  91.9 us (9%)
  local copies, waits for them, and re-layouts  51.1 us (5%)
  other arithmetic  10.2 us (1%)
  between operations  10.1 us (1%)
    pallas_call x3, Pallas kernels, expert_rows(): pl.pallas_call(functools.partial(expert_body, (own, units, shared, counts...  151 us
    ppermute x46, waiting for transfers between devices, hop(): return lax.ppermute(values, 'dp', [(i, i ^ bits) for i in range(count)])  148 us
    dot_general x7, matrix products, tn(): lax.dot_general(left, right, (((0,), (0,)), ((), ())), preferred_element_...  92.8 us
    pallas_call x21, Pallas kernels, add_blocks(): pl.pallas_call(body, out_shape=jax.ShapeDtypeStruct((count * height, tota...  83 us
    pallas_call x5, Pallas kernels, gathered_call(): pl.pallas_call(whole, grid_spec=pltpu.PrefetchScalarGridSpec(num_scalar_p...  80.8 us
    pallas_call x1, Pallas kernels, back_scan(): pl.pallas_call(back_body, grid=(steps,), out_shape=(jax.ShapeDtypeStruct(...  51.8 us
    pallas_call x17, Pallas kernels, small_call(): pl.pallas_call(body, out_shape=tuple((jax.ShapeDtypeStruct(shape, kind) f...  44.7 us
    ppermute x21, waiting for transfers between devices, next_line(): lax.ppermute(values, 'dp', [(i, (i + GROUP) % count) for i in range(count)])  42.7 us
  transfers between devices with their start and end apart: 92, of which 40 were waited for; matrix products, arithmetic and copies ran while one was open for 13% of the time, Pallas kernels for 47%

profile of v2, /device:TPU:1, one launch (start us, length us, event | category | flops | bytes accessed | tf_op | source)
XLA Modules:
  0.0 959.0 jit_solution(17138342929550582361)
XLA Ops:
  35.6 6.4 collective-permute-done.4.refs_6_
  65.8 8.9 collective-permute-done.6.refs_2_
  82.8 6.0 collective-permute-start.18
  91.3 31.4 %collective-permute-done.12.values_ref.refs_4_.refs_12_ = bf16[4,96,1920]{2,1,0:T(8,128)(2,1)S(1)} collective-permute-done((bf16[4,96,1920]{2,1,0:T(8,128)(2,1)S(1)}, bf16[4,96,1920]{2,1,0:T(8,128)(2,1)S(1)}, u32[]{:S(2)}, u32[]{:S(2)}) %collective-permute-start.12) | collective-permute-done | bytes 1474592 | tf_op jit(solution)/shard_map/ppermute | solution.py:39
  133.8 12.9 %collective-permute-done.16.refs_7_.refs_15_ = bf16[4,96,896]{2,1,0:T(8,128)(2,1)S(1)} collective-permute-done((bf16[4,96,896]{2,1,0:T(8,128)(2,1)}, bf16[4,96,896]{2,1,0:T(8,128)(2,1)S(1)}, u32[]{:S(2)}, u32[]{:S(2)}) %collective-permute-start.16) | collective-permute-done | bytes 688160 | tf_op jit(solution)/shard_map/ppermute | solution.py:39
  149.1 13.5 %inner_product.1 = (f32[1024,1920]{1,0:T(8,128)}, bf16[1536,128]{1,0:T(8,128)(2,1)}) custom-call(s32[20]{0:T(128)} %add.125.refs_0_, s32[1]{0:T(128)} %constant.88.clone.refs_1_, bf16[1024,1536]{1,0:T(8,128)(2,1)} %bitcast.97, bf16[4,96,1920]{2,1,0:T(8,128)(2,1)} %stack_pairs.1.refs_3_.refs_11_, bf16[4,96,1920]{2,1,0:T(8,128)(2,1)} %copy-done.10, ...), custom_call_target="tpu_custom_call" | custom-call | flops 1000 | bytes 1000 | tf_op jit(solution)/shard_map/inner_product/pallas_call | solution.py:751
  162.6 21.7 %front_scan.1 = (f32[1024,1536]{1,0:T(8,128)}, f32[8,128,1536]{2,1,0:T(8,128)}) custom-call(f32[1024,1920]{1,0:T(8,128)} %get-tuple-element.313.zi_ref.prev_ref, f32[8,1920]{1,0:T(8,128)} %fusion.3.kern_ref.refs_6_.refs_8_, f32[8,128]{1,0:T(8,128)} %select_maximum_fusion.3.head_ref, bf16[128,1536]{1,0:T(8,128)(2,1)} %compare_convert_fusion.spread_ref), custom_call_target="tpu_custom_call" | custom-call | flops 1000 | bytes 1000 | tf_op jit(solution)/shard_map/front_scan/pallas_call | solution.py:221
  194.6 10.1 %collective-permute-done.23.refs_7_.refs_9_ = bf16[4,96,768]{2,1,0:T(8,128)(2,1)S(1)} collective-permute-done((bf16[4,96,768]{2,1,0:T(8,128)(2,1)S(1)}, bf16[4,96,768]{2,1,0:T(8,128)(2,1)S(1)}, u32[]{:S(2)}, u32[]{:S(2)}) %collective-permute-start.23) | collective-permute-done | bytes 589856 | tf_op jit(solution)/shard_map/ppermute | solution.py:39
  208.4 13.2 %gate_product.1 = (f32[1024,1536]{1,0:T(8,128)}, f32[1024,128]{1,0:T(8,128)}) custom-call(s32[20]{0:T(128)} %add.125.refs_0_, s32[1]{0:T(128)} %constant.88.clone.refs_1_, bf16[1024,1536]{1,0:T(8,128)(2,1)} %bitcast.98, f32[1024,1536]{1,0:T(8,128)} %get-tuple-element.343.refs_3_.refs_2_, bf16[4,96,1536]{2,1,0:T(8,128)(2,1)} %stack_columns.4.refs_4_.refs_6_, ...), custom_call_target="tpu_custom_call" | custom-call | flops 1000 | bytes 1000 | tf_op jit(solution)/shard_map/gate_product/pallas_call | solution.py:751
  237.4 6.6 collective-permute-done.28.refs_10_.refs_12_
  252.8 15.6 %mixed_product.1 = (bf16[1024,1536]{1,0:T(8,128)(2,1)}, f32[512,1536]{1,0:T(8,128)}, f32[512,1536]{1,0:T(8,128)}) custom-call(s32[20]{0:T(128)} %add.125.refs_0_, s32[1]{0:T(128)} %bitcast.1.refs_1_, f32[1024,1536]{1,0:T(8,128)} %get-tuple-element.343.refs_3_.refs_2_, f32[1024,1536]{1,0:T(8,128)} %get-tuple-element.332.refs_3_.refs_4_, ...), custom_call_target="tpu_custom_call" | custom-call | flops 1000 | bytes 1000 | tf_op jit(solution)/shard_map/mixed_product/pallas_call | solution.py:751
  268.5 18.3 %collective-permute-done.31.values_ref.refs_6_ = bf16[512,1664]{1,0:T(8,128)(2,1)} collective-permute-done((bf16[512,1664]{1,0:T(8,128)(2,1)}, bf16[512,1664]{1,0:T(8,128)(2,1)}, u32[]{:S(2)}, u32[]{:S(2)}) %collective-permute-start.31) | collective-permute-done | bytes 1703968 | tf_op jit(solution)/shard_map/ppermute | solution.py:39
  292.7 15.9 %collective-permute-done.30.refs_10_.refs_14_ = bf16[4,96,3456]{2,1,0:T(8,128)(2,1)} collective-permute-done((bf16[4,96,3456]{2,1,0:T(8,128)(2,1)S(1)}, bf16[4,96,3456]{2,1,0:T(8,128)(2,1)}, u32[]{:S(2)}, u32[]{:S(2)}) %collective-permute-start.30) | collective-permute-done | bytes 2654240 | tf_op jit(solution)/shard_map/ppermute | solution.py:44
  320.3 5.6 mid_rows.1
  332.2 37.7 %expert_rows.3 = (bf16[4096,1536]{1,0:T(8,128)(2,1)}, bf16[4096,1536]{1,0:T(8,128)(2,1)}, bf16[4096,2432]{1,0:T(8,128)(2,1)}, bf16[4096,1152]{1,0:T(8,128)(2,1)}...) custom-call(s32[16]{0:T(128)} %add.120.refs_0_, ...), custom_call_target="tpu_custom_call" | custom-call | flops 1000 | bytes 1000 | tf_op jit(solution)/shard_map/expert_rows/pallas_call | solution.py:1323
  379.3 74.8 %expert_rows.4 = (bf16[4096,1536]{1,0:T(8,128)(2,1)}, bf16[4096,1536]{1,0:T(8,128)(2,1)}, bf16[4096,2432]{1,0:T(8,128)(2,1)}, bf16[4096,1152]{1,0:T(8,128)(2,1)}...) custom-call(s32[16]{0:T(128)} %add.120.refs_0_, ...), custom_call_target="tpu_custom_call", output_to_operand_aliasing={{0}: (15, {}), {1}: (16, {}), {2}: (17, {}), {3}: (18, {})} | custom-call | flops 1000 | bytes 1000 | tf_op jit(solution)/shard_map/expert_rows/pallas_call | solution.py:1323
  465.0 38.3 %expert_rows.5 = (bf16[4096,1536]{1,0:T(8,128)(2,1)}, bf16[4096,1536]{1,0:T(8,128)(2,1)}, bf16[4096,2432]{1,0:T(8,128)(2,1)}, bf16[4096,1152]{1,0:T(8,128)(2,1)}...) custom-call(s32[16]{0:T(128)} %add.120.refs_0_, ...), custom_call_target="tpu_custom_call", output_to_operand_aliasing={{0}: (15, {}), {1}: (16, {}), {2}: (17, {}), {3}: (18, {})} | custom-call | flops 1000 | bytes 1000 | tf_op jit(solution)/shard_map/expert_rows/pallas_call | solution.py:1323
  512.7 23.0 %fusion.15.refs_0_ = bf16[1536,1152]{1,0:T(8,128)(2,1)} fusion(bf16[4096,1536]{1,0:T(8,128)(2,1)} %get-tuple-element.407, bf16[4096,1152]{1,0:T(8,128)(2,1)} %get-tuple-element.408), kind=kOutput, calls=%fused_computation.84 | convolution fusion | flops 14495514624 | bytes 25559040 | tf_op jit(solution)/shard_map/dot_general | solution.py:34
  549.3 40.7 %fusion.16.refs_1_.refs_0_ = bf16[1536,2432]{1,0:T(8,128)(2,1)} fusion(bf16[4096,1536]{1,0:T(8,128)(2,1)} %get-tuple-element.425, bf16[4096,2432]{1,0:T(8,128)(2,1)} %get-tuple-element.426), kind=kOutput, calls=%fused_computation.85 | convolution fusion | flops 30601641984 | bytes 39976960 | tf_op jit(solution)/shard_map/dot_general | solution.py:34
  602.4 8.7 resid_back.1
  621.7 17.5 %gate_back.1 = (f32[1024,1536]{1,0:T(8,128)}, bf16[1024,768]{1,0:T(8,128)(2,1)}, bf16[1024,768]{1,0:T(8,128)(2,1)}, f32[8,1536]{1,0:T(8,128)}) custom-call(s32[20]{0:T(128)} %add.125.refs_0_, s32[1]{0:T(128)} %constant.88.clone.refs_1_, bf16[1024,1536]{1,0:T(8,128)(2,1)} %bitcast.103, f32[1024,1536]{1,0:T(8,128)} %get-tuple-element.343.refs_3_.refs_2_, ...), custom_call_target="tpu_custom_call" | custom-call | flops 1000 | bytes 1000 | tf_op jit(solution)/shard_map/gate_back/pallas_call | solution.py:751
  639.3 9.3 collective-permute-done.65.x_ref
  658.2 6.9 fusion.17.refs_0_.refs_6_
  675.3 5.7 line_step.15
  681.1 51.8 %back_scan.1 = (bf16[1024,1024]{1,0:T(8,128)(2,1)}, bf16[1024,896]{1,0:T(8,128)(2,1)}, f32[8,1920]{1,0:T(8,128)}, f32[8,128]{1,0:T(8,128)}) custom-call(f32[1024,1536]{1,0:T(8,128)} %get-tuple-element.457.dy_ref, f32[1024,1920]{1,0:T(8,128)} %get-tuple-element.313.zi_ref.prev_ref, f32[1024,1920]{1,0:T(8,128)} %get-tuple-element.313.zi_ref.prev_ref, ...), custom_call_target="tpu_custom_call" | custom-call | flops 1000 | bytes 1000 | tf_op jit(solution)/shard_map/back_scan/pallas_call | solution.py:388
  743.9 7.6 add_convert_fusion.refs_0_.refs_15_.refs_3_
  761.5 7.0 collective-permute-done.69.refs_2_.refs_5_
  777.6 21.0 %normed_back.1 = (f32[512,1536]{1,0:T(8,128)}, f32[512,1536]{1,0:T(8,128)}) custom-call(s32[20]{0:T(128)} %add.125.refs_0_, s32[1]{0:T(128)} %bitcast.1.refs_1_, bf16[1024,768]{1,0:T(8,128)(2,1)} %get-tuple-element.474.refs_2_, bf16[1024,768]{1,0:T(8,128)(2,1)} %get-tuple-element.475.refs_3_, bf16[1024,1024]{1,0:T(8,128)(2,1)} %get-tuple-element.476.refs_4_, ...), custom_call_target="tpu_custom_call" | custom-call | flops 1000 | bytes 1000 | tf_op jit(solution)/shard_map/normed_back/pallas_call | solution.py:751
  798.6 8.4 collective-permute-done.73.refs_1_.refs_13_
  848.5 6.8 tokens_back.1
  876.1 21.6 %collective-permute-done.81 = f32[8,3328]{1,0:T(8,128)S(1)} collective-permute-done((f32[8,3328]{1,0:T(8,128)S(1)}, f32[8,3328]{1,0:T(8,128)S(1)}, u32[]{:S(2)}, u32[]{:S(2)}) %collective-permute-start.81) | collective-permute-done | bytes 106528 | tf_op jit(solution)/shard_map/ppermute | solution.py:39
  943.6 10.8 %collective-permute-start.91 = (f32[48,272]{1,0:T(8,128)S(1)}, f32[48,272]{1,0:T(8,128)S(1)}, u32[]{:S(2)}, u32[]{:S(2)}) collective-permute-start(f32[48,272]{1,0:T(8,128)S(1)} %fusion), channel_id=1, source_target_pairs={{0,1},{1,0},{2,3},{3,2},{4,5},{5,4},{6,7},{7,6},{8,9},{9,8},{10,11... | collective-permute-start | bytes 156680 | tf_op jit(solution)/shard_map/ppermute | solution.py:48
  (453 shorter events, 365.3 us)
Async XLA Ops:
  6.8 51.8 %collective-permute-start.11 = (bf16[512,1536]{1,0:T(8,128)(2,1)}, bf16[512,1536]{1,0:T(8,128)(2,1)}, u32[]{:S(2)}, u32[]{:S(2)}) collective-permute-start(bf16[512,1536]{1,0:T(8,128)(2,1)} %tokens_ref.5), channel_id=1, source_target_pairs={{0,1},{1,0},{2,3},{3,2},{4,5},{5,4},{6,7},{7,6},{8,9},{9,8},{10,11... | collective-permute-start | bytes 4718600 | tf_op jit(solution)/shard_map/ppermute | solution.py:48
  82.8 45.6 %collective-permute-start.18 = (bf16[512,1664]{1,0:T(8,128)(2,1)}, bf16[512,1664]{1,0:T(8,128)(2,1)}, u32[]{:S(2)}, u32[]{:S(2)}) collective-permute-start(bf16[512,1664]{1,0:T(8,128)(2,1)} %marked_rows.1.refs_4_), channel_id=1, source_target_pairs={{0,1},{1,0},{2,3},{3,2},{4,5},{5,4},{6,7},{7,6},{8,9},{9,8},{10,11... | collective-permute-start | bytes 5111816 | tf_op jit(solution)/shard_map/ppermute | solution.py:48
  91.2 37.2 %collective-permute-start.17 = (bf16[96,3072]{1,0:T(8,128)(2,1)}, bf16[96,3072]{1,0:T(8,128)(2,1)}, u32[]{:S(2)}, u32[]{:S(2)}) collective-permute-start(bf16[96,3072]{1,0:T(8,128)(2,1)} %collective-permute-done.14.refs_2_), channel_id=1, source_target_pairs={{0,8},{2,10},{4,12},{6,14},{8,16},{10,18},{12,20},{14,22},{16,24},... | collective-permute-start | bytes 1769480 | tf_op jit(solution)/shard_map/ppermute | solution.py:44
  128.4 63.9 %collective-permute-start.19 = (bf16[4,96,3456]{2,1,0:T(8,128)(2,1)S(1)}, bf16[4,96,3456]{2,1,0:T(8,128)(2,1)}, u32[]{:S(2)}, u32[]{:S(2)}) collective-permute-start(bf16[4,96,3456]{2,1,0:T(8,128)(2,1)S(1)} %copy-done.5), channel_id=1, source_target_pairs={{0,8},{2,10},{4,12},{6,14},{8,16},{10,18},{12,20},{14,22},{16,24},... | collective-permute-start | bytes 7962632 | tf_op jit(solution)/shard_map/ppermute | solution.py:44
  147.8 36.4 %collective-permute-start.20 = (bf16[4,96,1536]{2,1,0:T(8,128)(2,1)}, bf16[4,96,1536]{2,1,0:T(8,128)(2,1)S(1)}, u32[]{:S(2)}, u32[]{:S(2)}) collective-permute-start(bf16[4,96,1536]{2,1,0:T(8,128)(2,1)} %stack_columns.4.refs_4_.refs_6_), channel_id=1, source_target_pairs={{0,2},{2,0},{4,6},{6,4},{8,10},{10,8},{12,14},{14,12},{16,18},{18,... | collective-permute-start | bytes 3538952 | tf_op jit(solution)/shard_map/ppermute | solution.py:39
  147.9 36.4 %collective-permute-start.21 = (bf16[4,96,1536]{2,1,0:T(8,128)(2,1)}, bf16[4,96,1536]{2,1,0:T(8,128)(2,1)}, u32[]{:S(2)}, u32[]{:S(2)}) collective-permute-start(bf16[4,96,1536]{2,1,0:T(8,128)(2,1)} %stack_columns.4.refs_4_.refs_6_), channel_id=1, source_target_pairs={{0,4},{2,6},{4,0},{6,2},{8,12},{10,14},{12,8},{14,10},{16,20},{18,... | collective-permute-start | bytes 3538952 | tf_op jit(solution)/shard_map/ppermute | solution.py:39
  192.3 58.8 %collective-permute-start.22 = (bf16[4,96,3456]{2,1,0:T(8,128)(2,1)}, bf16[4,96,3456]{2,1,0:T(8,128)(2,1)S(1)}, u32[]{:S(2)}, u32[]{:S(2)}) collective-permute-start(bf16[4,96,3456]{2,1,0:T(8,128)(2,1)} %collective-permute-done.19.refs_8_.refs_12_), channel_id=1, source_target_pairs={{0,8},{2,10},{4,12},{6,14},{8,16},{10,18},{12,20},{14,22},{16,24},... | collective-permute-start | bytes 7962632 | tf_op jit(solution)/shard_map/ppermute | solution.py:44
  251.2 57.4 %collective-permute-start.30 = (bf16[4,96,3456]{2,1,0:T(8,128)(2,1)S(1)}, bf16[4,96,3456]{2,1,0:T(8,128)(2,1)}, u32[]{:S(2)}, u32[]{:S(2)}) collective-permute-start(bf16[4,96,3456]{2,1,0:T(8,128)(2,1)S(1)} %collective-permute-done.22.refs_9_.refs_13_), channel_id=1, source_target_pairs={{0,8},{2,10},{4,12},{6,14},{8,16},{10,18},{12,20},{14,22},{16,24},... | collective-permute-start | bytes 7962632 | tf_op jit(solution)/shard_map/ppermute | solution.py:44
  329.5 40.4 %collective-permute-start.37 = (bf16[512,1664]{1,0:T(8,128)(2,1)}, bf16[512,1664]{1,0:T(8,128)(2,1)}, u32[]{:S(2)}, u32[]{:S(2)}) collective-permute-start(bf16[512,1664]{1,0:T(8,128)(2,1)} %collective-permute-done.31.values_ref.refs_6_), channel_id=1, source_target_pairs={{0,1},{1,0},{2,3},{3,2},{4,5},{5,4},{6,7},{7,6},{8,9},{9,8},{10,11... | collective-permute-start | bytes 5111816 | tf_op jit(solution)/shard_map/ppermute | solution.py:48
  329.9 40.1 %collective-permute-start.38 = (bf16[512,1664]{1,0:T(8,128)(2,1)}, bf16[512,1664]{1,0:T(8,128)(2,1)}, u32[]{:S(2)}, u32[]{:S(2)}) collective-permute-start(bf16[512,1664]{1,0:T(8,128)(2,1)} %collective-permute-done.32.values_ref.refs_8_), channel_id=1, source_target_pairs={{0,1},{1,0},{2,3},{3,2},{4,5},{5,4},{6,7},{7,6},{8,9},{9,8},{10,11... | collective-permute-start | bytes 5111816 | tf_op jit(solution)/shard_map/ppermute | solution.py:48
  330.7 39.3 %collective-permute-start.35 = (bf16[512,1536]{1,0:T(8,128)(2,1)}, bf16[512,1536]{1,0:T(8,128)(2,1)S(1)}, u32[]{:S(2)}, u32[]{:S(2)}) collective-permute-start(bf16[512,1536]{1,0:T(8,128)(2,1)} %get-tuple-element.354.refs_2_), channel_id=1, source_target_pairs={{0,2},{2,0},{4,6},{6,4},{8,10},{10,8},{12,14},{14,12},{16,18},{18,... | collective-permute-start | bytes 4718600 | tf_op jit(solution)/shard_map/ppermute | solution.py:39
  332.0 38.0 %collective-permute-start.36 = (bf16[512,1536]{1,0:T(8,128)(2,1)}, bf16[512,1536]{1,0:T(8,128)(2,1)S(1)}, u32[]{:S(2)}, u32[]{:S(2)}) collective-permute-start(bf16[512,1536]{1,0:T(8,128)(2,1)} %get-tuple-element.354.refs_2_), channel_id=1, source_target_pairs={{0,4},{2,6},{4,0},{6,2},{8,12},{10,14},{12,8},{14,10},{16,20},{18,... | collective-permute-start | bytes 4718600 | tf_op jit(solution)/shard_map/ppermute | solution.py:39
  376.4 77.8 %collective-permute-start.41 = (bf16[256,1664]{1,0:T(8,128)(2,1)}, bf16[256,1664]{1,0:T(8,128)(2,1)S(1)}, u32[]{:S(2)}, u32[]{:S(2)}) collective-permute-start(bf16[256,1664]{1,0:T(8,128)(2,1)} %cut_rows.4), channel_id=1, source_target_pairs={{0,4},{2,6},{4,0},{6,2},{8,12},{10,14},{12,8},{14,10},{16,20},{18,... | collective-permute-start | bytes 2555912 | tf_op jit(solution)/shard_map/ppermute | solution.py:39
  377.6 77.7 %collective-permute-start.42 = (bf16[256,1664]{1,0:T(8,128)(2,1)}, bf16[256,1664]{1,0:T(8,128)(2,1)S(1)}, u32[]{:S(2)}, u32[]{:S(2)}) collective-permute-start(bf16[256,1664]{1,0:T(8,128)(2,1)} %cut_rows.5), channel_id=1, source_target_pairs={{0,2},{2,0},{4,6},{6,4},{8,10},{10,8},{12,14},{14,12},{16,18},{18,... | collective-permute-start | bytes 2555912 | tf_op jit(solution)/shard_map/ppermute | solution.py:39
  377.8 76.4 %collective-permute-start.43 = (bf16[256,1536]{1,0:T(8,128)(2,1)}, bf16[256,1536]{1,0:T(8,128)(2,1)S(1)}, u32[]{:S(2)}, u32[]{:S(2)}) collective-permute-start(bf16[256,1536]{1,0:T(8,128)(2,1)} %cut_rows.6), channel_id=1, source_target_pairs={{0,4},{2,6},{4,0},{6,2},{8,12},{10,14},{12,8},{14,10},{16,20},{18,... | collective-permute-start | bytes 2359304 | tf_op jit(solution)/shard_map/ppermute | solution.py:39
  378.0 76.2 %collective-permute-start.44 = (bf16[256,1536]{1,0:T(8,128)(2,1)}, bf16[256,1536]{1,0:T(8,128)(2,1)S(1)}, u32[]{:S(2)}, u32[]{:S(2)}) collective-permute-start(bf16[256,1536]{1,0:T(8,128)(2,1)} %cut_rows.7), channel_id=1, source_target_pairs={{0,2},{2,0},{4,6},{6,4},{8,10},{10,8},{12,14},{14,12},{16,18},{18,... | collective-permute-start | bytes 2359304 | tf_op jit(solution)/shard_map/ppermute | solution.py:39
  464.4 39.2 %collective-permute-start.49 = (bf16[2,512,1536]{2,1,0:T(8,128)(2,1)}, bf16[2,512,1536]{2,1,0:T(8,128)(2,1)S(1)}, u32[]{:S(2)}, u32[]{:S(2)}) collective-permute-start(bf16[2,512,1536]{2,1,0:T(8,128)(2,1)} %get-tuple-element.388), channel_id=1, source_target_pairs={{0,1},{1,0},{2,3},{3,2},{4,5},{5,4},{6,7},{7,6},{8,9},{9,8},{10,11... | collective-permute-start | bytes 9437192 | tf_op jit(solution)/shard_map/ppermute | solution.py:48
  464.8 38.9 %collective-permute-start.50 = (bf16[1,512,1536]{2,1,0:T(8,128)(2,1)}, bf16[1,512,1536]{2,1,0:T(8,128)(2,1)}, u32[]{:S(2)}, u32[]{:S(2)}) collective-permute-start(bf16[1,512,1536]{2,1,0:T(8,128)(2,1)} %get-tuple-element.390), channel_id=1, source_target_pairs={{0,1},{1,0},{2,3},{3,2},{4,5},{5,4},{6,7},{7,6},{8,9},{9,8},{10,11... | collective-permute-start | bytes 4718600 | tf_op jit(solution)/shard_map/ppermute | solution.py:48
  538.6 51.4 %collective-permute-start.59 = (bf16[384,1152]{1,0:T(8,128)(2,1)}, bf16[384,1152]{1,0:T(8,128)(2,1)S(1)}, u32[]{:S(2)}, u32[]{:S(2)}) collective-permute-start(bf16[384,1152]{1,0:T(8,128)(2,1)} %line_step.13), channel_id=1, source_target_pairs={{0,8},{2,10},{4,12},{6,14},{8,16},{10,18},{12,20},{14,22},{16,24},... | collective-permute-start | bytes 2654216 | tf_op jit(solution)/shard_map/ppermute | solution.py:44
  543.5 52.2 %collective-permute-start.54 = (bf16[512,1536]{1,0:T(8,128)(2,1)}, bf16[512,1536]{1,0:T(8,128)(2,1)S(1)}, u32[]{:S(2)}, u32[]{:S(2)}) collective-permute-start(bf16[512,1536]{1,0:T(8,128)(2,1)} %get-tuple-element.411), channel_id=1, source_target_pairs={{0,2},{2,0},{4,6},{6,4},{8,10},{10,8},{12,14},{14,12},{16,18},{18,... | collective-permute-start | bytes 4718600 | tf_op jit(solution)/shard_map/ppermute | solution.py:39
  544.8 50.8 %collective-permute-start.55 = (bf16[512,1536]{1,0:T(8,128)(2,1)}, bf16[512,1536]{1,0:T(8,128)(2,1)S(1)}, u32[]{:S(2)}, u32[]{:S(2)}) collective-permute-start(bf16[512,1536]{1,0:T(8,128)(2,1)} %get-tuple-element.412), channel_id=1, source_target_pairs={{0,4},{2,6},{4,0},{6,2},{8,12},{10,14},{12,8},{14,10},{16,20},{18,... | collective-permute-start | bytes 4718600 | tf_op jit(solution)/shard_map/ppermute | solution.py:39
  547.9 48.7 %collective-permute-start.60 = (bf16[256,1536]{1,0:T(8,128)(2,1)}, bf16[256,1536]{1,0:T(8,128)(2,1)}, u32[]{:S(2)}, u32[]{:S(2)}) collective-permute-start(bf16[256,1536]{1,0:T(8,128)(2,1)} %get-tuple-element.424), channel_id=1, source_target_pairs={{0,2},{2,0},{4,6},{6,4},{8,10},{10,8},{12,14},{14,12},{16,18},{18,... | collective-permute-start | bytes 2359304 | tf_op jit(solution)/shard_map/ppermute | solution.py:39
  548.0 49.7 %collective-permute-start.61 = (bf16[256,1536]{1,0:T(8,128)(2,1)}, bf16[256,1536]{1,0:T(8,128)(2,1)}, u32[]{:S(2)}, u32[]{:S(2)}) collective-permute-start(bf16[256,1536]{1,0:T(8,128)(2,1)} %get-tuple-element.431), channel_id=1, source_target_pairs={{0,4},{2,6},{4,0},{6,2},{8,12},{10,14},{12,8},{14,10},{16,20},{18,... | collective-permute-start | bytes 2359304 | tf_op jit(solution)/shard_map/ppermute | solution.py:39
  612.3 36.3 %collective-permute-start.65 = (bf16[512,1536]{1,0:T(8,128)(2,1)}, bf16[512,1536]{1,0:T(8,128)(2,1)}, u32[]{:S(2)}, u32[]{:S(2)}) collective-permute-start(bf16[512,1536]{1,0:T(8,128)(2,1)} %get-tuple-element.434), channel_id=1, source_target_pairs={{0,2},{2,0},{4,6},{6,4},{8,10},{10,8},{12,14},{14,12},{16,18},{18,... | collective-permute-start | bytes 4718600 | tf_op jit(solution)/shard_map/ppermute | solution.py:39
  613.5 61.8 %collective-permute-start.64 = (bf16[384,3456]{1,0:T(8,128)(2,1)}, bf16[384,3456]{1,0:T(8,128)(2,1)}, u32[]{:S(2)}, u32[]{:S(2)}) collective-permute-start(bf16[384,3456]{1,0:T(8,128)(2,1)} %line_step.14), channel_id=1, source_target_pairs={{0,8},{2,10},{4,12},{6,14},{8,16},{10,18},{12,20},{14,22},{16,24},... | collective-permute-start | bytes 7962632 | tf_op jit(solution)/shard_map/ppermute | solution.py:44
  669.1 63.7 %collective-permute-start.67 = (bf16[768,1536]{1,0:T(8,128)(2,1)}, bf16[768,1536]{1,0:T(8,128)(2,1)S(1)}, u32[]{:S(2)}, u32[]{:S(2)}) collective-permute-start(bf16[768,1536]{1,0:T(8,128)(2,1)} %plane_start.4), channel_id=1, source_target_pairs={{0,2},{2,0},{4,6},{6,4},{8,10},{10,8},{12,14},{14,12},{16,18},{18,... | collective-permute-start | bytes 7077896 | tf_op jit(solution)/shard_map/ppermute | solution.py:39
  674.4 63.7 %collective-permute-start.68 = (bf16[768,1536]{1,0:T(8,128)(2,1)}, bf16[768,1536]{1,0:T(8,128)(2,1)}, u32[]{:S(2)}, u32[]{:S(2)}) collective-permute-start(bf16[768,1536]{1,0:T(8,128)(2,1)} %plane_start.5), channel_id=1, source_target_pairs={{0,4},{2,6},{4,0},{6,2},{8,12},{10,14},{12,8},{14,10},{16,20},{18,... | collective-permute-start | bytes 7077896 | tf_op jit(solution)/shard_map/ppermute | solution.py:39
  681.0 75.5 %collective-permute-start.70 = (bf16[384,3456]{1,0:T(8,128)(2,1)}, bf16[384,3456]{1,0:T(8,128)(2,1)}, u32[]{:S(2)}, u32[]{:S(2)}) collective-permute-start(bf16[384,3456]{1,0:T(8,128)(2,1)} %line_step.15), channel_id=1, source_target_pairs={{0,8},{2,10},{4,12},{6,14},{8,16},{10,18},{12,20},{14,22},{16,24},... | collective-permute-start | bytes 7962632 | tf_op jit(solution)/shard_map/ppermute | solution.py:44
  777.6 45.1 %collective-permute-start.75 = (bf16[384,2304]{1,0:T(8,128)(2,1)}, bf16[384,2304]{1,0:T(8,128)(2,1)S(1)}, u32[]{:S(2)}, u32[]{:S(2)}) collective-permute-start(bf16[384,2304]{1,0:T(8,128)(2,1)} %line_step.16), channel_id=1, source_target_pairs={{0,8},{2,10},{4,12},{6,14},{8,16},{10,18},{12,20},{14,22},{16,24},... | collective-permute-start | bytes 5308424 | tf_op jit(solution)/shard_map/ppermute | solution.py:44
  865.0 45.5 %collective-permute-start.85 = (bf16[96,3456]{1,0:T(8,128)(2,1)}, bf16[96,3456]{1,0:T(8,128)(2,1)S(1)}, u32[]{:S(2)}, u32[]{:S(2)}) collective-permute-start(bf16[96,3456]{1,0:T(8,128)(2,1)} %get-tuple-element.502), channel_id=1, source_target_pairs={{0,2},{2,0},{4,6},{6,4},{8,10},{10,8},{12,14},{14,12},{16,18},{18,... | collective-permute-start | bytes 1990664 | tf_op jit(solution)/shard_map/ppermute | solution.py:39
  865.8 44.7 %collective-permute-start.86 = (bf16[96,3456]{1,0:T(8,128)(2,1)}, bf16[96,3456]{1,0:T(8,128)(2,1)S(1)}, u32[]{:S(2)}, u32[]{:S(2)}) collective-permute-start(bf16[96,3456]{1,0:T(8,128)(2,1)} %get-tuple-element.503), channel_id=1, source_target_pairs={{0,4},{2,6},{4,0},{6,2},{8,12},{10,14},{12,8},{14,10},{16,20},{18,... | collective-permute-start | bytes 1990664 | tf_op jit(solution)/shard_map/ppermute | solution.py:39
  867.0 43.5 %collective-permute-start.87 = (bf16[96,3456]{1,0:T(8,128)(2,1)}, bf16[96,3456]{1,0:T(8,128)(2,1)}, u32[]{:S(2)}, u32[]{:S(2)}) collective-permute-start(bf16[96,3456]{1,0:T(8,128)(2,1)} %get-tuple-element.504), channel_id=1, source_target_pairs={{0,6},{2,4},{4,2},{6,0},{8,14},{10,12},{12,10},{14,8},{16,22},{18,... | collective-permute-start | bytes 1990664 | tf_op jit(solution)/shard_map/ppermute | solution.py:39
  (136 other events, 1625.2 us)

commit v3 on v2

--- a/solution.py
+++ b/solution.py
@@ -614,8 +614,8 @@
 
 
 class LineSums:
-    def __init__(self, parts, order, lines, height, where):
-        self.parts, self.order, self.lines = parts, order, lines
+    def __init__(self, parts, order, lines, height, where, apart=()):
+        self.parts, self.order, self.lines, self.apart = parts, order, lines, apart
         self.height, self.where = height, where
         self.steps, self.final, self.names = {}, {}, []
         self.sent = None
@@ -656,7 +656,10 @@
                     start += sum(width for width, _, _ in self.parts[name](None))
                     self.steps[name] += 1
                     if self.steps[name] + 1 == self.lines:
-                        self.final[name] = self._step([name], overs, F32)
+                        if name in self.apart:
+                            self.final[name] = overs[name]
+                        else:
+                            self.final[name] = self._step([name], overs, F32)
             staying = [name for name in self.names if name not in self.final]
             for name in joining:
                 self.steps[name] = 0
@@ -664,33 +667,96 @@
                 self._send(staying + joining, overs)
 
 
-def member_pieces(gu, down, where, height):
-    wide, narrow = gu.shape[1], down.shape[1]
-
-    def spot_of(k, spots):
+def member_pieces(parts, where, lines, height):
+    def member(k, spots):
         bit_0 = lax.rem(spots[0] + k % 2, 2)
         return bit_0 + 2 * lax.rem(spots[0] // 2 + k // 2, 2)
 
+    total = sum(item[3] for item in parts)
     if height % 32:
-        return [
-            jnp.concatenate(
-                [pick(item.reshape(GROUP, height, -1), spot_of(k, where)) for item in (gu, down)],
-                axis=1,
-            ).astype(BF)
-            for k in range(GROUP)
-        ]
-
-    def body(where_ref, gu_ref, down_ref, *out_refs):
+        done = []
+        for k in range(GROUP):
+            columns = []
+            for array, came, number, width in parts:
+                block = pick(array[:, :width].reshape(lines, GROUP, height, width), where[1])
+                other = came[:, number * width : (number + 1) * width]
+                block = block.astype(F32) + other.reshape(GROUP, height, width).astype(F32)
+                columns.append(pick(block, member(k, where)))
+            done.append(jnp.concatenate(columns, axis=1).astype(BF))
+        return done
+
+    def body(where_ref, *refs):
+        count = len(parts)
+        array_refs, came_refs = refs[:count], refs[count : 2 * count]
+        out_refs = refs[2 * count : 2 * count + GROUP]
+        helds, sems = refs[2 * count + GROUP : -1], refs[-1]
+        rows = GROUP * height
+        start = pl.multiple_of(where_ref[1] * rows, rows)
+        copies = []
+        for i, (_, _, number, width) in enumerate(parts):
+            copies += [
+                pltpu.make_async_copy(
+                    array_refs[i].at[pl.ds(start, rows), :width], helds[2 * i], sems.at[2 * i]
+                ),
+                pltpu.make_async_copy(
+                    came_refs[i].at[:, number * width : (number + 1) * width],
+                    helds[2 * i + 1], sems.at[2 * i + 1],
+                ),
+            ]
+        run_copies(copies)
         for k, out_ref in enumerate(out_refs):
-            rows = pl.ds(pl.multiple_of(spot_of(k, where_ref) * height, height), height)
-            out_ref[:, :wide] = gu_ref[rows, :].astype(BF)
-            out_ref[:, wide:] = down_ref[rows, :].astype(BF)
-
+            spot = pl.ds(pl.multiple_of(member(k, where_ref) * height, height), height)
+            at = 0
+            for i, (_, _, _, width) in enumerate(parts):
+                term = helds[2 * i][spot, :].astype(F32) + helds[2 * i + 1][spot, :].astype(F32)
+                out_ref[:, at : at + width] = term.astype(BF)
+                at += width
+
+    vmem, any_ref = pl.BlockSpec(memory_space=pltpu.VMEM), pl.BlockSpec(memory_space=pl.ANY)
+    held = [pltpu.VMEM((GROUP * height, width), BF) for *_, width in parts for _ in range(2)]
     return list(
-        small_call(
-            body, [((height, wide + narrow), BF)] * GROUP, [where, gu, down], "member_pieces", 1
-        )
-    )
+        pl.pallas_call(
+            body,
+            out_shape=(jax.ShapeDtypeStruct((height, total), BF),) * GROUP,
+            in_specs=[pl.BlockSpec(memory_space=pltpu.SMEM)] + [any_ref] * (2 * len(parts)),
+            out_specs=(vmem,) * GROUP,
+            scratch_shapes=held + [pltpu.SemaphoreType.DMA((2 * len(parts),))],
+            compiler_params=pltpu.CompilerParams(vmem_limit_bytes=VMEM),
+            cost_estimate=SMALL,
+            name="member_pieces",
+        )(where, *[item[0] for item in parts], *[item[1] for item in parts])
+    )
+
+
+def sum_in_order(pieces, place, count):
+    rows, width = pieces[0].shape
+
+    def body(place_ref, *refs):
+        out_ref, held = refs[-2:]
+        for k in range(count):
+            spot = 0
+            bit = 1
+            while bit < count:
+                own = lax.rem(place_ref[0] // bit, 2)
+                spot = spot + bit * (1 - own if k & bit else own)
+                bit *= 2
+            held[spot] = refs[k][...]
+        total = held[0]
+        for number in range(1, count):
+            total = total + held[number]
+        out_ref[...] = total
+
+    vmem = pl.BlockSpec(memory_space=pltpu.VMEM)
+    return pl.pallas_call(
+        body,
+        out_shape=jax.ShapeDtypeStruct((rows, width), F32),
+        in_specs=[pl.BlockSpec(memory_space=pltpu.SMEM)] + [vmem] * count,
+        out_specs=vmem,
+        scratch_shapes=[pltpu.VMEM((count, rows, width), F32)],
+        compiler_params=pltpu.CompilerParams(vmem_limit_bytes=VMEM),
+        cost_estimate=SMALL,
+        name="sum_in_order",
+    )(place, *pieces)
 
 
 def gathered_call(body, tile, row_args, fixed_args, matrices, shift, outs, name):
@@ -814,7 +880,7 @@
 def split_rows(value, number, steps, low_ref, high_ref):
     @pl.when(number < steps // 2)
     def _():
-        low_ref[...] = value
+        low_ref[...] = value.astype(BF)
 
     @pl.when(number >= steps // 2)
     def _():
@@ -838,7 +904,7 @@
     return gathered_call(
         body, tile, [y, gate, squares, others], [kern], [matrix], shift,
         [
-            ((rows, width), BF, "rows"), ((rows // 2, depth), F32, "low"),
+            ((rows, width), BF, "rows"), ((rows // 2, depth), BF, "low"),
             ((rows // 2, depth), F32, "high"),
         ],
         "mixed_product",
@@ -897,7 +963,7 @@
 
     return gathered_call(
         body, tile, grads, [], matrices, shift,
-        [((rows // 2, depth), F32, "low"), ((rows // 2, depth), F32, "high")], "normed_back",
+        [((rows // 2, depth), BF, "low"), ((rows // 2, depth), F32, "high")], "normed_back",
     )
 
 
@@ -981,27 +1047,79 @@
     )(core, tokens, others, gain).reshape(2 * rows, width)
 
 
-def marked_rows(grad_out, routes, first_lane):
+def marked_rows(grad_out, routes, core, first_lane):
     rows, width = grad_out.shape
-
-    def body(grad_ref, routes_ref, out_ref):
+    tile = 256
+
+    def body(core_ref, grad_ref, routes_ref, out_ref):
         out_ref[:, :width] = grad_ref[...]
-        lane = lax.broadcasted_iota(jnp.int32, (grad_ref.shape[0], LANES), 1)
+        lane = lax.broadcasted_iota(jnp.int32, (tile, LANES), 1)
+        start = pl.multiple_of(core_ref[0] * rows + pl.program_id(0) * tile, tile)
+        named = routes_ref[pl.ds(start, tile), :]
         marks = jnp.zeros(lane.shape, F32)
         for number in range(routes_ref.shape[1]):
-            marks = jnp.where(lane == routes_ref[:, number : number + 1] + first_lane, 1.0, marks)
+            marks = jnp.where(lane == named[:, number : number + 1] + first_lane, 1.0, marks)
         out_ref[:, width:] = marks.astype(BF)
 
-    return rows_call(
-        body, 256, [grad_out, routes], [], [((rows, width + LANES), BF, False)], "marked_rows"
-    )[0]
+    return pl.pallas_call(
+        body,
+        grid=(rows // tile,),
+        out_shape=jax.ShapeDtypeStruct((rows, width + LANES), BF),
+        in_specs=[
+            pl.BlockSpec(memory_space=pltpu.SMEM),
+            pl.BlockSpec((tile, width), lambda i: (i, 0)),
+            pl.BlockSpec(routes.shape, lambda i: (0, 0)),
+        ],
+        out_specs=pl.BlockSpec((tile, width + LANES), lambda i: (i, 0)),
+        compiler_params=pltpu.CompilerParams(
+            dimension_semantics=("arbitrary",), vmem_limit_bytes=VMEM
+        ),
+        cost_estimate=SMALL,
+        name="marked_rows",
+    )(core, grad_out, routes)
+
+
+def prepare_params(conv_w, conv_b, norm_gain, d_skip, dt_bias, a_log, core, local, heads):
+    wide = conv_w.shape[1]
+    both = norm_gain.shape[1]
+
+    def body(core_ref, w_ref, b_ref, gain_ref, skip_ref, bias_ref, log_ref, kern_ref, head_ref, spread_ref):
+        row = lax.broadcasted_iota(jnp.int32, (LANES, local), 0)
+        column = lax.broadcasted_iota(jnp.int32, (LANES, local), 1)
+        head = jnp.where(row >= LANES // 2, row - LANES // 2, row)
+        low = head * P_SIZE
+        spread = jnp.where((column >= low) & (column < low + P_SIZE), 1.0, 0.0).astype(BF)
+        spread_ref[...] = spread
+        first = core_ref[0] == 0
+
+        def mine(ref):
+            return jnp.where(first, ref[:, :heads], ref[:, heads : 2 * heads])
+
+        kern_ref[...] = jnp.zeros(kern_ref.shape, F32)
+        spot = pl.ds(pl.multiple_of(core_ref[0] * local, LANES), local)
+        kern_ref[0:4, :local] = w_ref[:, spot]
+        kern_ref[0:4, local + LANES :] = w_ref[:, both:]
+        kern_ref[4:5, :local] = b_ref[:, spot]
+        kern_ref[4:5, local + LANES :] = b_ref[:, both:]
+        head_ref[...] = jnp.zeros(head_ref.shape, F32)
+        head_ref[2:3, :heads] = mine(skip_ref)
+        kern_ref[5:6, :local] = spread_heads(head_ref[...], spread)[2:3]
+        kern_ref[6:7, :local] = gain_ref[:, spot]
+        head_ref[0:1, :heads] = mine(bias_ref)
+        head_ref[1:2, :heads] = jnp.exp(mine(log_ref))
+
+    return small_call(
+        body,
+        [((8, local + LANES + wide - both), F32), ((8, LANES), F32), ((LANES, local), BF)],
+        [core, conv_w, conv_b, norm_gain, d_skip, dt_bias, a_log], "prepare_params", 1,
+    )
 
 
 def mid_rows_of(mixed, others, tokens, gain):
     rows, width = tokens.shape
 
     def body(mixed_ref, other_ref, tokens_ref, gain_ref, resid_ref, mid_ref):
-        resid = tokens_ref[...].astype(F32) + mixed_ref[...] + other_ref[...]
+        resid = tokens_ref[...].astype(F32) + mixed_ref[...] + other_ref[...].astype(F32)
         resid_ref[...] = resid
         mid_ref[...] = (resid * norm_rows(resid) * gain_ref[...]).astype(BF)
 
@@ -1105,7 +1223,7 @@
     rows, width = tokens.shape
 
     def body(mine_ref, came_ref, tokens_ref, d_resid_ref, gain_ref, out_ref, gain_grad_ref):
-        d_rows = mine_ref[...] + came_ref[...]
+        d_rows = mine_ref[...] + came_ref[...].astype(F32)
         d_extra = norm_back(d_rows, tokens_ref[...].astype(F32), gain_ref[...], gain_grad_ref)
         out_ref[...] = (d_resid_ref[...] + d_extra).astype(BF)
 
@@ -1138,6 +1256,46 @@
         body, [((8, both + rest), F32)],
         [core, par_grads, head_grads, gain_grads, mid_gains, in_gains, spread], "pack_small", 1,
     )[0]
+
+
+def out_outputs(og_sums, cut):
+    height = og_sums.shape[0]
+
+    def body(sums_ref, out_ref):
+        out_ref[:cut, :] = sums_ref[:, :cut].T
+        out_ref[cut:, :] = sums_ref[:, 2 * cut : 3 * cut].T
+
+    return small_call(body, [((2 * cut, height), F32)], [og_sums], "out_outputs")[0]
+
+
+def inner_outputs(og_sums, in_sums, core, local, heads, cut):
+    height = in_sums.shape[0]
+    half = height // 2
+    if height % 32:
+        gate = jnp.concatenate([og_sums[:, cut : 2 * cut], og_sums[:, 3 * cut :]], axis=1)
+        joint = in_sums[:, local:].reshape(2, half, -1)
+        return (
+            jnp.stack([gate, in_sums[:, :local]], axis=1), in_sums[:, local : local + heads],
+            pick(joint, core[0]), pick(joint, 1 - core[0]),
+        )
+
+    def body(core_ref, og_ref, in_ref, zx_ref, dt_ref, mine_ref, sent_ref):
+        zx_ref[:, 0, :cut] = og_ref[:, cut : 2 * cut]
+        zx_ref[:, 0, cut:] = og_ref[:, 3 * cut :]
+        zx_ref[:, 1, :] = in_ref[:, :local]
+        dt_ref[...] = in_ref[:, local : local + heads]
+        for ref, spot in ((mine_ref, core_ref[0]), (sent_ref, 1 - core_ref[0])):
+            ref[...] = in_ref[pl.ds(pl.multiple_of(spot * half, half), half), local:]
+
+    rest = in_sums.shape[1] - local
+    return small_call(
+        body,
+        [
+            ((height, 2, local), F32), ((height, heads), F32), ((half, rest), F32),
+            ((half, rest), F32),
+        ],
+        [core, og_sums, in_sums], "inner_outputs", 1,
+    )
 
 
 def unpack_experts(came, place, units, shared_units):
@@ -1199,7 +1357,7 @@
     (router_ref,) = take(1)
     part_refs = take(part_count)
     take(aliased)
-    x_out, dy_out, gu_ref, down_ref = take(4)
+    x_out, dy_out, gate_ref, up_ref, down_ref = take(5)
     out_mine, out_other, dx_mine, dx_other = take(4)
     w, sems, x_held, ym_held, row_sems = refs
     step = pl.program_id(0)
@@ -1268,19 +1426,20 @@
             d_gates = jnp.where(here, d_gate, d_gates)
             d_act = d_act * gate
             act = act * gate
-        gu_ref[:, cols[0]] = (d_act * up * sig * (1.0 + pre * (1.0 - sig))).astype(BF)
-        gu_ref[:, cols[1]] = (d_act * silu).astype(BF)
+        gate_ref[:, cols[0]] = (d_act * up * sig * (1.0 + pre * (1.0 - sig))).astype(BF)
+        up_ref[:, cols[0]] = (d_act * silu).astype(BF)
         down_ref[:, start : start + size] = act.astype(BF)
     mean = jnp.sum(gates * d_gates, axis=1, keepdims=True)
     d_logits = (gates * (d_gates - mean)).astype(BF)
-    gu_ref[:, 2 * hidden :] = d_logits
+    up_ref[:, hidden:] = d_logits
     cut = 256
 
     def results(out_ref, dx_ref):
         for number in range(width // cut):
             rows = slice(number * cut, (number + 1) * cut)
             out_ref[0, :, rows] = nt(down_ref[...], w[rows, 2 * hidden :]).astype(BF)
-            d_x = nt(gu_ref[:, : 2 * hidden], w[rows, : 2 * hidden])
+            d_x = nt(gate_ref[...], w[rows, :hidden])
+            d_x = d_x + nt(up_ref[:, :hidden], w[rows, hidden : 2 * hidden])
             dx_ref[0, :, rows] = (d_x + nt(d_logits, router_ref[rows, :])).astype(BF)
 
     @pl.when(slot == 0)
@@ -1312,7 +1471,8 @@
         jax.ShapeDtypeStruct((count, tile, width), BF),
         pl.BlockSpec((1, tile, width), lambda i: (i // 2, 0, 0)),
     )
-    outs = [like(width), like(width), like(2 * hidden + LANES), like(hidden)] + [result] * 4
+    outs = [like(columns) for columns in (width, width, hidden, hidden + LANES, hidden)]
+    outs += [result] * 4
     any_ref = pl.BlockSpec(memory_space=pl.ANY)
     flat = [part for item in x_pieces + ym_pieces for part in item]
     args = [targets, base, *flat, router, *parts, *held]
@@ -1340,7 +1500,7 @@
         cost_estimate=SMALL,
         name="expert_rows",
     )(*args)
-    return list(done[:4]), list(done[4:])
+    return list(done[:5]), list(done[5:])
 
 
 def shards(
@@ -1374,7 +1534,8 @@
     order = Order()
 
     core_now = core.reshape(1)
-    gain_in, gain_mid = gain_in[None], gain_mid[None]
+    gain_in, gain_mid, conv_b, norm_gain = gain_in[None], gain_mid[None], conv_b[None], norm_gain[None]
+    d_skip, dt_bias, a_log = d_skip[None], dt_bias[None], a_log[None]
     joint = jnp.concatenate([w_bc, router], axis=1)
     joint_came = swap(joint)
     ring_a = [w_zx[:, 1, :cut_in]]
@@ -1384,15 +1545,15 @@
     bc_cols, router_cols = joint[:, : 2 * NS], joint[:, 2 * NS :]
     pad = jnp.zeros((height, LANES - heads - EXPERTS), BF)
     ring_b = [jnp.concatenate([w_zx[:, 1, cut_in:], w_dt, router_cols, pad, bc_cols], axis=1)]
-    order.set(
-        ring_b[0], gain_in, gain_mid, where, base, mine_last, place_now, core_now, mixer_targets,
-        expert_targets,
-    )
+    order.set(ring_b[0])
     shared_units = shared_gu.shape[2] // GROUP
     hidden = own * units + shared_units
     gu = order(expert_gu).reshape(GROUP, own, height, 2, units).transpose(0, 2, 3, 1, 4)
     gu = gu.reshape(GROUP, height, 2, own * units)
-    order.set(gu)
+    order.set(
+        gu, gain_in, gain_mid, where, base, mine_last, place_now, core_now, mixer_targets,
+        expert_targets,
+    )
     ring_on(ring_a, order, 1, 1 + third, lines)
     ring_on(ring_b, order, 1, 1 + third, lines)
     order.set(ring_a[-1], ring_b[-1])
@@ -1409,33 +1570,8 @@
     to_send = [pick(packed, members[k]) for k in range(GROUP)]
     order.set(*to_send)
     came = to_send[:1] + [hop(to_send[k], k) for k in range(1, GROUP)]
-    lane = jnp.arange(LANES, dtype=jnp.int32)
-    cut = functools.partial(lax.dynamic_slice_in_dim, start_index=core * local, slice_size=local)
-    cut_heads = functools.partial(lax.dynamic_slice_in_dim, start_index=core * heads, slice_size=heads)
-    conv_w, conv_b, norm_gain, routes = order((conv_w, conv_b, norm_gain, routes))
-    conv_all = jnp.concatenate([conv_w, conv_b[None]])
-    kern = jnp.concatenate(
-        [cut(conv_all, axis=1), jnp.zeros((5, LANES), F32), conv_all[:, inner_all:]], axis=1
-    )
-    tail = jnp.zeros((1, kern.shape[1] - local), F32)
-    skip_wide = jnp.repeat(cut_heads(d_skip, axis=0), P_SIZE)[None]
-    kern = jnp.concatenate(
-        [
-            kern,
-            jnp.concatenate([skip_wide, tail], axis=1),
-            jnp.concatenate([cut(norm_gain, axis=0)[None], tail], axis=1),
-            jnp.zeros((1, kern.shape[1]), F32),
-        ]
-    )
-    head_par = jnp.pad(
-        jnp.stack([cut_heads(dt_bias, axis=0), jnp.exp(cut_heads(a_log, axis=0))]),
-        ((0, 6), (0, LANES - heads)),
-    )
-    head_of = jnp.arange(local, dtype=jnp.int32) // P_SIZE
-    spread = (lax.rem(lane, LANES // 2)[:, None] == head_of[None, :]).astype(BF)
-    own_routes = lax.dynamic_slice_in_dim(routes, core * piece, piece, 0)
-    go_ring = [order(jnp.concatenate([w_zx[:, 0], w_out.T], axis=1))]
-    order.set(kern, head_par, spread, own_routes, go_ring[0])
+    go_block = order(jnp.concatenate([w_zx[:, 0], w_out.T], axis=1))
+    order.set(go_block)
     ring_on(ring_a, order, 1 + 2 * third, lines, lines)
     ring_on(ring_b, order, 1 + 2 * third, lines, lines)
     order.set(ring_a[-1], ring_b[-1])
@@ -1452,41 +1588,45 @@
         order.set(low, high)
         return parts + [hop(low, 2), hop(high, 1)]
 
+    go_ring = [order(go_block)]
     tokens_other = order.take(tokens_other)
     in_stack = stack_pairs(ring_a, ring_b)
-    marked = marked_rows(order(grad_out), own_routes, heads)
-    order.set(in_stack, marked)
+    order.set(in_stack)
     ring_on(go_ring, order, 1, 1 + third, lines)
     order.set(go_ring[-1])
-    in_w = along_both(order(in_stack))
     came = order.take(*came)
-    expert_ring = [stack_columns(came, 0, 3 * hidden)]
-    normed = normed_rows(order(tokens), tokens_other, gain_in, core_now)
-    order.set(normed, expert_ring[0])
     ring_on(go_ring, order, 1 + third, 1 + 2 * third, lines)
     order.set(go_ring[-1])
-    marked_other = swap(order(marked))
-    in_w = list(order.take(*in_w))
-    marked_other = order.take(marked_other)
-    in_w = across_halves(in_w, cut_in)
+    in_w = along_both(order(in_stack))
+    expert_ring = [stack_columns(order(came), 0, 3 * hidden)]
+    marked = marked_rows(order(grad_out), routes, core_now, heads)
+    normed = normed_rows(order(tokens), tokens_other, gain_in, core_now)
+    kern, head_par, spread = prepare_params(
+        order(conv_w), conv_b, norm_gain, d_skip, dt_bias, a_log, core_now, local, heads
+    )
+    order.set(normed, marked, expert_ring[0], kern)
     ring_on(go_ring, order, 1 + 2 * third, lines, lines)
     order.set(go_ring[-1])
-    gate_stack = stack_columns(go_ring, 0, local)
     expert_ring[0] = order(expert_ring[0])
+    in_w = list(order.take(*in_w))
+    in_w = across_halves(in_w, cut_in)
+    marked_other = order.take(swap(order(marked)))
+    gate_stack = stack_columns(order(go_ring), 0, local)
     in_w = order.take(*in_w, gate_stack)
     gate_stack, in_w = in_w[-1], list(in_w[:-1])
 
     gate_w = along_both(gate_stack)
     in_matrix = matrix(in_w, cut_in)
     zi, router_w = inner_product(order(normed), in_matrix, local)
-    y, states = front_scan(zi, kern, head_par, spread)
+    order.set(zi)
+    ring_on(expert_ring, order, 1, 1 + third, lines)
+    order.set(expert_ring[-1])
+    y, states = front_scan(order(zi), kern, head_par, spread)
     order.set(y)
     gate_w = list(order.take(*gate_w))
     gate_w = across_halves(gate_w, cut_gate)
     out_stack = stack_columns(order(go_ring), local, width_d)
     order.set(out_stack)
-    ring_on(expert_ring, order, 1, 1 + third, lines)
-    order.set(expert_ring[-1])
     gate_w = list(order.take(*gate_w))
     out_w = along_both(order(out_stack))
     gate_matrix = matrix(gate_w, cut_gate)
@@ -1494,10 +1634,10 @@
     order.set(gate)
     squares_other = order.take(swap(squares))
     out_w = list(order.take(*out_w))
+    ring_on(expert_ring, order, 1 + third, 1 + 2 * third, lines)
+    order.set(expert_ring[-1])
     out_w = across_halves(out_w, cut_gate)
     out_w = list(order.take(*out_w))
-    ring_on(expert_ring, order, 1 + third, 1 + 2 * third, lines)
-    order.set(expert_ring[-1])
     marked_sent = order(marked)
     marked_x, marked_y = hop(marked_sent, 1), hop(marked_sent, 2)
     out_matrix = matrix(out_w, cut_gate)
@@ -1534,9 +1674,9 @@
     mid_x, mid_y, marked_swap_x, marked_swap_y = order.take(
         mid_x, mid_y, marked_swap_x, marked_swap_y
     )
+    mid_halves = halves_of(mid_x, mid_y)
+    order.set(*mid_halves)
     mid_swap_x, mid_swap_y = order.take(swap(mid_x), swap(mid_y))
-    mid_halves = halves_of(mid_x, mid_y)
-    order.set(*mid_halves, mid_swap_x, mid_swap_y)
     mid_d, marked_d = across(order(mid_halves)), across(order(marked_halves))
     kept, result = expert_rows(
         [1, 2], order([mid_x, mid_swap_x, mid_y, mid_swap_y]),
@@ -1552,7 +1692,7 @@
         [3], [order(mid_d), mid_d_other], [marked_d, marked_d_other], kept, *common
     )
     order.set(result_3[0])
-    x_all, dy_all, gu, down = kept
+    x_all, dy_all, gate_acts, up_acts, down = kept
     d_others, d_other_0 = order.take(d_others, d_other_0)
     d_other_3 = order.take(swap(result_3[3]))
     over_low, over_high = across_sum(result_3[2], d_other_3, 0)
@@ -1572,21 +1712,21 @@
         return lambda line_at: [(width, [(arrays[name], 0, line_at)], None)]
 
     sums = LineSums(
-        {"gu": whole_block("gu", 2 * hidden), "down": whole_block("down", hidden)},
-        order, lines, GROUP * height, where,
+        {name: whole_block(name, hidden) for name in ("gate", "up", "down")},
+        order, lines, GROUP * height, where, ("gate", "up", "down"),
     )
     arrays["down"] = grad_down
-    arrays["gu"] = None
     sums.start("down")
     d_came = hop(to_x, 1), hop(to_y, 2)
     out_over = across_sum(result_3[0], order(out_other_3), 0)
     order.set(out_over[0], sums.sent)
     out_over = hop(out_over[0], 1), hop(out_over[1], 2)
-    grad_gu = tn(order(x_all), gu, BF)
-    order.set(grad_gu)
-    arrays["gu"] = grad_gu
-    sums.run(third, "gu")
+    arrays["gate"] = tn(order(x_all), gate_acts, BF)
+    order.set(arrays["gate"])
+    sums.run(third, "gate")
     order.set(sums.sent)
+    arrays["up"] = tn(order(x_all), up_acts, BF)
+    order.set(arrays["up"])
     d_came = order.take(*d_came)
     out_over = order.take(*out_over)
     out_sums = side_sums(result[0], out_others, *out_over)
@@ -1597,6 +1737,8 @@
         result_0[2], d_other_0, *d_came, order(resid), tokens, grad_out, gain_mid
     )
     order.set(d_mix_mine)
+    sums.run(third, "up")
+    order.set(sums.sent)
     d_mix_came, pulls_came = order.take(swap(d_mix_mine), swap(pulls))
     d_mix, pulls = pair_rows([(d_mix_mine, order(d_mix_came)), (pulls, pulls_came)], core_now)
     order.set(d_mix)
@@ -1604,13 +1746,14 @@
         order(d_mix), y, gate, squares, squares_other, pulls, kern, out_matrix, cut_gate, inner_all
     )
     order.set(d_y)
-    out_came = order.take(*out_came)
-
-    def hop_first(pair):
+
+    def hop_first(pair, *before):
         sent = [item.start(order) for item in pair]
         order.set(*sent)
+        for other in before:
+            all_came(other)
         for item, values in zip(pair, sent):
-            item.came = hop(values, item.bits)
+            item.came = hop(order(values), item.bits)
 
     def hop_second(pair):
         for item in pair:
@@ -1629,11 +1772,14 @@
     normed_now = order(normed)
     grad_gate_a, grad_gate_b = tn(normed_now, dz_a, BF), tn(normed_now, dz_b, BF)
     order.set(grad_gate_a, grad_gate_b, grad_out_w)
+    out_came = order.take(*out_came)
     og_pair = [
         Plane([(grad_out_w, 0, cut_gate), (grad_gate_a, 0, cut_gate)], 1, where, lines),
         Plane([(grad_out_w, 1, cut_gate), (grad_gate_b, 0, cut_gate)], 2, where, lines),
     ]
     hop_first(og_pair)
+    output = output_rows(order(result_0[0]), out_other_0, *out_came, resid)
+    order.set(output)
     sums.run(third)
     order.set(sums.sent)
     di_a, di_b, par_grads, head_grads = back_scan(
@@ -1644,39 +1790,35 @@
     grad_in_a = tn(order(normed), di_a, BF)
     start = local - cut_in
     grad_router = jnp.pad(
-        order(grad_gu[:, 2 * hidden :]).astype(F32),
+        order(arrays["up"][:, hidden:]).astype(F32),
         ((0, 0), (start, di_b.shape[1] - start - LANES)),
     )
     grad_in_b = (tn(order(normed), di_b) + grad_router).astype(BF)
     order.set(grad_in_a, grad_in_b)
     sums.run(third)
     order.set(sums.sent)
-    all_came(og_pair)
     in_pair = [
         Plane([(grad_in_a, 0, cut_in)], 1, where, lines),
         Plane([(grad_in_b, 0, grad_in_b.shape[1])], 2, where, lines),
     ]
-    hop_first(in_pair)
+    hop_first(in_pair, og_pair)
+
+    def pair_groups(pair):
+        return lambda line_at: [group for item in pair for group in item.groups(line_at)]
+
+    rest = LineSums(
+        {"og": pair_groups(og_pair), "in": pair_groups(in_pair)}, order, lines, height, where
+    )
+    rest.start("og")
+    order.set(rest.sent)
     d_sent, d_mine = normed_back(
         order([dz_a, dz_b, di_a, di_b]), [gate_matrix, in_matrix], mine_last
     )
     order.set(d_mine)
 
-    def pair_groups(pair):
-        return lambda line_at: [group for item in pair for group in item.groups(line_at)]
-
-    rest = LineSums(
-        {"og": pair_groups(og_pair), "in": pair_groups(in_pair)}, order, lines, height, where
-    )
     hop_second(in_pair)
     sums.run(third)
-    order.set(sums.final["gu"])
-    rest.start("og")
-    order.set(rest.sent)
-    to_send = member_pieces(sums.final["gu"], sums.final["down"], where, height)
-    order.set(*to_send)
-    all_came(in_pair)
-    came = to_send[:1] + [hop(order(to_send[k]), k) for k in range(1, GROUP)]
+    order.set(sums.final["up"][0])
     rest.run(third)
     order.set(rest.sent)
     d_other = order.take(swap(order(d_sent)))
@@ -1686,12 +1828,32 @@
         par_grads, head_grads, gain_grads, mid_gains, in_gains, spread, core_now, local, heads
     )
     order.set(small)
+    all_came(in_pair)
     rest.run(third, "in")
     order.set(rest.sent)
-    small = order.take(small + order(swap(small)))
-    output = output_rows(order(result_0[0]), out_other_0, *out_came, resid)
-    order.set(output)
-    small = order.take(small + order(hop(small, 1)))
+    to_send = member_pieces(
+        [
+            (arrays[name], order(sums.final[name][0]), sums.final[name][1] // hidden, hidden)
+            for name in ("gate", "up", "down")
+        ],
+        where, lines, height,
+    )
+    order.set(*to_send)
+    came = to_send[:1] + [hop(order(to_send[k]), k) for k in range(1, GROUP)]
+    small = sum_in_order([small, order(swap(small))], core_now, 2)
+    order.set(small)
+    small = sum_in_order([small] + order([hop(small, k) for k in range(1, GROUP)]), place_now, GROUP)
+    order.set(small)
+    bits = GROUP
+    while bits < lines * GROUP:
+        if 2 * bits < lines * GROUP:
+            others = order([hop(small, k * bits) for k in range(1, 4)])
+            small = sum_in_order([small] + others, (me // bits).reshape(1), 4)
+            bits *= 4
+        else:
+            small = sum_in_order([small, order(hop(small, bits))], (me // bits).reshape(1), 2)
+            bits *= 2
+        order.set(small)
     rest.run(third)
     order.set(rest.sent)
     came = list(order.take(*came))
@@ -1699,24 +1861,15 @@
     order.set(g_edown)
     rest.run(third)
     order.set(rest.sent)
-    bits = 2
-    while bits < lines * GROUP:
-        small = order.take(small + order(hop(small, bits)))
-        bits *= 2
+    g_out = out_outputs(order(rest.final["og"]), cut_gate)
+    order.set(g_out)
     rest.run(third)
-    og_held, g_inner = rest.final["og"], rest.final["in"]
-    quarters = [og_held[:, i * cut_gate : (i + 1) * cut_gate] for i in range(4)]
-    g_out = jnp.concatenate([quarters[0], quarters[2]], axis=1).T
-    g_gate = jnp.concatenate([quarters[1], quarters[3]], axis=1)
-    g_zx = jnp.stack([g_gate, g_inner[:, :local]], axis=1)
-    g_dt = g_inner[:, local : local + heads]
-    g_joint = jnp.concatenate(
-        [g_inner[:, local + heads : local + heads + EXPERTS], g_inner[:, local + LANES :]], axis=1
-    )
-    joint_rows = height // 2
-    g_joint = lax.dynamic_slice_in_dim(g_joint, core * joint_rows, joint_rows, 0) + swap(
-        lax.dynamic_slice_in_dim(g_joint, (1 - core) * joint_rows, joint_rows, 0)
-    )
+    order.set(rest.final["in"])
+    g_zx, g_dt, joint_mine, joint_sent = inner_outputs(
+        rest.final["og"], rest.final["in"], core_now, local, heads, cut_gate
+    )
+    joint = joint_mine + swap(joint_sent)
+    g_router, g_bc = joint[:, heads : heads + EXPERTS], joint[:, LANES:]
 
     def of_heads(number):
         return jnp.concatenate(
@@ -1727,9 +1880,9 @@
         )
 
     return (
-        output, grad_tokens, small[6, :width_d], g_zx, g_dt, g_joint[:, EXPERTS:], small[:4],
+        output, grad_tokens, small[6, :width_d], g_zx, g_dt, g_bc, small[:4],
         small[4], of_heads(0), of_heads(1), of_heads(2), small[5, :inner_all], g_out,
-        small[6, width_d : 2 * width_d], g_joint[:, :EXPERTS], g_sgu, g_sdown, g_egu, g_edown,
+        small[6, width_d : 2 * width_d], g_router, g_sgu, g_sdown, g_egu, g_edown,
     )
 
 

time: 970 us -> 916 us (0.944)
  waiting for transfers between devices: 217 us -> 170 us
    ppermute x46 -> x48, waiting for transfers between devices: 148 us -> 116 us  [hop(): return lax.ppermute(values, 'dp', [(i, i ^ bits) for i in range(count)])]
    pallas_call x0 -> x5, Pallas kernels: none -> 13.1 us  [the longest x3 5.14 us: sum_in_order(): pl.pallas_call(body, out_shape=jax.ShapeDtypeStruct((rows, width), F32),...]
    ppermute x21 -> x22, waiting for transfers between devices: 42.7 us -> 33.1 us  [next_line(): lax.ppermute(values, 'dp', [(i, (i + GROUP) % count) for i in range(count)])]
    pallas_call x21 -> x20, Pallas kernels: 83 us -> 76 us  [add_blocks(): pl.pallas_call(body, out_shape=jax.ShapeDtypeStruct((count * height, tota...]
    dot_general x7 -> x8, matrix products: 92.8 us -> 98.4 us  [tn(): lax.dot_general(left, right, (((0,), (0,)), ((), ())), preferred_element_...]
    ppermute x46 -> x48, starting transfers between devices: 38.1 us -> 43.3 us  [hop(): return lax.ppermute(values, 'dp', [(i, i ^ bits) for i in range(count)])]
    unnamed x163 -> x176, local copies, waits for them, and re-layouts: 29.9 us -> 34.2 us
    pallas_call x5 -> x4, Pallas kernels: 28.8 us -> 25.3 us  [rows_call(): pl.pallas_call(body, grid=(rows // tile,), out_shape=tuple((jax.ShapeDtyp...]
  transfers between devices with their start and end apart: 92 -> 95, of which waited for: 40 -> 39; matrix products, arithmetic and copies ran while one was open for 13% -> 14% of each run, Pallas kernels for 47% -> 51%
where the time goes in v3:
time: 916 us; the launch traced here: 907 us
  Pallas kernels  485 us (53%)
  waiting for transfers between devices  170 us (19%)
  matrix products  98.4 us (11%)
  starting transfers between devices  87.1 us (10%)
  local copies, waits for them, and re-layouts  51.1 us (6%)
  between operations  9.75 us (1%)
    pallas_call x3, Pallas kernels, expert_rows(): pl.pallas_call(functools.partial(expert_body, (own, units, shared, counts...  144 us
    ppermute x48, waiting for transfers between devices, hop(): return lax.ppermute(values, 'dp', [(i, i ^ bits) for i in range(count)])  116 us
    dot_general x8, matrix products, tn(): lax.dot_general(left, right, (((0,), (0,)), ((), ())), preferred_element_...  98.4 us
    pallas_call x5, Pallas kernels, gathered_call(): pl.pallas_call(whole, grid_spec=pltpu.PrefetchScalarGridSpec(num_scalar_p...  79.8 us
    pallas_call x20, Pallas kernels, add_blocks(): pl.pallas_call(body, out_shape=jax.ShapeDtypeStruct((count * height, tota...  76 us
    pallas_call x1, Pallas kernels, back_scan(): pl.pallas_call(back_body, grid=(steps,), out_shape=(jax.ShapeDtypeStruct(...  51.8 us
    pallas_call x19, Pallas kernels, small_call(): pl.pallas_call(body, out_shape=tuple((jax.ShapeDtypeStruct(shape, kind) f...  47.3 us
    ppermute x48, starting transfers between devices, hop(): return lax.ppermute(values, 'dp', [(i, i ^ bits) for i in range(count)])  43.3 us
  transfers between devices with their start and end apart: 95, of which 39 were waited for; matrix products, arithmetic and copies ran while one was open for 14% of the time, Pallas kernels for 51%

profile of v3, /device:TPU:1, one launch (start us, length us, event | category | flops | bytes accessed | tf_op | source)
XLA Modules:
  0.0 907.1 jit_solution(16948936987857157015)
XLA Ops:
  31.9 7.9 collective-permute-done.4.refs_6_
  55.7 9.0 collective-permute-done.7.refs_1_
  65.6 16.9 %collective-permute-done.11.refs_2_ = bf16[96,3456]{1,0:T(8,128)(2,1)} collective-permute-done((bf16[96,3456]{1,0:T(8,128)(2,1)S(1)}, bf16[96,3456]{1,0:T(8,128)(2,1)}, u32[]{:S(2)}, u32[]{:S(2)}) %collective-permute-start.11) | collective-permute-done | bytes 663584 | tf_op jit(solution)/shard_map/ppermute | solution.py:39
  100.5 15.7 %collective-permute-done.14.values_ref.refs_5_.refs_13_ = bf16[4,96,1920]{2,1,0:T(8,128)(2,1)S(1)} collective-permute-done((bf16[4,96,1920]{2,1,0:T(8,128)(2,1)}, bf16[4,96,1920]{2,1,0:T(8,128)(2,1)S(1)}, u32[]{:S(2)}, u32[]{:S(2)}) %collective-permute-start.14) | collective-permute-done | bytes 1474592 | tf_op jit(solution)/shard_map/ppermute | solution.py:39
  129.6 11.8 %collective-permute-done.17.refs_7_.refs_15_ = bf16[4,96,896]{2,1,0:T(8,128)(2,1)S(1)} collective-permute-done((bf16[4,96,896]{2,1,0:T(8,128)(2,1)}, bf16[4,96,896]{2,1,0:T(8,128)(2,1)S(1)}, u32[]{:S(2)}, u32[]{:S(2)}) %collective-permute-start.17) | collective-permute-done | bytes 688160 | tf_op jit(solution)/shard_map/ppermute | solution.py:39
  144.3 13.5 %inner_product.1 = (f32[1024,1920]{1,0:T(8,128)}, bf16[1536,128]{1,0:T(8,128)(2,1)}) custom-call(s32[20]{0:T(128)} %add.75.refs_0_, s32[1]{0:T(128)} %constant.53.clone.refs_1_, bf16[1024,1536]{1,0:T(8,128)(2,1)} %bitcast.92, bf16[4,96,1920]{2,1,0:T(8,128)(2,1)} %stack_pairs.1.refs_3_.refs_11_, ...), custom_call_target="tpu_custom_call" | custom-call | flops 1000 | bytes 1000 | tf_op jit(solution)/shard_map/inner_product/pallas_call | solution.py:817
  160.0 22.4 %front_scan.1 = (f32[1024,1536]{1,0:T(8,128)}, f32[8,128,1536]{2,1,0:T(8,128)}) custom-call(f32[1024,1920]{1,0:T(8,128)} %get-tuple-element.347.zi_ref.prev_ref, f32[8,1920]{1,0:T(8,128)} %get-tuple-element.326.kern_ref.refs_6_.refs_8_, f32[8,128]{1,0:T(8,128)} %get-tuple-element.348.head_ref, bf16[128,1536]{1,0:T(8,128)(2,1)} %get-tuple-element.349.spread_ref), custom_call_target="tpu_custom_call" | custom-call | flops 1000 | bytes 1000 | tf_op jit(solution)/shard_map/front_scan/pallas_call | solution.py:221
  192.1 6.1 collective-permute-done.23.refs_8_.refs_10_
  202.8 13.2 %gate_product.1 = (f32[1024,1536]{1,0:T(8,128)}, f32[1024,128]{1,0:T(8,128)}) custom-call(s32[20]{0:T(128)} %add.75.refs_0_, s32[1]{0:T(128)} %constant.53.clone.refs_1_, bf16[1024,1536]{1,0:T(8,128)(2,1)} %bitcast.93, f32[1024,1536]{1,0:T(8,128)} %get-tuple-element.377.refs_3_.refs_2_, bf16[4,96,1536]{2,1,0:T(8,128)(2,1)} %stack_columns.4.refs_4_.refs_6_, ...), custom_call_target="tpu_custom_call" | custom-call | flops 1000 | bytes 1000 | tf_op jit(solution)/shard_map/gate_product/pallas_call | solution.py:817
  233.4 6.9 collective-permute-done.28.refs_11_.refs_13_
  243.7 14.8 %mixed_product.1 = (bf16[1024,1536]{1,0:T(8,128)(2,1)}, bf16[512,1536]{1,0:T(8,128)(2,1)}, f32[512,1536]{1,0:T(8,128)}) custom-call(s32[20]{0:T(128)} %add.75.refs_0_, s32[1]{0:T(128)} %bitcast.1.refs_1_, f32[1024,1536]{1,0:T(8,128)} %get-tuple-element.377.refs_3_.refs_2_, f32[1024,1536]{1,0:T(8,128)} %get-tuple-element.366.refs_3_.refs_4_, ...), custom_call_target="tpu_custom_call" | custom-call | flops 1000 | bytes 1000 | tf_op jit(solution)/shard_map/mixed_product/pallas_call | solution.py:817
  258.6 19.1 %collective-permute-done.32.values_ref.refs_8_ = bf16[512,1664]{1,0:T(8,128)(2,1)} collective-permute-done((bf16[512,1664]{1,0:T(8,128)(2,1)}, bf16[512,1664]{1,0:T(8,128)(2,1)}, u32[]{:S(2)}, u32[]{:S(2)}) %collective-permute-start.32) | collective-permute-done | bytes 1703968 | tf_op jit(solution)/shard_map/ppermute | solution.py:39
  282.6 7.4 collective-permute-start.33
  304.4 38.9 %expert_rows.3 = (bf16[4096,1536]{1,0:T(8,128)(2,1)}, bf16[4096,1536]{1,0:T(8,128)(2,1)}, bf16[4096,1152]{1,0:T(8,128)(2,1)}, bf16[4096,1280]{1,0:T(8,128)(2,1)}...) custom-call(s32[16]{0:T(128)} %add.71.refs_0_, ...), custom_call_target="tpu_custom_call" | custom-call | flops 1000 | bytes 1000 | tf_op jit(solution)/shard_map/expert_rows/pallas_call | solution.py:1483
  352.7 66.3 %expert_rows.4 = (bf16[4096,1536]{1,0:T(8,128)(2,1)}, bf16[4096,1536]{1,0:T(8,128)(2,1)}, bf16[4096,1152]{1,0:T(8,128)(2,1)}, bf16[4096,1280]{1,0:T(8,128)(2,1)}...) custom-call(s32[16]{0:T(128)} %add.71.refs_0_, ...), custom_call_target="tpu_custom_call", output_to_operand_aliasing={{0}: (15, {}), {1}: (16, {}), {2}: (17, {}), {3}: (18, {}),... | custom-call | flops 1000 | bytes 1000 | tf_op jit(solution)/shard_map/expert_rows/pallas_call | solution.py:1483
  429.8 39.1 %expert_rows.5 = (bf16[4096,1536]{1,0:T(8,128)(2,1)}, bf16[4096,1536]{1,0:T(8,128)(2,1)}, bf16[4096,1152]{1,0:T(8,128)(2,1)}, bf16[4096,1280]{1,0:T(8,128)(2,1)}...) custom-call(s32[16]{0:T(128)} %add.71.refs_0_, ...), custom_call_target="tpu_custom_call", output_to_operand_aliasing={{0}: (15, {}), {1}: (16, {}), {2}: (17, {}), {3}: (18, {}),... | custom-call | flops 1000 | bytes 1000 | tf_op jit(solution)/shard_map/expert_rows/pallas_call | solution.py:1483
  478.4 23.0 %fusion.3.refs_0_.refs_2_ = bf16[1536,1152]{1,0:T(8,128)(2,1)} fusion(bf16[4096,1536]{1,0:T(8,128)(2,1)} %get-tuple-element.443, bf16[4096,1152]{1,0:T(8,128)(2,1)} %get-tuple-element.444), kind=kOutput, calls=%fused_computation.41 | convolution fusion | flops 14495514624 | bytes 25559040 | tf_op jit(solution)/shard_map/dot_general | solution.py:34
  516.4 23.0 %fusion.4.refs_1_.refs_0_ = bf16[1536,1152]{1,0:T(8,128)(2,1)} fusion(bf16[4096,1536]{1,0:T(8,128)(2,1)} %get-tuple-element.464, bf16[4096,1152]{1,0:T(8,128)(2,1)} %get-tuple-element.462), kind=kOutput, calls=%fused_computation.42 | convolution fusion | flops 14495514624 | bytes 25559040 | tf_op jit(solution)/shard_map/dot_general | solution.py:34
  545.6 23.3 %fusion.5.refs_2_.refs_1_.refs_0_ = bf16[1536,1280]{1,0:T(8,128)(2,1)} fusion(bf16[4096,1536]{1,0:T(8,128)(2,1)} %get-tuple-element.464, bf16[4096,1280]{1,0:T(8,128)(2,1)} %get-tuple-element.465), kind=kOutput, calls=%fused_computation.43 | convolution fusion | flops 16106127360 | bytes 27000832 | tf_op jit(solution)/shard_map/dot_general | solution.py:34
  574.6 8.7 resid_back.1
  587.9 5.2 line_step.14
  599.0 17.5 %gate_back.1 = (f32[1024,1536]{1,0:T(8,128)}, bf16[1024,768]{1,0:T(8,128)(2,1)}, bf16[1024,768]{1,0:T(8,128)(2,1)}, f32[8,1536]{1,0:T(8,128)}) custom-call(s32[20]{0:T(128)} %add.75.refs_0_, s32[1]{0:T(128)} %constant.53.clone.refs_1_, bf16[1024,1536]{1,0:T(8,128)(2,1)} %bitcast.98, f32[1024,1536]{1,0:T(8,128)} %get-tuple-element.377.refs_3_.refs_2_, ...), custom_call_target="tpu_custom_call" | custom-call | flops 1000 | bytes 1000 | tf_op jit(solution)/shard_map/gate_back/pallas_call | solution.py:817
  616.6 5.5 fusion.8.refs_1_.refs_2_.refs_9_
  622.1 6.8 fusion.6.refs_0_.refs_6_
  642.8 5.1 output_rows.1
  647.8 5.5 collective-permute-done.67.refs_2_.refs_5_
  658.3 51.8 %back_scan.1 = (bf16[1024,1024]{1,0:T(8,128)(2,1)}, bf16[1024,896]{1,0:T(8,128)(2,1)}, f32[8,1920]{1,0:T(8,128)}, f32[8,128]{1,0:T(8,128)}) custom-call(f32[1024,1536]{1,0:T(8,128)} %get-tuple-element.497.dy_ref, f32[1024,1920]{1,0:T(8,128)} %get-tuple-element.347.zi_ref.prev_ref, f32[1024,1920]{1,0:T(8,128)} %get-tuple-element.347.zi_ref.prev_ref, ...), custom_call_target="tpu_custom_call" | custom-call | flops 1000 | bytes 1000 | tf_op jit(solution)/shard_map/back_scan/pallas_call | solution.py:388
  720.8 7.7 add_convert_fusion.refs_0_.refs_15_.refs_3_
  751.7 20.7 %normed_back.1 = (bf16[512,1536]{1,0:T(8,128)(2,1)}, f32[512,1536]{1,0:T(8,128)}) custom-call(s32[20]{0:T(128)} %add.75.refs_0_, s32[1]{0:T(128)} %bitcast.1.refs_1_, bf16[1024,768]{1,0:T(8,128)(2,1)} %get-tuple-element.512.refs_2_, bf16[1024,768]{1,0:T(8,128)(2,1)} %get-tuple-element.513.refs_3_, bf16[1024,1024]{1,0:T(8,128)(2,1)} %get-tuple-element.514.refs_4_, ...), custom_call_target="tpu_custom_call" | custom-call | flops 1000 | bytes 1000 | tf_op jit(solution)/shard_map/normed_back/pallas_call | solution.py:817
  796.4 6.9 tokens_back.1
  817.6 5.1 member_pieces.1
  862.9 7.3 collective-permute-done.92.refs_3_
  (447 shorter events, 365.3 us)
Async XLA Ops:
  6.7 49.0 %collective-permute-start.8 = (bf16[512,1536]{1,0:T(8,128)(2,1)}, bf16[512,1536]{1,0:T(8,128)(2,1)}, u32[]{:S(2)}, u32[]{:S(2)}) collective-permute-start(bf16[512,1536]{1,0:T(8,128)(2,1)} %tokens_ref.5), channel_id=1, source_target_pairs={{0,1},{1,0},{2,3},{3,2},{4,5},{5,4},{6,7},{7,6},{8,9},{9,8},{10,11... | collective-permute-start | bytes 4718600 | tf_op jit(solution)/shard_map/ppermute | solution.py:48
  100.5 59.3 %collective-permute-start.19 = (bf16[4,96,3456]{2,1,0:T(8,128)(2,1)}, bf16[4,96,3456]{2,1,0:T(8,128)(2,1)S(1)}, u32[]{:S(2)}, u32[]{:S(2)}) collective-permute-start(bf16[4,96,3456]{2,1,0:T(8,128)(2,1)} %stack_columns.3.refs_7_.refs_11_), channel_id=1, source_target_pairs={{0,8},{2,10},{4,12},{6,14},{8,16},{10,18},{12,20},{14,22},{16,24},... | collective-permute-start | bytes 7962632 | tf_op jit(solution)/shard_map/ppermute | solution.py:44
  142.9 39.6 %collective-permute-start.21 = (bf16[4,96,1536]{2,1,0:T(8,128)(2,1)}, bf16[4,96,1536]{2,1,0:T(8,128)(2,1)S(1)}, u32[]{:S(2)}, u32[]{:S(2)}) collective-permute-start(bf16[4,96,1536]{2,1,0:T(8,128)(2,1)} %stack_columns.4.refs_4_.refs_6_), channel_id=1, source_target_pairs={{0,4},{2,6},{4,0},{6,2},{8,12},{10,14},{12,8},{14,10},{16,20},{18,... | collective-permute-start | bytes 3538952 | tf_op jit(solution)/shard_map/ppermute | solution.py:39
  143.8 38.6 %collective-permute-start.20 = (bf16[4,96,1536]{2,1,0:T(8,128)(2,1)}, bf16[4,96,1536]{2,1,0:T(8,128)(2,1)}, u32[]{:S(2)}, u32[]{:S(2)}) collective-permute-start(bf16[4,96,1536]{2,1,0:T(8,128)(2,1)} %stack_columns.4.refs_4_.refs_6_), channel_id=1, source_target_pairs={{0,2},{2,0},{4,6},{6,4},{8,10},{10,8},{12,14},{14,12},{16,18},{18,... | collective-permute-start | bytes 3538952 | tf_op jit(solution)/shard_map/ppermute | solution.py:39
  159.9 65.9 %collective-permute-start.29 = (bf16[4,96,3456]{2,1,0:T(8,128)(2,1)S(1)}, bf16[4,96,3456]{2,1,0:T(8,128)(2,1)}, u32[]{:S(2)}, u32[]{:S(2)}) collective-permute-start(bf16[4,96,3456]{2,1,0:T(8,128)(2,1)S(1)} %collective-permute-done.19.refs_8_.refs_12_), channel_id=1, source_target_pairs={{0,8},{2,10},{4,12},{6,14},{8,16},{10,18},{12,20},{14,22},{16,24},... | collective-permute-start | bytes 7962632 | tf_op jit(solution)/shard_map/ppermute | solution.py:44
  225.8 56.8 %collective-permute-start.30 = (bf16[4,96,3456]{2,1,0:T(8,128)(2,1)}, bf16[4,96,3456]{2,1,0:T(8,128)(2,1)S(1)}, u32[]{:S(2)}, u32[]{:S(2)}) collective-permute-start(bf16[4,96,3456]{2,1,0:T(8,128)(2,1)} %collective-permute-done.29.refs_9_.refs_13_), channel_id=1, source_target_pairs={{0,8},{2,10},{4,12},{6,14},{8,16},{10,18},{12,20},{14,22},{16,24},... | collective-permute-start | bytes 7962632 | tf_op jit(solution)/shard_map/ppermute | solution.py:44
  242.0 35.7 %collective-permute-start.32 = (bf16[512,1664]{1,0:T(8,128)(2,1)}, bf16[512,1664]{1,0:T(8,128)(2,1)}, u32[]{:S(2)}, u32[]{:S(2)}) collective-permute-start(bf16[512,1664]{1,0:T(8,128)(2,1)} %marked_rows.1.refs_4_), channel_id=1, source_target_pairs={{0,4},{2,6},{4,0},{6,2},{8,12},{10,14},{12,8},{14,10},{16,20},{18,... | collective-permute-start | bytes 5111816 | tf_op jit(solution)/shard_map/ppermute | solution.py:39
  301.6 41.8 %collective-permute-start.37 = (bf16[512,1664]{1,0:T(8,128)(2,1)}, bf16[512,1664]{1,0:T(8,128)(2,1)}, u32[]{:S(2)}, u32[]{:S(2)}) collective-permute-start(bf16[512,1664]{1,0:T(8,128)(2,1)} %collective-permute-done.31.values_ref.refs_6_), channel_id=1, source_target_pairs={{0,1},{1,0},{2,3},{3,2},{4,5},{5,4},{6,7},{7,6},{8,9},{9,8},{10,11... | collective-permute-start | bytes 5111816 | tf_op jit(solution)/shard_map/ppermute | solution.py:48
  302.0 41.4 %collective-permute-start.38 = (bf16[512,1664]{1,0:T(8,128)(2,1)}, bf16[512,1664]{1,0:T(8,128)(2,1)}, u32[]{:S(2)}, u32[]{:S(2)}) collective-permute-start(bf16[512,1664]{1,0:T(8,128)(2,1)} %collective-permute-done.32.values_ref.refs_8_), channel_id=1, source_target_pairs={{0,1},{1,0},{2,3},{3,2},{4,5},{5,4},{6,7},{7,6},{8,9},{9,8},{10,11... | collective-permute-start | bytes 5111816 | tf_op jit(solution)/shard_map/ppermute | solution.py:48
  302.8 40.6 %collective-permute-start.36 = (bf16[512,1536]{1,0:T(8,128)(2,1)}, bf16[512,1536]{1,0:T(8,128)(2,1)S(1)}, u32[]{:S(2)}, u32[]{:S(2)}) collective-permute-start(bf16[512,1536]{1,0:T(8,128)(2,1)} %get-tuple-element.388.refs_2_), channel_id=1, source_target_pairs={{0,4},{2,6},{4,0},{6,2},{8,12},{10,14},{12,8},{14,10},{16,20},{18,... | collective-permute-start | bytes 4718600 | tf_op jit(solution)/shard_map/ppermute | solution.py:39
  303.6 39.7 %collective-permute-start.35 = (bf16[512,1536]{1,0:T(8,128)(2,1)}, bf16[512,1536]{1,0:T(8,128)(2,1)S(1)}, u32[]{:S(2)}, u32[]{:S(2)}) collective-permute-start(bf16[512,1536]{1,0:T(8,128)(2,1)} %get-tuple-element.388.refs_2_), channel_id=1, source_target_pairs={{0,2},{2,0},{4,6},{6,4},{8,10},{10,8},{12,14},{14,12},{16,18},{18,... | collective-permute-start | bytes 4718600 | tf_op jit(solution)/shard_map/ppermute | solution.py:39
  349.8 69.2 %collective-permute-start.41 = (bf16[256,1664]{1,0:T(8,128)(2,1)}, bf16[256,1664]{1,0:T(8,128)(2,1)S(1)}, u32[]{:S(2)}, u32[]{:S(2)}) collective-permute-start(bf16[256,1664]{1,0:T(8,128)(2,1)} %cut_rows.4), channel_id=1, source_target_pairs={{0,4},{2,6},{4,0},{6,2},{8,12},{10,14},{12,8},{14,10},{16,20},{18,... | collective-permute-start | bytes 2555912 | tf_op jit(solution)/shard_map/ppermute | solution.py:39
  350.6 69.6 %collective-permute-start.42 = (bf16[256,1664]{1,0:T(8,128)(2,1)}, bf16[256,1664]{1,0:T(8,128)(2,1)S(1)}, u32[]{:S(2)}, u32[]{:S(2)}) collective-permute-start(bf16[256,1664]{1,0:T(8,128)(2,1)} %cut_rows.5), channel_id=1, source_target_pairs={{0,2},{2,0},{4,6},{6,4},{8,10},{10,8},{12,14},{14,12},{16,18},{18,... | collective-permute-start | bytes 2555912 | tf_op jit(solution)/shard_map/ppermute | solution.py:39
  351.1 67.9 %collective-permute-start.43 = (bf16[256,1536]{1,0:T(8,128)(2,1)}, bf16[256,1536]{1,0:T(8,128)(2,1)S(1)}, u32[]{:S(2)}, u32[]{:S(2)}) collective-permute-start(bf16[256,1536]{1,0:T(8,128)(2,1)} %cut_rows.6), channel_id=1, source_target_pairs={{0,4},{2,6},{4,0},{6,2},{8,12},{10,14},{12,8},{14,10},{16,20},{18,... | collective-permute-start | bytes 2359304 | tf_op jit(solution)/shard_map/ppermute | solution.py:39
  352.0 67.1 %collective-permute-start.44 = (bf16[256,1536]{1,0:T(8,128)(2,1)}, bf16[256,1536]{1,0:T(8,128)(2,1)S(1)}, u32[]{:S(2)}, u32[]{:S(2)}) collective-permute-start(bf16[256,1536]{1,0:T(8,128)(2,1)} %cut_rows.7), channel_id=1, source_target_pairs={{0,2},{2,0},{4,6},{6,4},{8,10},{10,8},{12,14},{14,12},{16,18},{18,... | collective-permute-start | bytes 2359304 | tf_op jit(solution)/shard_map/ppermute | solution.py:39
  429.3 40.0 %collective-permute-start.49 = (bf16[2,512,1536]{2,1,0:T(8,128)(2,1)}, bf16[2,512,1536]{2,1,0:T(8,128)(2,1)S(1)}, u32[]{:S(2)}, u32[]{:S(2)}) collective-permute-start(bf16[2,512,1536]{2,1,0:T(8,128)(2,1)} %get-tuple-element.423), channel_id=1, source_target_pairs={{0,1},{1,0},{2,3},{3,2},{4,5},{5,4},{6,7},{7,6},{8,9},{9,8},{10,11... | collective-permute-start | bytes 9437192 | tf_op jit(solution)/shard_map/ppermute | solution.py:48
  429.7 39.7 %collective-permute-start.50 = (bf16[1,512,1536]{2,1,0:T(8,128)(2,1)}, bf16[1,512,1536]{2,1,0:T(8,128)(2,1)}, u32[]{:S(2)}, u32[]{:S(2)}) collective-permute-start(bf16[1,512,1536]{2,1,0:T(8,128)(2,1)} %get-tuple-element.425), channel_id=1, source_target_pairs={{0,1},{1,0},{2,3},{3,2},{4,5},{5,4},{6,7},{7,6},{8,9},{9,8},{10,11... | collective-permute-start | bytes 4718600 | tf_op jit(solution)/shard_map/ppermute | solution.py:48
  477.8 35.4 %collective-permute-start.58 = (bf16[1,512,1536]{2,1,0:T(8,128)(2,1)}, bf16[1,512,1536]{2,1,0:T(8,128)(2,1)}, u32[]{:S(2)}, u32[]{:S(2)}) collective-permute-start(bf16[1,512,1536]{2,1,0:T(8,128)(2,1)} %get-tuple-element.455), channel_id=1, source_target_pairs={{0,1},{1,0},{2,3},{3,2},{4,5},{5,4},{6,7},{7,6},{8,9},{9,8},{10,11... | collective-permute-start | bytes 4718600 | tf_op jit(solution)/shard_map/ppermute | solution.py:48
  477.8 35.4 %collective-permute-start.57 = (bf16[2,512,1536]{2,1,0:T(8,128)(2,1)}, bf16[2,512,1536]{2,1,0:T(8,128)(2,1)}, u32[]{:S(2)}, u32[]{:S(2)}) collective-permute-start(bf16[2,512,1536]{2,1,0:T(8,128)(2,1)} %get-tuple-element.453), channel_id=1, source_target_pairs={{0,1},{1,0},{2,3},{3,2},{4,5},{5,4},{6,7},{7,6},{8,9},{9,8},{10,11... | collective-permute-start | bytes 9437192 | tf_op jit(solution)/shard_map/ppermute | solution.py:48
  504.2 35.2 %collective-permute-start.59 = (bf16[384,1152]{1,0:T(8,128)(2,1)}, bf16[384,1152]{1,0:T(8,128)(2,1)S(1)}, u32[]{:S(2)}, u32[]{:S(2)}) collective-permute-start(bf16[384,1152]{1,0:T(8,128)(2,1)} %line_step.12), channel_id=1, source_target_pairs={{0,8},{2,10},{4,12},{6,14},{8,16},{10,18},{12,20},{14,22},{16,24},... | collective-permute-start | bytes 2654216 | tf_op jit(solution)/shard_map/ppermute | solution.py:44
  511.6 57.3 %collective-permute-start.55 = (bf16[512,1536]{1,0:T(8,128)(2,1)}, bf16[512,1536]{1,0:T(8,128)(2,1)S(1)}, u32[]{:S(2)}, u32[]{:S(2)}) collective-permute-start(bf16[512,1536]{1,0:T(8,128)(2,1)} %get-tuple-element.448), channel_id=1, source_target_pairs={{0,4},{2,6},{4,0},{6,2},{8,12},{10,14},{12,8},{14,10},{16,20},{18,... | collective-permute-start | bytes 4718600 | tf_op jit(solution)/shard_map/ppermute | solution.py:39
  512.0 56.9 %collective-permute-start.54 = (bf16[512,1536]{1,0:T(8,128)(2,1)}, bf16[512,1536]{1,0:T(8,128)(2,1)}, u32[]{:S(2)}, u32[]{:S(2)}) collective-permute-start(bf16[512,1536]{1,0:T(8,128)(2,1)} %get-tuple-element.447), channel_id=1, source_target_pairs={{0,2},{2,0},{4,6},{6,4},{8,10},{10,8},{12,14},{14,12},{16,18},{18,... | collective-permute-start | bytes 4718600 | tf_op jit(solution)/shard_map/ppermute | solution.py:39
  516.1 52.8 %collective-permute-start.60 = (bf16[256,1536]{1,0:T(8,128)(2,1)}, bf16[256,1536]{1,0:T(8,128)(2,1)S(1)}, u32[]{:S(2)}, u32[]{:S(2)}) collective-permute-start(bf16[256,1536]{1,0:T(8,128)(2,1)} %get-tuple-element.460), channel_id=1, source_target_pairs={{0,2},{2,0},{4,6},{6,4},{8,10},{10,8},{12,14},{14,12},{16,18},{18,... | collective-permute-start | bytes 2359304 | tf_op jit(solution)/shard_map/ppermute | solution.py:39
  544.4 42.3 %collective-permute-start.64 = (bf16[384,2304]{1,0:T(8,128)(2,1)}, bf16[384,2304]{1,0:T(8,128)(2,1)S(1)}, u32[]{:S(2)}, u32[]{:S(2)}) collective-permute-start(bf16[384,2304]{1,0:T(8,128)(2,1)} %line_step.13), channel_id=1, source_target_pairs={{0,8},{2,10},{4,12},{6,14},{8,16},{10,18},{12,20},{14,22},{16,24},... | collective-permute-start | bytes 5308424 | tf_op jit(solution)/shard_map/ppermute | solution.py:44
  585.1 47.9 %collective-permute-start.65 = (bf16[512,1536]{1,0:T(8,128)(2,1)}, bf16[512,1536]{1,0:T(8,128)(2,1)}, u32[]{:S(2)}, u32[]{:S(2)}) collective-permute-start(bf16[512,1536]{1,0:T(8,128)(2,1)} %get-tuple-element.472), channel_id=1, source_target_pairs={{0,2},{2,0},{4,6},{6,4},{8,10},{10,8},{12,14},{14,12},{16,18},{18,... | collective-permute-start | bytes 4718600 | tf_op jit(solution)/shard_map/ppermute | solution.py:39
  586.5 46.5 %collective-permute-start.66 = (bf16[512,1536]{1,0:T(8,128)(2,1)}, bf16[512,1536]{1,0:T(8,128)(2,1)}, u32[]{:S(2)}, u32[]{:S(2)}) collective-permute-start(bf16[512,1536]{1,0:T(8,128)(2,1)} %get-tuple-element.486), channel_id=1, source_target_pairs={{0,4},{2,6},{4,0},{6,2},{8,12},{10,14},{12,8},{14,10},{16,20},{18,... | collective-permute-start | bytes 4718600 | tf_op jit(solution)/shard_map/ppermute | solution.py:39
  593.1 60.2 %collective-permute-start.67 = (bf16[384,3456]{1,0:T(8,128)(2,1)}, bf16[384,3456]{1,0:T(8,128)(2,1)}, u32[]{:S(2)}, u32[]{:S(2)}) collective-permute-start(bf16[384,3456]{1,0:T(8,128)(2,1)} %line_step.14), channel_id=1, source_target_pairs={{0,8},{2,10},{4,12},{6,14},{8,16},{10,18},{12,20},{14,22},{16,24},... | collective-permute-start | bytes 7962632 | tf_op jit(solution)/shard_map/ppermute | solution.py:44
  641.3 68.8 %collective-permute-start.68 = (bf16[768,1536]{1,0:T(8,128)(2,1)}, bf16[768,1536]{1,0:T(8,128)(2,1)S(1)}, u32[]{:S(2)}, u32[]{:S(2)}) collective-permute-start(bf16[768,1536]{1,0:T(8,128)(2,1)} %plane_start.4), channel_id=1, source_target_pairs={{0,2},{2,0},{4,6},{6,4},{8,10},{10,8},{12,14},{14,12},{16,18},{18,... | collective-permute-start | bytes 7077896 | tf_op jit(solution)/shard_map/ppermute | solution.py:39
  642.5 72.9 %collective-permute-start.70 = (bf16[768,1536]{1,0:T(8,128)(2,1)}, bf16[768,1536]{1,0:T(8,128)(2,1)}, u32[]{:S(2)}, u32[]{:S(2)}) collective-permute-start(bf16[768,1536]{1,0:T(8,128)(2,1)} %plane_start.5), channel_id=1, source_target_pairs={{0,4},{2,6},{4,0},{6,2},{8,12},{10,14},{12,8},{14,10},{16,20},{18,... | collective-permute-start | bytes 7077896 | tf_op jit(solution)/shard_map/ppermute | solution.py:39
  658.2 75.3 %collective-permute-start.71 = (bf16[384,2304]{1,0:T(8,128)(2,1)}, bf16[384,2304]{1,0:T(8,128)(2,1)}, u32[]{:S(2)}, u32[]{:S(2)}) collective-permute-start(bf16[384,2304]{1,0:T(8,128)(2,1)} %line_step.15), channel_id=1, source_target_pairs={{0,8},{2,10},{4,12},{6,14},{8,16},{10,18},{12,20},{14,22},{16,24},... | collective-permute-start | bytes 5308424 | tf_op jit(solution)/shard_map/ppermute | solution.py:44
  747.4 35.9 %collective-permute-start.74 = (bf16[384,1152]{1,0:T(8,128)(2,1)}, bf16[384,1152]{1,0:T(8,128)(2,1)}, u32[]{:S(2)}, u32[]{:S(2)}) collective-permute-start(bf16[384,1152]{1,0:T(8,128)(2,1)} %line_step.16), channel_id=1, source_target_pairs={{0,8},{2,10},{4,12},{6,14},{8,16},{10,18},{12,20},{14,22},{16,24},... | collective-permute-start | bytes 2654216 | tf_op jit(solution)/shard_map/ppermute | solution.py:44
  816.5 40.4 %collective-permute-start.88 = (bf16[96,4992]{1,0:T(8,128)(2,1)}, bf16[96,4992]{1,0:T(8,128)(2,1)S(1)}, u32[]{:S(2)}, u32[]{:S(2)}) collective-permute-start(bf16[96,4992]{1,0:T(8,128)(2,1)} %line_step.19), channel_id=1, source_target_pairs={{0,8},{2,10},{4,12},{6,14},{8,16},{10,18},{12,20},{14,22},{16,24},... | collective-permute-start | bytes 2875400 | tf_op jit(solution)/shard_map/ppermute | solution.py:44
  (144 other events, 1503.0 us)

commit v4 on v3

--- a/solution.py
+++ b/solution.py
@@ -1546,24 +1546,26 @@
     pad = jnp.zeros((height, LANES - heads - EXPERTS), BF)
     ring_b = [jnp.concatenate([w_zx[:, 1, cut_in:], w_dt, router_cols, pad, bc_cols], axis=1)]
     order.set(ring_b[0])
+    ring_on(ring_a, order, 1, 1 + third, lines)
+    order.set(ring_a[-1])
     shared_units = shared_gu.shape[2] // GROUP
     hidden = own * units + shared_units
     gu = order(expert_gu).reshape(GROUP, own, height, 2, units).transpose(0, 2, 3, 1, 4)
     gu = gu.reshape(GROUP, height, 2, own * units)
-    order.set(
-        gu, gain_in, gain_mid, where, base, mine_last, place_now, core_now, mixer_targets,
-        expert_targets,
-    )
-    ring_on(ring_a, order, 1, 1 + third, lines)
+    order.set(gu)
     ring_on(ring_b, order, 1, 1 + third, lines)
+    ring_on(ring_a, order, 1 + third, 1 + 2 * third, lines)
     order.set(ring_a[-1], ring_b[-1])
     down = order(expert_down).reshape(GROUP, own, units, height).transpose(0, 3, 1, 2)
     down = down.reshape(GROUP, height, own * units)
     sgu = order(shared_gu).reshape(height, 2, GROUP, shared_units).transpose(2, 0, 1, 3)
     sdown = order(shared_down).reshape(GROUP, shared_units, height).transpose(0, 2, 1)
-    order.set(down, sgu, sdown)
-    ring_on(ring_a, order, 1 + third, 1 + 2 * third, lines)
+    order.set(
+        down, sgu, sdown, gain_in, gain_mid, where, base, mine_last, place_now, core_now,
+        mixer_targets, expert_targets,
+    )
     ring_on(ring_b, order, 1 + third, 1 + 2 * third, lines)
+    ring_on(ring_a, order, 1 + 2 * third, lines, lines)
     order.set(ring_a[-1], ring_b[-1])
     gu, sgu, down, sdown = order((gu, sgu, down, sdown))
     packed = jnp.concatenate([gu[:, :, 0], sgu[:, :, 0], gu[:, :, 1], sgu[:, :, 1], down, sdown], axis=2)
@@ -1572,7 +1574,6 @@
     came = to_send[:1] + [hop(to_send[k], k) for k in range(1, GROUP)]
     go_block = order(jnp.concatenate([w_zx[:, 0], w_out.T], axis=1))
     order.set(go_block)
-    ring_on(ring_a, order, 1 + 2 * third, lines, lines)
     ring_on(ring_b, order, 1 + 2 * third, lines, lines)
     order.set(ring_a[-1], ring_b[-1])
 

time: 916 us -> 910 us (level)
    unnamed x176 -> x174, local copies, waits for them, and re-layouts: 34.2 us -> 34.3 us
  transfers between devices with their start and end apart: 95 -> 95, of which waited for: 39 -> 40; matrix products, arithmetic and copies ran while one was open for 14% -> 14% of each run, Pallas kernels for 51% -> 51%
where the time goes in v4:
time: 910 us; the launch traced here: 900 us
  Pallas kernels  485 us (53%)
  waiting for transfers between devices  161 us (18%)
  matrix products  98.5 us (11%)
  starting transfers between devices  89.4 us (10%)
  local copies, waits for them, and re-layouts  51.1 us (6%)
  between operations  9.72 us (1%)
    pallas_call x3, Pallas kernels, expert_rows(): pl.pallas_call(functools.partial(expert_body, (own, units, shared, counts...  144 us
    ppermute x48, waiting for transfers between devices, hop(): return lax.ppermute(values, 'dp', [(i, i ^ bits) for i in range(count)])  116 us
    dot_general x8, matrix products, tn(): lax.dot_general(left, right, (((0,), (0,)), ((), ())), preferred_element_...  98.5 us
    pallas_call x5, Pallas kernels, gathered_call(): pl.pallas_call(whole, grid_spec=pltpu.PrefetchScalarGridSpec(num_scalar_p...  79.8 us
    pallas_call x20, Pallas kernels, add_blocks(): pl.pallas_call(body, out_shape=jax.ShapeDtypeStruct((count * height, tota...  76 us
    pallas_call x1, Pallas kernels, back_scan(): pl.pallas_call(back_body, grid=(steps,), out_shape=(jax.ShapeDtypeStruct(...  51.8 us
    pallas_call x19, Pallas kernels, small_call(): pl.pallas_call(body, out_shape=tuple((jax.ShapeDtypeStruct(shape, kind) f...  47.4 us
    ppermute x48, starting transfers between devices, hop(): return lax.ppermute(values, 'dp', [(i, i ^ bits) for i in range(count)])  43.7 us
  transfers between devices with their start and end apart: 95, of which 40 were waited for; matrix products, arithmetic and copies ran while one was open for 14% of the time, Pallas kernels for 51%

profile of v4, /device:TPU:1, one launch (start us, length us, event | category | flops | bytes accessed | tf_op | source)
XLA Modules:
  0.0 900.5 jit_solution(16203860670503759628)
XLA Ops:
  49.0 8.1 collective-permute-done.7.refs_1_
  58.0 17.7 %collective-permute-done.11.refs_2_ = bf16[96,3456]{1,0:T(8,128)(2,1)} collective-permute-done((bf16[96,3456]{1,0:T(8,128)(2,1)S(1)}, bf16[96,3456]{1,0:T(8,128)(2,1)}, u32[]{:S(2)}, u32[]{:S(2)}) %collective-permute-start.11) | collective-permute-done | bytes 663584 | tf_op jit(solution)/shard_map/ppermute | solution.py:39
  95.3 14.1 %collective-permute-done.14.values_ref.refs_5_.refs_13_ = bf16[4,96,1920]{2,1,0:T(8,128)(2,1)S(1)} collective-permute-done((bf16[4,96,1920]{2,1,0:T(8,128)(2,1)}, bf16[4,96,1920]{2,1,0:T(8,128)(2,1)S(1)}, u32[]{:S(2)}, u32[]{:S(2)}) %collective-permute-start.14) | collective-permute-done | bytes 1474592 | tf_op jit(solution)/shard_map/ppermute | solution.py:39
  122.9 11.8 %collective-permute-done.17.refs_7_.refs_15_ = bf16[4,96,896]{2,1,0:T(8,128)(2,1)S(1)} collective-permute-done((bf16[4,96,896]{2,1,0:T(8,128)(2,1)}, bf16[4,96,896]{2,1,0:T(8,128)(2,1)S(1)}, u32[]{:S(2)}, u32[]{:S(2)}) %collective-permute-start.17) | collective-permute-done | bytes 688160 | tf_op jit(solution)/shard_map/ppermute | solution.py:39
  137.6 13.5 %inner_product.1 = (f32[1024,1920]{1,0:T(8,128)}, bf16[1536,128]{1,0:T(8,128)(2,1)}) custom-call(s32[20]{0:T(128)} %add.75.refs_0_, s32[1]{0:T(128)} %constant.53.clone.refs_1_, bf16[1024,1536]{1,0:T(8,128)(2,1)} %bitcast.92, bf16[4,96,1920]{2,1,0:T(8,128)(2,1)} %stack_pairs.1.refs_3_.refs_11_, ...), custom_call_target="tpu_custom_call" | custom-call | flops 1000 | bytes 1000 | tf_op jit(solution)/shard_map/inner_product/pallas_call | solution.py:817
  153.5 22.4 %front_scan.1 = (f32[1024,1536]{1,0:T(8,128)}, f32[8,128,1536]{2,1,0:T(8,128)}) custom-call(f32[1024,1920]{1,0:T(8,128)} %get-tuple-element.347.zi_ref.prev_ref, f32[8,1920]{1,0:T(8,128)} %get-tuple-element.326.kern_ref.refs_6_.refs_8_, f32[8,128]{1,0:T(8,128)} %get-tuple-element.348.head_ref, bf16[128,1536]{1,0:T(8,128)(2,1)} %get-tuple-element.349.spread_ref), custom_call_target="tpu_custom_call" | custom-call | flops 1000 | bytes 1000 | tf_op jit(solution)/shard_map/front_scan/pallas_call | solution.py:221
  185.9 6.2 collective-permute-done.23.refs_8_.refs_10_
  196.8 13.3 %gate_product.1 = (f32[1024,1536]{1,0:T(8,128)}, f32[1024,128]{1,0:T(8,128)}) custom-call(s32[20]{0:T(128)} %add.75.refs_0_, s32[1]{0:T(128)} %constant.53.clone.refs_1_, bf16[1024,1536]{1,0:T(8,128)(2,1)} %bitcast.93, f32[1024,1536]{1,0:T(8,128)} %get-tuple-element.377.refs_3_.refs_2_, bf16[4,96,1536]{2,1,0:T(8,128)(2,1)} %stack_columns.4.refs_4_.refs_6_, ...), custom_call_target="tpu_custom_call" | custom-call | flops 1000 | bytes 1000 | tf_op jit(solution)/shard_map/gate_product/pallas_call | solution.py:817
  226.7 6.9 collective-permute-done.28.refs_11_.refs_13_
  237.1 14.8 %mixed_product.1 = (bf16[1024,1536]{1,0:T(8,128)(2,1)}, bf16[512,1536]{1,0:T(8,128)(2,1)}, f32[512,1536]{1,0:T(8,128)}) custom-call(s32[20]{0:T(128)} %add.75.refs_0_, s32[1]{0:T(128)} %bitcast.1.refs_1_, f32[1024,1536]{1,0:T(8,128)} %get-tuple-element.377.refs_3_.refs_2_, f32[1024,1536]{1,0:T(8,128)} %get-tuple-element.366.refs_3_.refs_4_, ...), custom_call_target="tpu_custom_call" | custom-call | flops 1000 | bytes 1000 | tf_op jit(solution)/shard_map/mixed_product/pallas_call | solution.py:817
  251.9 19.1 %collective-permute-done.32.values_ref.refs_8_ = bf16[512,1664]{1,0:T(8,128)(2,1)} collective-permute-done((bf16[512,1664]{1,0:T(8,128)(2,1)}, bf16[512,1664]{1,0:T(8,128)(2,1)}, u32[]{:S(2)}, u32[]{:S(2)}) %collective-permute-start.32) | collective-permute-done | bytes 1703968 | tf_op jit(solution)/shard_map/ppermute | solution.py:39
  276.5 6.8 collective-permute-start.33
  297.7 38.9 %expert_rows.3 = (bf16[4096,1536]{1,0:T(8,128)(2,1)}, bf16[4096,1536]{1,0:T(8,128)(2,1)}, bf16[4096,1152]{1,0:T(8,128)(2,1)}, bf16[4096,1280]{1,0:T(8,128)(2,1)}...) custom-call(s32[16]{0:T(128)} %add.71.refs_0_, ...), custom_call_target="tpu_custom_call" | custom-call | flops 1000 | bytes 1000 | tf_op jit(solution)/shard_map/expert_rows/pallas_call | solution.py:1483
  346.1 66.3 %expert_rows.4 = (bf16[4096,1536]{1,0:T(8,128)(2,1)}, bf16[4096,1536]{1,0:T(8,128)(2,1)}, bf16[4096,1152]{1,0:T(8,128)(2,1)}, bf16[4096,1280]{1,0:T(8,128)(2,1)}...) custom-call(s32[16]{0:T(128)} %add.71.refs_0_, ...), custom_call_target="tpu_custom_call", output_to_operand_aliasing={{0}: (15, {}), {1}: (16, {}), {2}: (17, {}), {3}: (18, {}),... | custom-call | flops 1000 | bytes 1000 | tf_op jit(solution)/shard_map/expert_rows/pallas_call | solution.py:1483
  423.1 39.1 %expert_rows.5 = (bf16[4096,1536]{1,0:T(8,128)(2,1)}, bf16[4096,1536]{1,0:T(8,128)(2,1)}, bf16[4096,1152]{1,0:T(8,128)(2,1)}, bf16[4096,1280]{1,0:T(8,128)(2,1)}...) custom-call(s32[16]{0:T(128)} %add.71.refs_0_, ...), custom_call_target="tpu_custom_call", output_to_operand_aliasing={{0}: (15, {}), {1}: (16, {}), {2}: (17, {}), {3}: (18, {}),... | custom-call | flops 1000 | bytes 1000 | tf_op jit(solution)/shard_map/expert_rows/pallas_call | solution.py:1483
  471.6 23.0 %fusion.3.refs_0_.refs_2_ = bf16[1536,1152]{1,0:T(8,128)(2,1)} fusion(bf16[4096,1536]{1,0:T(8,128)(2,1)} %get-tuple-element.443, bf16[4096,1152]{1,0:T(8,128)(2,1)} %get-tuple-element.444), kind=kOutput, calls=%fused_computation.41 | convolution fusion | flops 14495514624 | bytes 25559040 | tf_op jit(solution)/shard_map/dot_general | solution.py:34
  500.1 4.9 side_sums.2
  509.7 23.0 %fusion.4.refs_1_.refs_0_ = bf16[1536,1152]{1,0:T(8,128)(2,1)} fusion(bf16[4096,1536]{1,0:T(8,128)(2,1)} %get-tuple-element.464, bf16[4096,1152]{1,0:T(8,128)(2,1)} %get-tuple-element.462), kind=kOutput, calls=%fused_computation.42 | convolution fusion | flops 14495514624 | bytes 25559040 | tf_op jit(solution)/shard_map/dot_general | solution.py:34
  538.9 23.3 %fusion.5.refs_2_.refs_1_.refs_0_ = bf16[1536,1280]{1,0:T(8,128)(2,1)} fusion(bf16[4096,1536]{1,0:T(8,128)(2,1)} %get-tuple-element.464, bf16[4096,1280]{1,0:T(8,128)(2,1)} %get-tuple-element.465), kind=kOutput, calls=%fused_computation.43 | convolution fusion | flops 16106127360 | bytes 27000832 | tf_op jit(solution)/shard_map/dot_general | solution.py:34
  568.0 8.7 resid_back.1
  581.2 5.2 line_step.14
  593.5 17.5 %gate_back.1 = (f32[1024,1536]{1,0:T(8,128)}, bf16[1024,768]{1,0:T(8,128)(2,1)}, bf16[1024,768]{1,0:T(8,128)(2,1)}, f32[8,1536]{1,0:T(8,128)}) custom-call(s32[20]{0:T(128)} %add.75.refs_0_, s32[1]{0:T(128)} %constant.53.clone.refs_1_, bf16[1024,1536]{1,0:T(8,128)(2,1)} %bitcast.98, f32[1024,1536]{1,0:T(8,128)} %get-tuple-element.377.refs_3_.refs_2_, ...), custom_call_target="tpu_custom_call" | custom-call | flops 1000 | bytes 1000 | tf_op jit(solution)/shard_map/gate_back/pallas_call | solution.py:817
  611.0 5.5 fusion.8.refs_1_.refs_2_.refs_9_
  616.6 6.9 fusion.6.refs_0_.refs_6_
  637.3 5.1 output_rows.1
  651.6 51.8 %back_scan.1 = (bf16[1024,1024]{1,0:T(8,128)(2,1)}, bf16[1024,896]{1,0:T(8,128)(2,1)}, f32[8,1920]{1,0:T(8,128)}, f32[8,128]{1,0:T(8,128)}) custom-call(f32[1024,1536]{1,0:T(8,128)} %get-tuple-element.497.dy_ref, f32[1024,1920]{1,0:T(8,128)} %get-tuple-element.347.zi_ref.prev_ref, f32[1024,1920]{1,0:T(8,128)} %get-tuple-element.347.zi_ref.prev_ref, ...), custom_call_target="tpu_custom_call" | custom-call | flops 1000 | bytes 1000 | tf_op jit(solution)/shard_map/back_scan/pallas_call | solution.py:388
  714.2 7.7 add_convert_fusion.refs_0_.refs_15_.refs_3_
  721.8 5.1 fusion.9.refs_0_.refs_12_
  745.1 20.7 %normed_back.1 = (bf16[512,1536]{1,0:T(8,128)(2,1)}, f32[512,1536]{1,0:T(8,128)}) custom-call(s32[20]{0:T(128)} %add.75.refs_0_, s32[1]{0:T(128)} %bitcast.1.refs_1_, bf16[1024,768]{1,0:T(8,128)(2,1)} %get-tuple-element.512.refs_2_, bf16[1024,768]{1,0:T(8,128)(2,1)} %get-tuple-element.513.refs_3_, bf16[1024,1024]{1,0:T(8,128)(2,1)} %get-tuple-element.514.refs_4_, ...), custom_call_target="tpu_custom_call" | custom-call | flops 1000 | bytes 1000 | tf_op jit(solution)/shard_map/normed_back/pallas_call | solution.py:817
  789.8 6.9 tokens_back.1
  811.0 5.0 member_pieces.1
  856.3 7.3 collective-permute-done.92.refs_3_
  (445 shorter events, 364.2 us)
Async XLA Ops:
  6.7 42.2 %collective-permute-start.8 = (bf16[512,1536]{1,0:T(8,128)(2,1)}, bf16[512,1536]{1,0:T(8,128)(2,1)}, u32[]{:S(2)}, u32[]{:S(2)}) collective-permute-start(bf16[512,1536]{1,0:T(8,128)(2,1)} %tokens_ref.5), channel_id=1, source_target_pairs={{0,1},{1,0},{2,3},{3,2},{4,5},{5,4},{6,7},{7,6},{8,9},{9,8},{10,11... | collective-permute-start | bytes 4718600 | tf_op jit(solution)/shard_map/ppermute | solution.py:48
  94.0 59.3 %collective-permute-start.19 = (bf16[4,96,3456]{2,1,0:T(8,128)(2,1)}, bf16[4,96,3456]{2,1,0:T(8,128)(2,1)S(1)}, u32[]{:S(2)}, u32[]{:S(2)}) collective-permute-start(bf16[4,96,3456]{2,1,0:T(8,128)(2,1)} %stack_columns.3.refs_7_.refs_11_), channel_id=1, source_target_pairs={{0,8},{2,10},{4,12},{6,14},{8,16},{10,18},{12,20},{14,22},{16,24},... | collective-permute-start | bytes 7962632 | tf_op jit(solution)/shard_map/ppermute | solution.py:44
  136.1 39.8 %collective-permute-start.21 = (bf16[4,96,1536]{2,1,0:T(8,128)(2,1)}, bf16[4,96,1536]{2,1,0:T(8,128)(2,1)S(1)}, u32[]{:S(2)}, u32[]{:S(2)}) collective-permute-start(bf16[4,96,1536]{2,1,0:T(8,128)(2,1)} %stack_columns.4.refs_4_.refs_6_), channel_id=1, source_target_pairs={{0,4},{2,6},{4,0},{6,2},{8,12},{10,14},{12,8},{14,10},{16,20},{18,... | collective-permute-start | bytes 3538952 | tf_op jit(solution)/shard_map/ppermute | solution.py:39
  137.1 38.8 %collective-permute-start.20 = (bf16[4,96,1536]{2,1,0:T(8,128)(2,1)}, bf16[4,96,1536]{2,1,0:T(8,128)(2,1)}, u32[]{:S(2)}, u32[]{:S(2)}) collective-permute-start(bf16[4,96,1536]{2,1,0:T(8,128)(2,1)} %stack_columns.4.refs_4_.refs_6_), channel_id=1, source_target_pairs={{0,2},{2,0},{4,6},{6,4},{8,10},{10,8},{12,14},{14,12},{16,18},{18,... | collective-permute-start | bytes 3538952 | tf_op jit(solution)/shard_map/ppermute | solution.py:39
  153.3 66.5 %collective-permute-start.29 = (bf16[4,96,3456]{2,1,0:T(8,128)(2,1)S(1)}, bf16[4,96,3456]{2,1,0:T(8,128)(2,1)}, u32[]{:S(2)}, u32[]{:S(2)}) collective-permute-start(bf16[4,96,3456]{2,1,0:T(8,128)(2,1)S(1)} %collective-permute-done.19.refs_8_.refs_12_), channel_id=1, source_target_pairs={{0,8},{2,10},{4,12},{6,14},{8,16},{10,18},{12,20},{14,22},{16,24},... | collective-permute-start | bytes 7962632 | tf_op jit(solution)/shard_map/ppermute | solution.py:44
  219.8 56.7 %collective-permute-start.30 = (bf16[4,96,3456]{2,1,0:T(8,128)(2,1)}, bf16[4,96,3456]{2,1,0:T(8,128)(2,1)S(1)}, u32[]{:S(2)}, u32[]{:S(2)}) collective-permute-start(bf16[4,96,3456]{2,1,0:T(8,128)(2,1)} %collective-permute-done.29.refs_9_.refs_13_), channel_id=1, source_target_pairs={{0,8},{2,10},{4,12},{6,14},{8,16},{10,18},{12,20},{14,22},{16,24},... | collective-permute-start | bytes 7962632 | tf_op jit(solution)/shard_map/ppermute | solution.py:44
  235.3 35.7 %collective-permute-start.32 = (bf16[512,1664]{1,0:T(8,128)(2,1)}, bf16[512,1664]{1,0:T(8,128)(2,1)}, u32[]{:S(2)}, u32[]{:S(2)}) collective-permute-start(bf16[512,1664]{1,0:T(8,128)(2,1)} %marked_rows.1.refs_4_), channel_id=1, source_target_pairs={{0,4},{2,6},{4,0},{6,2},{8,12},{10,14},{12,8},{14,10},{16,20},{18,... | collective-permute-start | bytes 5111816 | tf_op jit(solution)/shard_map/ppermute | solution.py:39
  294.9 41.8 %collective-permute-start.37 = (bf16[512,1664]{1,0:T(8,128)(2,1)}, bf16[512,1664]{1,0:T(8,128)(2,1)}, u32[]{:S(2)}, u32[]{:S(2)}) collective-permute-start(bf16[512,1664]{1,0:T(8,128)(2,1)} %collective-permute-done.31.values_ref.refs_6_), channel_id=1, source_target_pairs={{0,1},{1,0},{2,3},{3,2},{4,5},{5,4},{6,7},{7,6},{8,9},{9,8},{10,11... | collective-permute-start | bytes 5111816 | tf_op jit(solution)/shard_map/ppermute | solution.py:48
  295.3 41.4 %collective-permute-start.38 = (bf16[512,1664]{1,0:T(8,128)(2,1)}, bf16[512,1664]{1,0:T(8,128)(2,1)}, u32[]{:S(2)}, u32[]{:S(2)}) collective-permute-start(bf16[512,1664]{1,0:T(8,128)(2,1)} %collective-permute-done.32.values_ref.refs_8_), channel_id=1, source_target_pairs={{0,1},{1,0},{2,3},{3,2},{4,5},{5,4},{6,7},{7,6},{8,9},{9,8},{10,11... | collective-permute-start | bytes 5111816 | tf_op jit(solution)/shard_map/ppermute | solution.py:48
  296.1 40.6 %collective-permute-start.36 = (bf16[512,1536]{1,0:T(8,128)(2,1)}, bf16[512,1536]{1,0:T(8,128)(2,1)S(1)}, u32[]{:S(2)}, u32[]{:S(2)}) collective-permute-start(bf16[512,1536]{1,0:T(8,128)(2,1)} %get-tuple-element.388.refs_2_), channel_id=1, source_target_pairs={{0,4},{2,6},{4,0},{6,2},{8,12},{10,14},{12,8},{14,10},{16,20},{18,... | collective-permute-start | bytes 4718600 | tf_op jit(solution)/shard_map/ppermute | solution.py:39
  296.9 39.8 %collective-permute-start.35 = (bf16[512,1536]{1,0:T(8,128)(2,1)}, bf16[512,1536]{1,0:T(8,128)(2,1)S(1)}, u32[]{:S(2)}, u32[]{:S(2)}) collective-permute-start(bf16[512,1536]{1,0:T(8,128)(2,1)} %get-tuple-element.388.refs_2_), channel_id=1, source_target_pairs={{0,2},{2,0},{4,6},{6,4},{8,10},{10,8},{12,14},{14,12},{16,18},{18,... | collective-permute-start | bytes 4718600 | tf_op jit(solution)/shard_map/ppermute | solution.py:39
  343.1 69.3 %collective-permute-start.41 = (bf16[256,1664]{1,0:T(8,128)(2,1)}, bf16[256,1664]{1,0:T(8,128)(2,1)S(1)}, u32[]{:S(2)}, u32[]{:S(2)}) collective-permute-start(bf16[256,1664]{1,0:T(8,128)(2,1)} %cut_rows.4), channel_id=1, source_target_pairs={{0,4},{2,6},{4,0},{6,2},{8,12},{10,14},{12,8},{14,10},{16,20},{18,... | collective-permute-start | bytes 2555912 | tf_op jit(solution)/shard_map/ppermute | solution.py:39
  343.9 69.6 %collective-permute-start.42 = (bf16[256,1664]{1,0:T(8,128)(2,1)}, bf16[256,1664]{1,0:T(8,128)(2,1)S(1)}, u32[]{:S(2)}, u32[]{:S(2)}) collective-permute-start(bf16[256,1664]{1,0:T(8,128)(2,1)} %cut_rows.5), channel_id=1, source_target_pairs={{0,2},{2,0},{4,6},{6,4},{8,10},{10,8},{12,14},{14,12},{16,18},{18,... | collective-permute-start | bytes 2555912 | tf_op jit(solution)/shard_map/ppermute | solution.py:39
  344.4 68.0 %collective-permute-start.43 = (bf16[256,1536]{1,0:T(8,128)(2,1)}, bf16[256,1536]{1,0:T(8,128)(2,1)S(1)}, u32[]{:S(2)}, u32[]{:S(2)}) collective-permute-start(bf16[256,1536]{1,0:T(8,128)(2,1)} %cut_rows.6), channel_id=1, source_target_pairs={{0,4},{2,6},{4,0},{6,2},{8,12},{10,14},{12,8},{14,10},{16,20},{18,... | collective-permute-start | bytes 2359304 | tf_op jit(solution)/shard_map/ppermute | solution.py:39
  345.3 67.1 %collective-permute-start.44 = (bf16[256,1536]{1,0:T(8,128)(2,1)}, bf16[256,1536]{1,0:T(8,128)(2,1)S(1)}, u32[]{:S(2)}, u32[]{:S(2)}) collective-permute-start(bf16[256,1536]{1,0:T(8,128)(2,1)} %cut_rows.7), channel_id=1, source_target_pairs={{0,2},{2,0},{4,6},{6,4},{8,10},{10,8},{12,14},{14,12},{16,18},{18,... | collective-permute-start | bytes 2359304 | tf_op jit(solution)/shard_map/ppermute | solution.py:39
  422.6 40.0 %collective-permute-start.49 = (bf16[2,512,1536]{2,1,0:T(8,128)(2,1)}, bf16[2,512,1536]{2,1,0:T(8,128)(2,1)S(1)}, u32[]{:S(2)}, u32[]{:S(2)}) collective-permute-start(bf16[2,512,1536]{2,1,0:T(8,128)(2,1)} %get-tuple-element.423), channel_id=1, source_target_pairs={{0,1},{1,0},{2,3},{3,2},{4,5},{5,4},{6,7},{7,6},{8,9},{9,8},{10,11... | collective-permute-start | bytes 9437192 | tf_op jit(solution)/shard_map/ppermute | solution.py:48
  423.0 39.7 %collective-permute-start.50 = (bf16[1,512,1536]{2,1,0:T(8,128)(2,1)}, bf16[1,512,1536]{2,1,0:T(8,128)(2,1)}, u32[]{:S(2)}, u32[]{:S(2)}) collective-permute-start(bf16[1,512,1536]{2,1,0:T(8,128)(2,1)} %get-tuple-element.425), channel_id=1, source_target_pairs={{0,1},{1,0},{2,3},{3,2},{4,5},{5,4},{6,7},{7,6},{8,9},{9,8},{10,11... | collective-permute-start | bytes 4718600 | tf_op jit(solution)/shard_map/ppermute | solution.py:48
  471.1 35.5 %collective-permute-start.58 = (bf16[1,512,1536]{2,1,0:T(8,128)(2,1)}, bf16[1,512,1536]{2,1,0:T(8,128)(2,1)}, u32[]{:S(2)}, u32[]{:S(2)}) collective-permute-start(bf16[1,512,1536]{2,1,0:T(8,128)(2,1)} %get-tuple-element.455), channel_id=1, source_target_pairs={{0,1},{1,0},{2,3},{3,2},{4,5},{5,4},{6,7},{7,6},{8,9},{9,8},{10,11... | collective-permute-start | bytes 4718600 | tf_op jit(solution)/shard_map/ppermute | solution.py:48
  471.1 35.5 %collective-permute-start.57 = (bf16[2,512,1536]{2,1,0:T(8,128)(2,1)}, bf16[2,512,1536]{2,1,0:T(8,128)(2,1)}, u32[]{:S(2)}, u32[]{:S(2)}) collective-permute-start(bf16[2,512,1536]{2,1,0:T(8,128)(2,1)} %get-tuple-element.453), channel_id=1, source_target_pairs={{0,1},{1,0},{2,3},{3,2},{4,5},{5,4},{6,7},{7,6},{8,9},{9,8},{10,11... | collective-permute-start | bytes 9437192 | tf_op jit(solution)/shard_map/ppermute | solution.py:48
  497.5 35.2 %collective-permute-start.59 = (bf16[384,1152]{1,0:T(8,128)(2,1)}, bf16[384,1152]{1,0:T(8,128)(2,1)S(1)}, u32[]{:S(2)}, u32[]{:S(2)}) collective-permute-start(bf16[384,1152]{1,0:T(8,128)(2,1)} %line_step.12), channel_id=1, source_target_pairs={{0,8},{2,10},{4,12},{6,14},{8,16},{10,18},{12,20},{14,22},{16,24},... | collective-permute-start | bytes 2654216 | tf_op jit(solution)/shard_map/ppermute | solution.py:44
  505.0 57.3 %collective-permute-start.55 = (bf16[512,1536]{1,0:T(8,128)(2,1)}, bf16[512,1536]{1,0:T(8,128)(2,1)S(1)}, u32[]{:S(2)}, u32[]{:S(2)}) collective-permute-start(bf16[512,1536]{1,0:T(8,128)(2,1)} %get-tuple-element.448), channel_id=1, source_target_pairs={{0,4},{2,6},{4,0},{6,2},{8,12},{10,14},{12,8},{14,10},{16,20},{18,... | collective-permute-start | bytes 4718600 | tf_op jit(solution)/shard_map/ppermute | solution.py:39
  505.3 56.9 %collective-permute-start.54 = (bf16[512,1536]{1,0:T(8,128)(2,1)}, bf16[512,1536]{1,0:T(8,128)(2,1)}, u32[]{:S(2)}, u32[]{:S(2)}) collective-permute-start(bf16[512,1536]{1,0:T(8,128)(2,1)} %get-tuple-element.447), channel_id=1, source_target_pairs={{0,2},{2,0},{4,6},{6,4},{8,10},{10,8},{12,14},{14,12},{16,18},{18,... | collective-permute-start | bytes 4718600 | tf_op jit(solution)/shard_map/ppermute | solution.py:39
  509.4 52.8 %collective-permute-start.60 = (bf16[256,1536]{1,0:T(8,128)(2,1)}, bf16[256,1536]{1,0:T(8,128)(2,1)S(1)}, u32[]{:S(2)}, u32[]{:S(2)}) collective-permute-start(bf16[256,1536]{1,0:T(8,128)(2,1)} %get-tuple-element.460), channel_id=1, source_target_pairs={{0,2},{2,0},{4,6},{6,4},{8,10},{10,8},{12,14},{14,12},{16,18},{18,... | collective-permute-start | bytes 2359304 | tf_op jit(solution)/shard_map/ppermute | solution.py:39
  537.7 42.3 %collective-permute-start.64 = (bf16[384,2304]{1,0:T(8,128)(2,1)}, bf16[384,2304]{1,0:T(8,128)(2,1)S(1)}, u32[]{:S(2)}, u32[]{:S(2)}) collective-permute-start(bf16[384,2304]{1,0:T(8,128)(2,1)} %line_step.13), channel_id=1, source_target_pairs={{0,8},{2,10},{4,12},{6,14},{8,16},{10,18},{12,20},{14,22},{16,24},... | collective-permute-start | bytes 5308424 | tf_op jit(solution)/shard_map/ppermute | solution.py:44
  578.4 49.1 %collective-permute-start.65 = (bf16[512,1536]{1,0:T(8,128)(2,1)}, bf16[512,1536]{1,0:T(8,128)(2,1)}, u32[]{:S(2)}, u32[]{:S(2)}) collective-permute-start(bf16[512,1536]{1,0:T(8,128)(2,1)} %get-tuple-element.472), channel_id=1, source_target_pairs={{0,2},{2,0},{4,6},{6,4},{8,10},{10,8},{12,14},{14,12},{16,18},{18,... | collective-permute-start | bytes 4718600 | tf_op jit(solution)/shard_map/ppermute | solution.py:39
  579.8 47.7 %collective-permute-start.66 = (bf16[512,1536]{1,0:T(8,128)(2,1)}, bf16[512,1536]{1,0:T(8,128)(2,1)}, u32[]{:S(2)}, u32[]{:S(2)}) collective-permute-start(bf16[512,1536]{1,0:T(8,128)(2,1)} %get-tuple-element.486), channel_id=1, source_target_pairs={{0,4},{2,6},{4,0},{6,2},{8,12},{10,14},{12,8},{14,10},{16,20},{18,... | collective-permute-start | bytes 4718600 | tf_op jit(solution)/shard_map/ppermute | solution.py:39
  586.4 60.2 %collective-permute-start.67 = (bf16[384,3456]{1,0:T(8,128)(2,1)}, bf16[384,3456]{1,0:T(8,128)(2,1)}, u32[]{:S(2)}, u32[]{:S(2)}) collective-permute-start(bf16[384,3456]{1,0:T(8,128)(2,1)} %line_step.14), channel_id=1, source_target_pairs={{0,8},{2,10},{4,12},{6,14},{8,16},{10,18},{12,20},{14,22},{16,24},... | collective-permute-start | bytes 7962632 | tf_op jit(solution)/shard_map/ppermute | solution.py:44
  635.8 67.5 %collective-permute-start.68 = (bf16[768,1536]{1,0:T(8,128)(2,1)}, bf16[768,1536]{1,0:T(8,128)(2,1)S(1)}, u32[]{:S(2)}, u32[]{:S(2)}) collective-permute-start(bf16[768,1536]{1,0:T(8,128)(2,1)} %plane_start.4), channel_id=1, source_target_pairs={{0,2},{2,0},{4,6},{6,4},{8,10},{10,8},{12,14},{14,12},{16,18},{18,... | collective-permute-start | bytes 7077896 | tf_op jit(solution)/shard_map/ppermute | solution.py:39
  636.6 72.2 %collective-permute-start.70 = (bf16[768,1536]{1,0:T(8,128)(2,1)}, bf16[768,1536]{1,0:T(8,128)(2,1)}, u32[]{:S(2)}, u32[]{:S(2)}) collective-permute-start(bf16[768,1536]{1,0:T(8,128)(2,1)} %plane_start.5), channel_id=1, source_target_pairs={{0,4},{2,6},{4,0},{6,2},{8,12},{10,14},{12,8},{14,10},{16,20},{18,... | collective-permute-start | bytes 7077896 | tf_op jit(solution)/shard_map/ppermute | solution.py:39
  651.5 75.4 %collective-permute-start.71 = (bf16[384,2304]{1,0:T(8,128)(2,1)}, bf16[384,2304]{1,0:T(8,128)(2,1)}, u32[]{:S(2)}, u32[]{:S(2)}) collective-permute-start(bf16[384,2304]{1,0:T(8,128)(2,1)} %line_step.15), channel_id=1, source_target_pairs={{0,8},{2,10},{4,12},{6,14},{8,16},{10,18},{12,20},{14,22},{16,24},... | collective-permute-start | bytes 5308424 | tf_op jit(solution)/shard_map/ppermute | solution.py:44
  740.8 35.9 %collective-permute-start.74 = (bf16[384,1152]{1,0:T(8,128)(2,1)}, bf16[384,1152]{1,0:T(8,128)(2,1)}, u32[]{:S(2)}, u32[]{:S(2)}) collective-permute-start(bf16[384,1152]{1,0:T(8,128)(2,1)} %line_step.16), channel_id=1, source_target_pairs={{0,8},{2,10},{4,12},{6,14},{8,16},{10,18},{12,20},{14,22},{16,24},... | collective-permute-start | bytes 2654216 | tf_op jit(solution)/shard_map/ppermute | solution.py:44
  809.9 40.3 %collective-permute-start.88 = (bf16[96,4992]{1,0:T(8,128)(2,1)}, bf16[96,4992]{1,0:T(8,128)(2,1)S(1)}, u32[]{:S(2)}, u32[]{:S(2)}) collective-permute-start(bf16[96,4992]{1,0:T(8,128)(2,1)} %line_step.19), channel_id=1, source_target_pairs={{0,8},{2,10},{4,12},{6,14},{8,16},{10,18},{12,20},{14,22},{16,24},... | collective-permute-start | bytes 2875400 | tf_op jit(solution)/shard_map/ppermute | solution.py:44
  (143 other events, 1488.5 us)

commit v5 on v4

--- a/solution.py
+++ b/solution.py
@@ -142,6 +142,10 @@
     high, low = split_two(values)
     packed = high.astype(F32) + pltpu.roll(low.astype(F32), LANES // 2, 1)
     return nn(packed.astype(BF), spread)
+
+
+def sum_heads(values, spread, heads_on):
+    return jnp.where(heads_on, nt(values.astype(BF), spread), 0.0)
 
 
 def gather_heads(values, spread, heads_on):
@@ -326,10 +330,10 @@
     before_low, d_after_low = before.astype(BF), d_after.astype(BF)
     dy_start = d_y * from_start
     dy_start_low = dy_start.astype(BF)
-    reach = gather_heads(dy_start * nn(c_low, before_low), spread, heads_on)
+    reach = sum_heads(dy_start * nn(c_low, before_low), spread, heads_on)
     u_end = u * to_end
     d_from_state = nn(b_low, d_after_low)
-    kept = gather_heads(u_end * d_from_state, spread, heads_on)
+    kept = sum_heads(u_end * d_from_state, spread, heads_on)
     carried = jnp.sum(before * d_after, axis=0, keepdims=True) * whole
     carried = gather_heads(jnp.broadcast_to(carried, (8, width)), spread, heads_on[:8])[0:1]
     d_c = nt(dy_start_low, before_low) + nn(d_scores_t.T.astype(BF), b_low)
@@ -346,7 +350,7 @@
         )
         + carried
     )
-    d_step = gather_heads(x * d_u, spread, heads_on)
+    d_step = sum_heads(x * d_u, spread, heads_on)
     rate = head_ref[1:2]
     d_raw = jnp.where(heads_on, (d_step - rate * d_decay) * sigmoid(shifted), 0.0)
     hg_ref[0:1, :] += jnp.sum(d_raw, axis=0, keepdims=True)

time: 910 us -> 906 us (level)
  no operation moved by 1% of the time
where the time goes in v5:
time: 906 us; the launch traced here: 897 us
  Pallas kernels  481 us (53%)
  waiting for transfers between devices  161 us (18%)
  matrix products  98.5 us (11%)
  starting transfers between devices  89.4 us (10%)
  local copies, waits for them, and re-layouts  51.1 us (6%)
  between operations  9.72 us (1%)
    pallas_call x3, Pallas kernels, expert_rows(): pl.pallas_call(functools.partial(expert_body, (own, units, shared, counts...  144 us
    ppermute x48, waiting for transfers between devices, hop(): return lax.ppermute(values, 'dp', [(i, i ^ bits) for i in range(count)])  116 us
    dot_general x8, matrix products, tn(): lax.dot_general(left, right, (((0,), (0,)), ((), ())), preferred_element_...  98.5 us
    pallas_call x5, Pallas kernels, gathered_call(): pl.pallas_call(whole, grid_spec=pltpu.PrefetchScalarGridSpec(num_scalar_p...  79.8 us
    pallas_call x20, Pallas kernels, add_blocks(): pl.pallas_call(body, out_shape=jax.ShapeDtypeStruct((count * height, tota...  76 us
    pallas_call x1, Pallas kernels, back_scan(): pl.pallas_call(back_body, grid=(steps,), out_shape=(jax.ShapeDtypeStruct(...  48.1 us
    pallas_call x19, Pallas kernels, small_call(): pl.pallas_call(body, out_shape=tuple((jax.ShapeDtypeStruct(shape, kind) f...  47.4 us
    ppermute x48, starting transfers between devices, hop(): return lax.ppermute(values, 'dp', [(i, i ^ bits) for i in range(count)])  43.7 us
  transfers between devices with their start and end apart: 95, of which 40 were waited for; matrix products, arithmetic and copies ran while one was open for 14% of the time, Pallas kernels for 51%

profile of v5, /device:TPU:1, one launch (start us, length us, event | category | flops | bytes accessed | tf_op | source)
XLA Modules:
  0.0 896.8 jit_solution(676459142594302243)
XLA Ops:
  49.0 8.1 collective-permute-done.7.refs_1_
  58.0 17.7 %collective-permute-done.11.refs_2_ = bf16[96,3456]{1,0:T(8,128)(2,1)} collective-permute-done((bf16[96,3456]{1,0:T(8,128)(2,1)S(1)}, bf16[96,3456]{1,0:T(8,128)(2,1)}, u32[]{:S(2)}, u32[]{:S(2)}) %collective-permute-start.11) | collective-permute-done | bytes 663584 | tf_op jit(solution)/shard_map/ppermute | solution.py:39
  95.3 14.1 %collective-permute-done.14.values_ref.refs_5_.refs_13_ = bf16[4,96,1920]{2,1,0:T(8,128)(2,1)S(1)} collective-permute-done((bf16[4,96,1920]{2,1,0:T(8,128)(2,1)}, bf16[4,96,1920]{2,1,0:T(8,128)(2,1)S(1)}, u32[]{:S(2)}, u32[]{:S(2)}) %collective-permute-start.14) | collective-permute-done | bytes 1474592 | tf_op jit(solution)/shard_map/ppermute | solution.py:39
  122.9 11.8 %collective-permute-done.17.refs_7_.refs_15_ = bf16[4,96,896]{2,1,0:T(8,128)(2,1)S(1)} collective-permute-done((bf16[4,96,896]{2,1,0:T(8,128)(2,1)}, bf16[4,96,896]{2,1,0:T(8,128)(2,1)S(1)}, u32[]{:S(2)}, u32[]{:S(2)}) %collective-permute-start.17) | collective-permute-done | bytes 688160 | tf_op jit(solution)/shard_map/ppermute | solution.py:39
  137.6 13.5 %inner_product.1 = (f32[1024,1920]{1,0:T(8,128)}, bf16[1536,128]{1,0:T(8,128)(2,1)}) custom-call(s32[20]{0:T(128)} %add.75.refs_0_, s32[1]{0:T(128)} %constant.53.clone.refs_1_, bf16[1024,1536]{1,0:T(8,128)(2,1)} %bitcast.92, bf16[4,96,1920]{2,1,0:T(8,128)(2,1)} %stack_pairs.1.refs_3_.refs_11_, ...), custom_call_target="tpu_custom_call" | custom-call | flops 1000 | bytes 1000 | tf_op jit(solution)/shard_map/inner_product/pallas_call | solution.py:821
  153.5 22.4 %front_scan.1 = (f32[1024,1536]{1,0:T(8,128)}, f32[8,128,1536]{2,1,0:T(8,128)}) custom-call(f32[1024,1920]{1,0:T(8,128)} %get-tuple-element.347.zi_ref.prev_ref, f32[8,1920]{1,0:T(8,128)} %get-tuple-element.326.kern_ref.refs_6_.refs_8_, f32[8,128]{1,0:T(8,128)} %get-tuple-element.348.head_ref, bf16[128,1536]{1,0:T(8,128)(2,1)} %get-tuple-element.349.spread_ref), custom_call_target="tpu_custom_call" | custom-call | flops 1000 | bytes 1000 | tf_op jit(solution)/shard_map/front_scan/pallas_call | solution.py:225
  185.9 6.2 collective-permute-done.23.refs_8_.refs_10_
  196.8 13.3 %gate_product.1 = (f32[1024,1536]{1,0:T(8,128)}, f32[1024,128]{1,0:T(8,128)}) custom-call(s32[20]{0:T(128)} %add.75.refs_0_, s32[1]{0:T(128)} %constant.53.clone.refs_1_, bf16[1024,1536]{1,0:T(8,128)(2,1)} %bitcast.93, f32[1024,1536]{1,0:T(8,128)} %get-tuple-element.377.refs_3_.refs_2_, bf16[4,96,1536]{2,1,0:T(8,128)(2,1)} %stack_columns.4.refs_4_.refs_6_, ...), custom_call_target="tpu_custom_call" | custom-call | flops 1000 | bytes 1000 | tf_op jit(solution)/shard_map/gate_product/pallas_call | solution.py:821
  226.7 6.9 collective-permute-done.28.refs_11_.refs_13_
  237.1 14.8 %mixed_product.1 = (bf16[1024,1536]{1,0:T(8,128)(2,1)}, bf16[512,1536]{1,0:T(8,128)(2,1)}, f32[512,1536]{1,0:T(8,128)}) custom-call(s32[20]{0:T(128)} %add.75.refs_0_, s32[1]{0:T(128)} %bitcast.1.refs_1_, f32[1024,1536]{1,0:T(8,128)} %get-tuple-element.377.refs_3_.refs_2_, f32[1024,1536]{1,0:T(8,128)} %get-tuple-element.366.refs_3_.refs_4_, ...), custom_call_target="tpu_custom_call" | custom-call | flops 1000 | bytes 1000 | tf_op jit(solution)/shard_map/mixed_product/pallas_call | solution.py:821
  251.9 19.1 %collective-permute-done.32.values_ref.refs_8_ = bf16[512,1664]{1,0:T(8,128)(2,1)} collective-permute-done((bf16[512,1664]{1,0:T(8,128)(2,1)}, bf16[512,1664]{1,0:T(8,128)(2,1)}, u32[]{:S(2)}, u32[]{:S(2)}) %collective-permute-start.32) | collective-permute-done | bytes 1703968 | tf_op jit(solution)/shard_map/ppermute | solution.py:39
  276.5 6.8 collective-permute-start.33
  297.7 38.9 %expert_rows.3 = (bf16[4096,1536]{1,0:T(8,128)(2,1)}, bf16[4096,1536]{1,0:T(8,128)(2,1)}, bf16[4096,1152]{1,0:T(8,128)(2,1)}, bf16[4096,1280]{1,0:T(8,128)(2,1)}...) custom-call(s32[16]{0:T(128)} %add.71.refs_0_, ...), custom_call_target="tpu_custom_call" | custom-call | flops 1000 | bytes 1000 | tf_op jit(solution)/shard_map/expert_rows/pallas_call | solution.py:1487
  346.1 66.3 %expert_rows.4 = (bf16[4096,1536]{1,0:T(8,128)(2,1)}, bf16[4096,1536]{1,0:T(8,128)(2,1)}, bf16[4096,1152]{1,0:T(8,128)(2,1)}, bf16[4096,1280]{1,0:T(8,128)(2,1)}...) custom-call(s32[16]{0:T(128)} %add.71.refs_0_, ...), custom_call_target="tpu_custom_call", output_to_operand_aliasing={{0}: (15, {}), {1}: (16, {}), {2}: (17, {}), {3}: (18, {}),... | custom-call | flops 1000 | bytes 1000 | tf_op jit(solution)/shard_map/expert_rows/pallas_call | solution.py:1487
  423.1 39.1 %expert_rows.5 = (bf16[4096,1536]{1,0:T(8,128)(2,1)}, bf16[4096,1536]{1,0:T(8,128)(2,1)}, bf16[4096,1152]{1,0:T(8,128)(2,1)}, bf16[4096,1280]{1,0:T(8,128)(2,1)}...) custom-call(s32[16]{0:T(128)} %add.71.refs_0_, ...), custom_call_target="tpu_custom_call", output_to_operand_aliasing={{0}: (15, {}), {1}: (16, {}), {2}: (17, {}), {3}: (18, {}),... | custom-call | flops 1000 | bytes 1000 | tf_op jit(solution)/shard_map/expert_rows/pallas_call | solution.py:1487
  471.6 23.0 %fusion.3.refs_0_.refs_2_ = bf16[1536,1152]{1,0:T(8,128)(2,1)} fusion(bf16[4096,1536]{1,0:T(8,128)(2,1)} %get-tuple-element.443, bf16[4096,1152]{1,0:T(8,128)(2,1)} %get-tuple-element.444), kind=kOutput, calls=%fused_computation.41 | convolution fusion | flops 14495514624 | bytes 25559040 | tf_op jit(solution)/shard_map/dot_general | solution.py:34
  500.1 4.9 side_sums.2
  509.7 23.0 %fusion.4.refs_1_.refs_0_ = bf16[1536,1152]{1,0:T(8,128)(2,1)} fusion(bf16[4096,1536]{1,0:T(8,128)(2,1)} %get-tuple-element.464, bf16[4096,1152]{1,0:T(8,128)(2,1)} %get-tuple-element.462), kind=kOutput, calls=%fused_computation.42 | convolution fusion | flops 14495514624 | bytes 25559040 | tf_op jit(solution)/shard_map/dot_general | solution.py:34
  538.9 23.3 %fusion.5.refs_2_.refs_1_.refs_0_ = bf16[1536,1280]{1,0:T(8,128)(2,1)} fusion(bf16[4096,1536]{1,0:T(8,128)(2,1)} %get-tuple-element.464, bf16[4096,1280]{1,0:T(8,128)(2,1)} %get-tuple-element.465), kind=kOutput, calls=%fused_computation.43 | convolution fusion | flops 16106127360 | bytes 27000832 | tf_op jit(solution)/shard_map/dot_general | solution.py:34
  568.0 8.7 resid_back.1
  581.2 5.2 line_step.14
  593.5 17.5 %gate_back.1 = (f32[1024,1536]{1,0:T(8,128)}, bf16[1024,768]{1,0:T(8,128)(2,1)}, bf16[1024,768]{1,0:T(8,128)(2,1)}, f32[8,1536]{1,0:T(8,128)}) custom-call(s32[20]{0:T(128)} %add.75.refs_0_, s32[1]{0:T(128)} %constant.53.clone.refs_1_, bf16[1024,1536]{1,0:T(8,128)(2,1)} %bitcast.98, f32[1024,1536]{1,0:T(8,128)} %get-tuple-element.377.refs_3_.refs_2_, ...), custom_call_target="tpu_custom_call" | custom-call | flops 1000 | bytes 1000 | tf_op jit(solution)/shard_map/gate_back/pallas_call | solution.py:821
  611.0 5.5 fusion.8.refs_1_.refs_2_.refs_9_
  616.6 6.9 fusion.6.refs_0_.refs_6_
  637.3 5.1 output_rows.1
  651.6 48.1 %back_scan.1 = (bf16[1024,1024]{1,0:T(8,128)(2,1)}, bf16[1024,896]{1,0:T(8,128)(2,1)}, f32[8,1920]{1,0:T(8,128)}, f32[8,128]{1,0:T(8,128)}) custom-call(f32[1024,1536]{1,0:T(8,128)} %get-tuple-element.497.dy_ref, f32[1024,1920]{1,0:T(8,128)} %get-tuple-element.347.zi_ref.prev_ref, f32[1024,1920]{1,0:T(8,128)} %get-tuple-element.347.zi_ref.prev_ref, ...), custom_call_target="tpu_custom_call" | custom-call | flops 1000 | bytes 1000 | tf_op jit(solution)/shard_map/back_scan/pallas_call | solution.py:392
  710.5 7.7 add_convert_fusion.refs_0_.refs_15_.refs_3_
  718.2 5.1 fusion.9.refs_0_.refs_12_
  741.4 20.7 %normed_back.1 = (bf16[512,1536]{1,0:T(8,128)(2,1)}, f32[512,1536]{1,0:T(8,128)}) custom-call(s32[20]{0:T(128)} %add.75.refs_0_, s32[1]{0:T(128)} %bitcast.1.refs_1_, bf16[1024,768]{1,0:T(8,128)(2,1)} %get-tuple-element.512.refs_2_, bf16[1024,768]{1,0:T(8,128)(2,1)} %get-tuple-element.513.refs_3_, bf16[1024,1024]{1,0:T(8,128)(2,1)} %get-tuple-element.514.refs_4_, ...), custom_call_target="tpu_custom_call" | custom-call | flops 1000 | bytes 1000 | tf_op jit(solution)/shard_map/normed_back/pallas_call | solution.py:821
  786.1 6.9 tokens_back.1
  807.3 5.0 member_pieces.1
  852.6 7.3 collective-permute-done.92.refs_3_
  (445 shorter events, 364.2 us)
Async XLA Ops:
  6.7 42.2 %collective-permute-start.8 = (bf16[512,1536]{1,0:T(8,128)(2,1)}, bf16[512,1536]{1,0:T(8,128)(2,1)}, u32[]{:S(2)}, u32[]{:S(2)}) collective-permute-start(bf16[512,1536]{1,0:T(8,128)(2,1)} %tokens_ref.5), channel_id=1, source_target_pairs={{0,1},{1,0},{2,3},{3,2},{4,5},{5,4},{6,7},{7,6},{8,9},{9,8},{10,11... | collective-permute-start | bytes 4718600 | tf_op jit(solution)/shard_map/ppermute | solution.py:48
  94.0 59.3 %collective-permute-start.19 = (bf16[4,96,3456]{2,1,0:T(8,128)(2,1)}, bf16[4,96,3456]{2,1,0:T(8,128)(2,1)S(1)}, u32[]{:S(2)}, u32[]{:S(2)}) collective-permute-start(bf16[4,96,3456]{2,1,0:T(8,128)(2,1)} %stack_columns.3.refs_7_.refs_11_), channel_id=1, source_target_pairs={{0,8},{2,10},{4,12},{6,14},{8,16},{10,18},{12,20},{14,22},{16,24},... | collective-permute-start | bytes 7962632 | tf_op jit(solution)/shard_map/ppermute | solution.py:44
  136.1 39.8 %collective-permute-start.21 = (bf16[4,96,1536]{2,1,0:T(8,128)(2,1)}, bf16[4,96,1536]{2,1,0:T(8,128)(2,1)S(1)}, u32[]{:S(2)}, u32[]{:S(2)}) collective-permute-start(bf16[4,96,1536]{2,1,0:T(8,128)(2,1)} %stack_columns.4.refs_4_.refs_6_), channel_id=1, source_target_pairs={{0,4},{2,6},{4,0},{6,2},{8,12},{10,14},{12,8},{14,10},{16,20},{18,... | collective-permute-start | bytes 3538952 | tf_op jit(solution)/shard_map/ppermute | solution.py:39
  137.1 38.8 %collective-permute-start.20 = (bf16[4,96,1536]{2,1,0:T(8,128)(2,1)}, bf16[4,96,1536]{2,1,0:T(8,128)(2,1)}, u32[]{:S(2)}, u32[]{:S(2)}) collective-permute-start(bf16[4,96,1536]{2,1,0:T(8,128)(2,1)} %stack_columns.4.refs_4_.refs_6_), channel_id=1, source_target_pairs={{0,2},{2,0},{4,6},{6,4},{8,10},{10,8},{12,14},{14,12},{16,18},{18,... | collective-permute-start | bytes 3538952 | tf_op jit(solution)/shard_map/ppermute | solution.py:39
  153.3 66.5 %collective-permute-start.29 = (bf16[4,96,3456]{2,1,0:T(8,128)(2,1)S(1)}, bf16[4,96,3456]{2,1,0:T(8,128)(2,1)}, u32[]{:S(2)}, u32[]{:S(2)}) collective-permute-start(bf16[4,96,3456]{2,1,0:T(8,128)(2,1)S(1)} %collective-permute-done.19.refs_8_.refs_12_), channel_id=1, source_target_pairs={{0,8},{2,10},{4,12},{6,14},{8,16},{10,18},{12,20},{14,22},{16,24},... | collective-permute-start | bytes 7962632 | tf_op jit(solution)/shard_map/ppermute | solution.py:44
  219.8 56.7 %collective-permute-start.30 = (bf16[4,96,3456]{2,1,0:T(8,128)(2,1)}, bf16[4,96,3456]{2,1,0:T(8,128)(2,1)S(1)}, u32[]{:S(2)}, u32[]{:S(2)}) collective-permute-start(bf16[4,96,3456]{2,1,0:T(8,128)(2,1)} %collective-permute-done.29.refs_9_.refs_13_), channel_id=1, source_target_pairs={{0,8},{2,10},{4,12},{6,14},{8,16},{10,18},{12,20},{14,22},{16,24},... | collective-permute-start | bytes 7962632 | tf_op jit(solution)/shard_map/ppermute | solution.py:44
  235.3 35.7 %collective-permute-start.32 = (bf16[512,1664]{1,0:T(8,128)(2,1)}, bf16[512,1664]{1,0:T(8,128)(2,1)}, u32[]{:S(2)}, u32[]{:S(2)}) collective-permute-start(bf16[512,1664]{1,0:T(8,128)(2,1)} %marked_rows.1.refs_4_), channel_id=1, source_target_pairs={{0,4},{2,6},{4,0},{6,2},{8,12},{10,14},{12,8},{14,10},{16,20},{18,... | collective-permute-start | bytes 5111816 | tf_op jit(solution)/shard_map/ppermute | solution.py:39
  294.9 41.8 %collective-permute-start.37 = (bf16[512,1664]{1,0:T(8,128)(2,1)}, bf16[512,1664]{1,0:T(8,128)(2,1)}, u32[]{:S(2)}, u32[]{:S(2)}) collective-permute-start(bf16[512,1664]{1,0:T(8,128)(2,1)} %collective-permute-done.31.values_ref.refs_6_), channel_id=1, source_target_pairs={{0,1},{1,0},{2,3},{3,2},{4,5},{5,4},{6,7},{7,6},{8,9},{9,8},{10,11... | collective-permute-start | bytes 5111816 | tf_op jit(solution)/shard_map/ppermute | solution.py:48
  295.3 41.4 %collective-permute-start.38 = (bf16[512,1664]{1,0:T(8,128)(2,1)}, bf16[512,1664]{1,0:T(8,128)(2,1)}, u32[]{:S(2)}, u32[]{:S(2)}) collective-permute-start(bf16[512,1664]{1,0:T(8,128)(2,1)} %collective-permute-done.32.values_ref.refs_8_), channel_id=1, source_target_pairs={{0,1},{1,0},{2,3},{3,2},{4,5},{5,4},{6,7},{7,6},{8,9},{9,8},{10,11... | collective-permute-start | bytes 5111816 | tf_op jit(solution)/shard_map/ppermute | solution.py:48
  296.1 40.6 %collective-permute-start.36 = (bf16[512,1536]{1,0:T(8,128)(2,1)}, bf16[512,1536]{1,0:T(8,128)(2,1)S(1)}, u32[]{:S(2)}, u32[]{:S(2)}) collective-permute-start(bf16[512,1536]{1,0:T(8,128)(2,1)} %get-tuple-element.388.refs_2_), channel_id=1, source_target_pairs={{0,4},{2,6},{4,0},{6,2},{8,12},{10,14},{12,8},{14,10},{16,20},{18,... | collective-permute-start | bytes 4718600 | tf_op jit(solution)/shard_map/ppermute | solution.py:39
  296.9 39.8 %collective-permute-start.35 = (bf16[512,1536]{1,0:T(8,128)(2,1)}, bf16[512,1536]{1,0:T(8,128)(2,1)S(1)}, u32[]{:S(2)}, u32[]{:S(2)}) collective-permute-start(bf16[512,1536]{1,0:T(8,128)(2,1)} %get-tuple-element.388.refs_2_), channel_id=1, source_target_pairs={{0,2},{2,0},{4,6},{6,4},{8,10},{10,8},{12,14},{14,12},{16,18},{18,... | collective-permute-start | bytes 4718600 | tf_op jit(solution)/shard_map/ppermute | solution.py:39
  343.1 69.3 %collective-permute-start.41 = (bf16[256,1664]{1,0:T(8,128)(2,1)}, bf16[256,1664]{1,0:T(8,128)(2,1)S(1)}, u32[]{:S(2)}, u32[]{:S(2)}) collective-permute-start(bf16[256,1664]{1,0:T(8,128)(2,1)} %cut_rows.4), channel_id=1, source_target_pairs={{0,4},{2,6},{4,0},{6,2},{8,12},{10,14},{12,8},{14,10},{16,20},{18,... | collective-permute-start | bytes 2555912 | tf_op jit(solution)/shard_map/ppermute | solution.py:39
  343.9 69.6 %collective-permute-start.42 = (bf16[256,1664]{1,0:T(8,128)(2,1)}, bf16[256,1664]{1,0:T(8,128)(2,1)S(1)}, u32[]{:S(2)}, u32[]{:S(2)}) collective-permute-start(bf16[256,1664]{1,0:T(8,128)(2,1)} %cut_rows.5), channel_id=1, source_target_pairs={{0,2},{2,0},{4,6},{6,4},{8,10},{10,8},{12,14},{14,12},{16,18},{18,... | collective-permute-start | bytes 2555912 | tf_op jit(solution)/shard_map/ppermute | solution.py:39
  344.4 68.0 %collective-permute-start.43 = (bf16[256,1536]{1,0:T(8,128)(2,1)}, bf16[256,1536]{1,0:T(8,128)(2,1)S(1)}, u32[]{:S(2)}, u32[]{:S(2)}) collective-permute-start(bf16[256,1536]{1,0:T(8,128)(2,1)} %cut_rows.6), channel_id=1, source_target_pairs={{0,4},{2,6},{4,0},{6,2},{8,12},{10,14},{12,8},{14,10},{16,20},{18,... | collective-permute-start | bytes 2359304 | tf_op jit(solution)/shard_map/ppermute | solution.py:39
  345.3 67.1 %collective-permute-start.44 = (bf16[256,1536]{1,0:T(8,128)(2,1)}, bf16[256,1536]{1,0:T(8,128)(2,1)S(1)}, u32[]{:S(2)}, u32[]{:S(2)}) collective-permute-start(bf16[256,1536]{1,0:T(8,128)(2,1)} %cut_rows.7), channel_id=1, source_target_pairs={{0,2},{2,0},{4,6},{6,4},{8,10},{10,8},{12,14},{14,12},{16,18},{18,... | collective-permute-start | bytes 2359304 | tf_op jit(solution)/shard_map/ppermute | solution.py:39
  422.6 40.0 %collective-permute-start.49 = (bf16[2,512,1536]{2,1,0:T(8,128)(2,1)}, bf16[2,512,1536]{2,1,0:T(8,128)(2,1)S(1)}, u32[]{:S(2)}, u32[]{:S(2)}) collective-permute-start(bf16[2,512,1536]{2,1,0:T(8,128)(2,1)} %get-tuple-element.423), channel_id=1, source_target_pairs={{0,1},{1,0},{2,3},{3,2},{4,5},{5,4},{6,7},{7,6},{8,9},{9,8},{10,11... | collective-permute-start | bytes 9437192 | tf_op jit(solution)/shard_map/ppermute | solution.py:48
  423.0 39.7 %collective-permute-start.50 = (bf16[1,512,1536]{2,1,0:T(8,128)(2,1)}, bf16[1,512,1536]{2,1,0:T(8,128)(2,1)}, u32[]{:S(2)}, u32[]{:S(2)}) collective-permute-start(bf16[1,512,1536]{2,1,0:T(8,128)(2,1)} %get-tuple-element.425), channel_id=1, source_target_pairs={{0,1},{1,0},{2,3},{3,2},{4,5},{5,4},{6,7},{7,6},{8,9},{9,8},{10,11... | collective-permute-start | bytes 4718600 | tf_op jit(solution)/shard_map/ppermute | solution.py:48
  471.1 35.5 %collective-permute-start.58 = (bf16[1,512,1536]{2,1,0:T(8,128)(2,1)}, bf16[1,512,1536]{2,1,0:T(8,128)(2,1)}, u32[]{:S(2)}, u32[]{:S(2)}) collective-permute-start(bf16[1,512,1536]{2,1,0:T(8,128)(2,1)} %get-tuple-element.455), channel_id=1, source_target_pairs={{0,1},{1,0},{2,3},{3,2},{4,5},{5,4},{6,7},{7,6},{8,9},{9,8},{10,11... | collective-permute-start | bytes 4718600 | tf_op jit(solution)/shard_map/ppermute | solution.py:48
  471.1 35.5 %collective-permute-start.57 = (bf16[2,512,1536]{2,1,0:T(8,128)(2,1)}, bf16[2,512,1536]{2,1,0:T(8,128)(2,1)}, u32[]{:S(2)}, u32[]{:S(2)}) collective-permute-start(bf16[2,512,1536]{2,1,0:T(8,128)(2,1)} %get-tuple-element.453), channel_id=1, source_target_pairs={{0,1},{1,0},{2,3},{3,2},{4,5},{5,4},{6,7},{7,6},{8,9},{9,8},{10,11... | collective-permute-start | bytes 9437192 | tf_op jit(solution)/shard_map/ppermute | solution.py:48
  497.5 35.2 %collective-permute-start.59 = (bf16[384,1152]{1,0:T(8,128)(2,1)}, bf16[384,1152]{1,0:T(8,128)(2,1)S(1)}, u32[]{:S(2)}, u32[]{:S(2)}) collective-permute-start(bf16[384,1152]{1,0:T(8,128)(2,1)} %line_step.12), channel_id=1, source_target_pairs={{0,8},{2,10},{4,12},{6,14},{8,16},{10,18},{12,20},{14,22},{16,24},... | collective-permute-start | bytes 2654216 | tf_op jit(solution)/shard_map/ppermute | solution.py:44
  505.0 57.3 %collective-permute-start.55 = (bf16[512,1536]{1,0:T(8,128)(2,1)}, bf16[512,1536]{1,0:T(8,128)(2,1)S(1)}, u32[]{:S(2)}, u32[]{:S(2)}) collective-permute-start(bf16[512,1536]{1,0:T(8,128)(2,1)} %get-tuple-element.448), channel_id=1, source_target_pairs={{0,4},{2,6},{4,0},{6,2},{8,12},{10,14},{12,8},{14,10},{16,20},{18,... | collective-permute-start | bytes 4718600 | tf_op jit(solution)/shard_map/ppermute | solution.py:39
  505.3 56.9 %collective-permute-start.54 = (bf16[512,1536]{1,0:T(8,128)(2,1)}, bf16[512,1536]{1,0:T(8,128)(2,1)}, u32[]{:S(2)}, u32[]{:S(2)}) collective-permute-start(bf16[512,1536]{1,0:T(8,128)(2,1)} %get-tuple-element.447), channel_id=1, source_target_pairs={{0,2},{2,0},{4,6},{6,4},{8,10},{10,8},{12,14},{14,12},{16,18},{18,... | collective-permute-start | bytes 4718600 | tf_op jit(solution)/shard_map/ppermute | solution.py:39
  509.4 52.8 %collective-permute-start.60 = (bf16[256,1536]{1,0:T(8,128)(2,1)}, bf16[256,1536]{1,0:T(8,128)(2,1)S(1)}, u32[]{:S(2)}, u32[]{:S(2)}) collective-permute-start(bf16[256,1536]{1,0:T(8,128)(2,1)} %get-tuple-element.460), channel_id=1, source_target_pairs={{0,2},{2,0},{4,6},{6,4},{8,10},{10,8},{12,14},{14,12},{16,18},{18,... | collective-permute-start | bytes 2359304 | tf_op jit(solution)/shard_map/ppermute | solution.py:39
  537.7 42.3 %collective-permute-start.64 = (bf16[384,2304]{1,0:T(8,128)(2,1)}, bf16[384,2304]{1,0:T(8,128)(2,1)S(1)}, u32[]{:S(2)}, u32[]{:S(2)}) collective-permute-start(bf16[384,2304]{1,0:T(8,128)(2,1)} %line_step.13), channel_id=1, source_target_pairs={{0,8},{2,10},{4,12},{6,14},{8,16},{10,18},{12,20},{14,22},{16,24},... | collective-permute-start | bytes 5308424 | tf_op jit(solution)/shard_map/ppermute | solution.py:44
  578.4 49.1 %collective-permute-start.65 = (bf16[512,1536]{1,0:T(8,128)(2,1)}, bf16[512,1536]{1,0:T(8,128)(2,1)}, u32[]{:S(2)}, u32[]{:S(2)}) collective-permute-start(bf16[512,1536]{1,0:T(8,128)(2,1)} %get-tuple-element.472), channel_id=1, source_target_pairs={{0,2},{2,0},{4,6},{6,4},{8,10},{10,8},{12,14},{14,12},{16,18},{18,... | collective-permute-start | bytes 4718600 | tf_op jit(solution)/shard_map/ppermute | solution.py:39
  579.8 47.7 %collective-permute-start.66 = (bf16[512,1536]{1,0:T(8,128)(2,1)}, bf16[512,1536]{1,0:T(8,128)(2,1)}, u32[]{:S(2)}, u32[]{:S(2)}) collective-permute-start(bf16[512,1536]{1,0:T(8,128)(2,1)} %get-tuple-element.486), channel_id=1, source_target_pairs={{0,4},{2,6},{4,0},{6,2},{8,12},{10,14},{12,8},{14,10},{16,20},{18,... | collective-permute-start | bytes 4718600 | tf_op jit(solution)/shard_map/ppermute | solution.py:39
  586.4 60.2 %collective-permute-start.67 = (bf16[384,3456]{1,0:T(8,128)(2,1)}, bf16[384,3456]{1,0:T(8,128)(2,1)}, u32[]{:S(2)}, u32[]{:S(2)}) collective-permute-start(bf16[384,3456]{1,0:T(8,128)(2,1)} %line_step.14), channel_id=1, source_target_pairs={{0,8},{2,10},{4,12},{6,14},{8,16},{10,18},{12,20},{14,22},{16,24},... | collective-permute-start | bytes 7962632 | tf_op jit(solution)/shard_map/ppermute | solution.py:44
  635.8 63.8 %collective-permute-start.68 = (bf16[768,1536]{1,0:T(8,128)(2,1)}, bf16[768,1536]{1,0:T(8,128)(2,1)S(1)}, u32[]{:S(2)}, u32[]{:S(2)}) collective-permute-start(bf16[768,1536]{1,0:T(8,128)(2,1)} %plane_start.4), channel_id=1, source_target_pairs={{0,2},{2,0},{4,6},{6,4},{8,10},{10,8},{12,14},{14,12},{16,18},{18,... | collective-permute-start | bytes 7077896 | tf_op jit(solution)/shard_map/ppermute | solution.py:39
  636.6 68.5 %collective-permute-start.70 = (bf16[768,1536]{1,0:T(8,128)(2,1)}, bf16[768,1536]{1,0:T(8,128)(2,1)}, u32[]{:S(2)}, u32[]{:S(2)}) collective-permute-start(bf16[768,1536]{1,0:T(8,128)(2,1)} %plane_start.5), channel_id=1, source_target_pairs={{0,4},{2,6},{4,0},{6,2},{8,12},{10,14},{12,8},{14,10},{16,20},{18,... | collective-permute-start | bytes 7077896 | tf_op jit(solution)/shard_map/ppermute | solution.py:39
  651.5 71.7 %collective-permute-start.71 = (bf16[384,2304]{1,0:T(8,128)(2,1)}, bf16[384,2304]{1,0:T(8,128)(2,1)}, u32[]{:S(2)}, u32[]{:S(2)}) collective-permute-start(bf16[384,2304]{1,0:T(8,128)(2,1)} %line_step.15), channel_id=1, source_target_pairs={{0,8},{2,10},{4,12},{6,14},{8,16},{10,18},{12,20},{14,22},{16,24},... | collective-permute-start | bytes 5308424 | tf_op jit(solution)/shard_map/ppermute | solution.py:44
  737.1 35.9 %collective-permute-start.74 = (bf16[384,1152]{1,0:T(8,128)(2,1)}, bf16[384,1152]{1,0:T(8,128)(2,1)}, u32[]{:S(2)}, u32[]{:S(2)}) collective-permute-start(bf16[384,1152]{1,0:T(8,128)(2,1)} %line_step.16), channel_id=1, source_target_pairs={{0,8},{2,10},{4,12},{6,14},{8,16},{10,18},{12,20},{14,22},{16,24},... | collective-permute-start | bytes 2654216 | tf_op jit(solution)/shard_map/ppermute | solution.py:44
  806.2 40.3 %collective-permute-start.88 = (bf16[96,4992]{1,0:T(8,128)(2,1)}, bf16[96,4992]{1,0:T(8,128)(2,1)S(1)}, u32[]{:S(2)}, u32[]{:S(2)}) collective-permute-start(bf16[96,4992]{1,0:T(8,128)(2,1)} %line_step.19), channel_id=1, source_target_pairs={{0,8},{2,10},{4,12},{6,14},{8,16},{10,18},{12,20},{14,22},{16,24},... | collective-permute-start | bytes 2875400 | tf_op jit(solution)/shard_map/ppermute | solution.py:44
  (143 other events, 1488.5 us)
